TPU v7x, 32 devices: a whole 2x2x4 slice. The times are simulated.
32 devices in a mesh: span: 8 (over z, x), cross: 4 (over y, core).
Axes of the slice: x: 2, y: 2, z: 4, core: 2. Of those that a mesh axis runs over, the one named last changes fastest.
Arguments:
- populations: bfloat16 [19, 128, 128, 128], P(None, 'span', 'cross'), may hold values from 0.2 to 1.8
- cell_index: int32 [4096, 8], P(('span', 'cross')), may hold values from 0 to 65535
- marker_weight: float32 [4096, 8], P(('span', 'cross')), may hold values from 0 to 0.25
- segment_id: int32 [4096], P(('span', 'cross')), may hold values from 0 to 255, as said below
Outputs:
- populations_next: bfloat16 [19, 128, 128, 128], P(None, 'span', 'cross')
- eddy_coeff: float32 [128, 128], P('cross')
- segment_force: float32 [3, 256], P(None, ('span', 'cross'))
Inputs may be any that keep to these rules, and one draw needn't show every extreme that they name: cell_index addresses a cell of the block of the device that holds the marker, flat in the order (span, crossflow, stream) of that 16 x 32 x 128 block. `segment_id`: segments are owned 8 to a device in device order (span slowest); a marker's segment may be owned by any device.
All inputs are finite; a program needn't handle non-finite values.
Results may differ from a plain program's by a relative error of at most 0.0019.
The roundings to bfloat16 on the way count: a program that leaves them out, or rounds other values in their place, can miss the bound.
Values may be sent and summed in bfloat16 or wider, within the bound.
No kernel may reach another device: no remote copies, remote signals or barrier semaphores. Data moves between devices by JAX's collectives and lax.ppermute only.
A program may use at most 128 MiB of HBM per device.

v0:
```python
import functools

import jax
import jax.numpy as jnp
from jax import lax
from jax.experimental import pallas as pl
from jax.experimental.pallas import tpu as pltpu
from jax.sharding import PartitionSpec as P

SEG_DEV = 8
LANES = 128
HALO = 3
EXT = 40
PAD = 56
OWN = 11
TOP = 8
CHUNKS = (8, 16, 24, 32, 40)
VMEM = 28 * 1024 * 1024

eps_sum = 1e-06
base_visc = 0.005

VELOCITIES = [
    [0, 0, 0],
    [1, 0, 0],
    [-1, 0, 0],
    [0, 1, 0],
    [0, -1, 0],
    [0, 0, 1],
    [0, 0, -1],
    [1, 1, 0],
    [-1, -1, 0],
    [1, -1, 0],
    [-1, 1, 0],
    [1, 0, 1],
    [-1, 0, -1],
    [1, 0, -1],
    [-1, 0, 1],
    [0, 1, 1],
    [0, -1, -1],
    [0, 1, -1],
    [0, -1, 1],
]


def swap(first, second, axis):
    count = lax.axis_size(axis)
    near = [(i, i ^ 1) for i in range(count)]
    other = [(i, (i + 1 if i % 2 else i - 1) % count) for i in range(count)]
    return lax.ppermute(first, axis, near), lax.ppermute(second, axis, other)


def is_odd(axis):
    return lax.rem(lax.axis_index(axis), 2) == 1


def send_pair(axis, upwards, downwards, first, second):
    odd = is_odd(axis)

    @pl.when(odd)
    def _():
        first[...] = downwards
        second[...] = upwards

    @pl.when(jnp.logical_not(odd))
    def _():
        first[...] = upwards
        second[...] = downwards


def below_above(axis, first, second):
    odd = is_odd(axis)
    return jnp.where(odd, first, second), jnp.where(odd, second, first)


def full(shape, dtype):
    return jax.ShapeDtypeStruct(shape, dtype)


def in_vmem(count):
    return [pl.BlockSpec(memory_space=pltpu.VMEM)] * count


def params():
    return pltpu.CompilerParams(vmem_limit_bytes=VMEM)


def cost(micros):
    return pl.CostEstimate(flops=0, bytes_accessed=int(micros * 3.6e6), transcendentals=0)


def plus(array):
    return pltpu.roll(array, LANES - 1, 1)


def minus(array):
    return pltpu.roll(array, 1, 1)


STEP = 2.0**-15


def encode(value):
    return jnp.round(value * (1.0 / STEP)).astype(jnp.int32).astype(jnp.int16)


def decode(coded):
    return coded.astype(jnp.int32).astype(jnp.float32) * STEP


def split(value):
    high = value.astype(jnp.bfloat16)
    return high, (value - high.astype(jnp.float32)).astype(jnp.bfloat16)


def moments_kernel(pops, vel_ref, first, second, rows):
    depth, width = pops.shape[1:3]

    def plane(z, carry):
        for half in range(width // 16):
            at = pl.ds(16 * half, 16)
            f = [pops[q, z, at, :].astype(jnp.float32) for q in range(19)]
            flux = [0.0, 0.0, 0.0]
            density = f[0]
            for q in range(1, 19, 2):
                even, odd = f[q] + f[q + 1], f[q] - f[q + 1]
                density = density + even
                for dim in range(3):
                    sign = VELOCITIES[q][dim]
                    if sign:
                        flux[dim] = flux[dim] + odd if sign > 0 else flux[dim] - odd
            inverse = 1.0 / density
            for dim in range(3):
                speed = flux[dim] * inverse
                vel_ref[dim, z, at, :] = speed
                for k in range(HALO):
                    if half == 0:
                        rows[0, dim * HALO + k, pl.ds(z, 1), :] = speed[k : k + 1]
                    if half == width // 16 - 1:
                        rows[1, dim * HALO + k, pl.ds(z, 1), :] = speed[15 - k : 16 - k]
        return carry

    lax.fori_loop(0, depth, plane, 0)
    send_pair("cross", encode(rows[1]), encode(rows[0]), first, second)


def block_moments(populations):
    _, depth, width, lanes = populations.shape
    edge = full((3 * HALO, depth, lanes), jnp.int16)
    return pl.pallas_call(
        moments_kernel,
        out_shape=(full((3, depth, width, lanes), jnp.float32), edge, edge),
        in_specs=in_vmem(1),
        out_specs=tuple(in_vmem(3)),
        scratch_shapes=[pltpu.VMEM((2, 3 * HALO, depth, lanes), jnp.float32)],
        compiler_params=params(),
        cost_estimate=cost(1),
        name="moments",
    )(populations)


def decode_rows(first, second, rows):
    rows[0], rows[1] = below_above("cross", decode(first[...]), decode(second[...]))


def place_plane(ext, p, vel_ref, rows, z):
    width = vel_ref.shape[2]
    for dim in range(3):
        ext[dim, p, pl.ds(OWN, width), :] = vel_ref[dim, z]
        for k in range(HALO):
            line = pl.ds(z, 1)
            ext[dim, p, pl.ds(OWN - 1 - k, 1), :] = rows[0, dim * HALO + k, line, :]
            ext[dim, p, pl.ds(OWN + width + k, 1), :] = rows[1, dim * HALO + k, line, :]


TALL = 40


def edges_kernel(
    vel_ref,
    low_ref,
    high_ref,
    cell_ref,
    weight_ref,
    segment_ref,
    first,
    second,
    rows,
    planes,
    note,
    coded,
):
    depth, width = vel_ref.shape[1:3]
    taps = cell_ref.shape[0]
    decode_rows(low_ref, high_ref, rows)
    fixed = weight_ref[...] * 2.0**16
    coarse = jnp.round(fixed)
    note[...] = jnp.zeros_like(note)
    note[pl.ds(0, taps), :] = cell_ref[...].astype(jnp.float32) - 2.0**15
    note[pl.ds(taps, taps), :] = coarse
    note[pl.ds(2 * taps, taps), :] = jnp.round((fixed - coarse) * 2.0**15)
    note[pl.ds(3 * taps, 1), :] = segment_ref[...].astype(jnp.float32)
    for side, pair in enumerate(((0, 1), (depth - 1, depth - 2))):
        planes[...] = jnp.zeros_like(planes)
        for dim in range(3):
            for index, z in enumerate(pair):
                slot = 2 * dim + index
                planes[slot, pl.ds(HALO, width), :] = vel_ref[dim, z]
                for k in range(HALO):
                    line = pl.ds(z, 1)
                    planes[slot, pl.ds(HALO - 1 - k, 1), :] = rows[0, dim * HALO + k, line, :]
                    planes[slot, pl.ds(HALO + width + k, 1), :] = rows[1, dim * HALO + k, line, :]
        coded[side, pl.ds(0, 6)] = encode(planes[...])
        coded[side, 6] = note[...].astype(jnp.int32).astype(jnp.int16)
    send_pair("span", coded[1], coded[0], first, second)


def edge_planes(vel, low, high, cells, weights, segments):
    pair = full((7, TALL, LANES), jnp.int16)
    return pl.pallas_call(
        edges_kernel,
        out_shape=(pair, pair),
        in_specs=in_vmem(6),
        out_specs=tuple(in_vmem(2)),
        scratch_shapes=[
            pltpu.VMEM((2, 3 * HALO, vel.shape[1], LANES), jnp.float32),
            pltpu.VMEM((6, TALL, LANES), jnp.float32),
            pltpu.VMEM((TALL, LANES), jnp.float32),
            pltpu.VMEM((2, 7, TALL, LANES), jnp.int16),
        ],
        compiler_params=params(),
        cost_estimate=cost(0.2),
        name="edges",
    )(vel, low, high, cells, weights, segments)


def plane_loop(start, stop, body, carry, most):
    count = stop - start
    step = max(size for size in range(1, most + 1) if count % size == 0)

    def block(index, carry):
        for shift in range(step):
            carry = body(start + index * step + shift, carry)
        return carry

    if count == step:
        return block(0, carry)
    return lax.fori_loop(0, count // step, block, carry)


def strain_parts(ref, p, row, before, here, after):
    grads = [
        (
            plus(here[dim]) - minus(here[dim]),
            ref[dim, p, pl.ds(row + 1, 8), :] - ref[dim, p, pl.ds(row - 1, 8), :],
            after[dim] - before[dim],
        )
        for dim in range(3)
    ]
    parts = [
        grads[0][0],
        grads[1][1],
        grads[2][2],
        grads[0][1] + grads[1][0],
        grads[0][2] + grads[2][0],
        grads[1][2] + grads[2][1],
    ]
    straight = parts[0] * parts[0] + parts[1] * parts[1] + parts[2] * parts[2]
    mixed = parts[3] * parts[3] + parts[4] * parts[4] + parts[5] * parts[5]
    return parts, jnp.sqrt(0.5 * straight + 0.25 * mixed)


def weigh(low, middle, high):
    return (low + high) + (middle + middle)


PAIRS = ((0, 0), (1, 1), (2, 2), (0, 1), (0, 2), (1, 2))


def three(ref, p, rows):
    return [ref[dim, p, rows, :] for dim in range(3)]


def model_sums(planes, ext, hat, zsum, zvel, acc_ref, store_mag):
    for row in CHUNKS:
        rows = pl.ds(row, 8)

        def first_pass(p, carry):
            before, here, lag, last = carry
            after = three(ext, p + 1, rows)
            parts, size = strain_parts(ext, p, row, before, here, after)
            store_mag(p, row, size)
            prods = [size * part for part in parts] + [here[i] * here[j] for i, j in PAIRS]
            for k in range(12):
                zsum[k, p - 1, rows, :] = lag[k] + prods[k]
            for dim in range(3):
                zvel[dim, p, rows, :] = weigh(before[dim], here[dim], after[dim])
            lag = [last[k] + (prods[k] + prods[k]) for k in range(12)]
            return here, after, lag, prods

        none = [jnp.zeros((8, LANES), jnp.float32)] * 12
        carry = (three(ext, 0, rows), three(ext, 1, rows), none, none)
        plane_loop(1, planes - 1, first_pass, carry, 14)

    def second_pass(p, carry):
        for row in CHUNKS:
            for dim in range(3):
                line = weigh(*[zvel[dim, p, pl.ds(row + shift, 8), :] for shift in (-1, 0, 1)])
                hat[dim, p, pl.ds(row, 8), :] = (1.0 / 64.0) * weigh(minus(line), line, plus(line))
        return carry

    plane_loop(1, planes - 1, second_pass, 0, 14)

    for row in CHUNKS:
        rows = pl.ds(row, 8)

        def third_pass(p, carry):
            before, here, lm, mm = carry
            after = three(hat, p + 1, rows)
            parts, size = strain_parts(hat, p, row, before, here, after)
            size = 256.0 * size
            scaled = [64.0 * speed for speed in here]
            squares = [0.0, 0.0]
            for k, (i, j) in enumerate(PAIRS):
                smooth = []
                for field in (k, 6 + k):
                    line = weigh(
                        *[zsum[field, p, pl.ds(row + shift, 8), :] for shift in (-1, 0, 1)]
                    )
                    smooth.append(weigh(minus(line), line, plus(line)))
                model = smooth[0] - size * parts[k]
                lm = lm + (smooth[1] - scaled[i] * here[j]) * model
                squares[k // 3] = squares[k // 3] + model * model
            return here, after, lm, mm + (squares[0] + 0.5 * squares[1])

        none = jnp.zeros((8, LANES), jnp.float32)
        carry = (three(hat, 1, rows), three(hat, 2, rows), none, none)
        _, _, lm, mm = plane_loop(2, planes - 2, third_pass, carry, 12)
        out = pl.ds(row - TOP, 8)
        acc_ref[0, out, :] += (1.0 / 4096.0) * lm
        acc_ref[1, out, :] += (1.0 / 4096.0) * mm


def inner_kernel(vel_ref, low_ref, high_ref, acc_ref, mag_ref, ext, hat, zsum, zvel, rows):
    depth = vel_ref.shape[1]
    decode_rows(low_ref, high_ref, rows)

    def assemble(p, carry):
        place_plane(ext, p, vel_ref, rows, p)
        return carry

    lax.fori_loop(0, depth, assemble, 0)
    acc_ref[...] = jnp.zeros_like(acc_ref)

    def store_mag(p, row, size):
        mag_ref[p - 1, pl.ds(row - TOP, 8), :] = size

    model_sums(depth, ext, hat, zsum, zvel, acc_ref, store_mag)


def model_scratch(planes, depth):
    return [
        pltpu.VMEM((3, planes, PAD, LANES), jnp.float32),
        pltpu.VMEM((3, planes, PAD, LANES), jnp.float32),
        pltpu.VMEM((12, planes, PAD, LANES), jnp.float32),
        pltpu.VMEM((3, planes, PAD, LANES), jnp.float32),
        pltpu.VMEM((2, 3 * HALO, depth, LANES), jnp.float32),
    ]


def inner_sums(vel, low, high):
    depth = vel.shape[1]
    return pl.pallas_call(
        inner_kernel,
        out_shape=(
            full((2, EXT, LANES), jnp.float32),
            full((depth - 2, EXT, LANES), jnp.float32),
        ),
        in_specs=in_vmem(3),
        out_specs=tuple(in_vmem(2)),
        scratch_shapes=model_scratch(depth, depth),
        compiler_params=params(),
        cost_estimate=cost(5),
        name="inner_sums",
    )(vel, low, high)


def outer_kernel(
    vel_ref,
    low_ref,
    high_ref,
    first_ref,
    second_ref,
    partial_ref,
    sums_ref,
    mag_ref,
    ext,
    hat,
    zsum,
    zvel,
    rows,
    acc,
):
    depth, width = vel_ref.shape[1:3]
    decode_rows(low_ref, high_ref, rows)
    acc[...] = partial_ref[...]
    below, above = below_above(
        "span", decode(first_ref[pl.ds(0, 6)]), decode(second_ref[pl.ds(0, 6)])
    )
    for side, (message, places, start) in enumerate(
        ((below, (1, 0), 0), (above, (4, 5), depth - 4))
    ):
        for index in range(4):
            place_plane(ext, index + (2 if side == 0 else 0), vel_ref, rows, start + index)
        for dim in range(3):
            for index, p in enumerate(places):
                ext[dim, p, pl.ds(OWN - HALO, TALL), :] = message[2 * dim + index]

        def store_mag(p, row, size):
            mag_ref[4 * side + p - 1, pl.ds(row - TOP, 8), :] = size

        model_sums(6, ext, hat, zsum, zvel, acc, store_mag)
    lines = width + 2
    sums_ref[...] = jnp.zeros_like(sums_ref)
    for index in range(2):
        sums_ref[pl.ds(index * lines, lines), :] = acc[index, pl.ds(OWN - TOP - 1, lines), :]


def outer_sums(vel, low, high, below, above, partial):
    depth, width = vel.shape[1:3]
    return pl.pallas_call(
        outer_kernel,
        out_shape=(
            full((-(-2 * (width + 2) // 8) * 8, LANES), jnp.float32),
            full((8, EXT, LANES), jnp.float32),
        ),
        in_specs=in_vmem(6),
        out_specs=tuple(in_vmem(2)),
        scratch_shapes=model_scratch(6, depth) + [pltpu.VMEM((2, EXT, LANES), jnp.float32)],
        compiler_params=params(),
        cost_estimate=cost(2),
        name="outer_sums",
    )(vel, low, high, below, above, partial)


def rows_kernel(pops, after_this, first, second, rows):
    depth, width = pops.shape[1:3]

    def plane(z, carry):
        for q in range(19):
            low = pops[q, z, pl.ds(0, 16), :].astype(jnp.float32)
            high = pops[q, z, pl.ds(width - 16, 16), :].astype(jnp.float32)
            rows[0, q, pl.ds(z, 1), :] = low[:1]
            rows[1, q, pl.ds(z, 1), :] = high[15:]
        return carry

    lax.fori_loop(0, depth, plane, 0)
    send_pair(
        "cross", rows[1].astype(jnp.bfloat16), rows[0].astype(jnp.bfloat16), first, second
    )


def face_rows(populations, after_this):
    _, depth, width, lanes = populations.shape
    edge = full((19, depth, lanes), jnp.bfloat16)
    return pl.pallas_call(
        rows_kernel,
        out_shape=(edge, edge),
        in_specs=in_vmem(1) + [pl.BlockSpec(memory_space=pl.ANY)],
        out_specs=tuple(in_vmem(2)),
        scratch_shapes=[pltpu.VMEM((2, 19, depth, lanes), jnp.float32)],
        compiler_params=params(),
        cost_estimate=cost(0.5),
        name="face_rows",
    )(populations, after_this)


def relax_parts(f):
    even = {q: f[q] + f[q + 1] for q in range(1, 19, 2)}
    odd = {q: f[q] - f[q + 1] for q in range(1, 19, 2)}
    x_xy, x_xz = odd[7] + odd[9], odd[11] + odd[13]
    y_yz, y_xy = odd[15] + odd[17], odd[7] - odd[9]
    z_xz, z_yz = odd[11] - odd[13], odd[15] - odd[17]
    flux, up, down, axis_odd = [], [], [], []
    for first, second, along in ((x_xy, x_xz, 1), (y_yz, y_xy, 3), (z_xz, z_yz, 5)):
        sides = first + second
        total = odd[along] + sides
        heat = 0.15 * (sides - (2.0 / 3.0) * total)
        twist = (1.98 / 8.0) * (first - second)
        flux.append(total)
        up.append(heat + twist)
        down.append(heat - twist)
        axis_odd.append(4.0 * heat)
    a, b, c = even[7] + even[9], even[11] + even[13], even[15] + even[17]
    axes = even[1] + even[3] + even[5]
    diagonals = a + b + c
    density = f[0] + axes + diagonals
    inverse = 1.0 / density
    speed = [total * inverse for total in flux]
    square = [total * part for total, part in zip(flux, speed)]
    energy = square[0] + square[1] + square[2]
    d_e = (1.19 / 126.0) * (diagonals - f[0] - energy)
    d_eps = (1.4 / 252.0) * (9.0 * f[0] - 7.0 * axes - 2.0 * diagonals + 5.5 * energy)
    ax_n, dg_n, eq_n = 3.0 * even[1] - axes, diagonals - 3.0 * c, 3.0 * square[0] - energy
    ax_w, dg_w, eq_w = even[3] - even[5], a - b, square[1] - square[2]
    d_pn = (1.4 / 72.0) * (dg_n - 2.0 * ax_n + 0.5 * eq_n)
    d_pw = (1.4 / 24.0) * (dg_w - 2.0 * ax_w + 0.5 * eq_w)
    shear = [
        (1.0 / 36.0) * (ax_n + dg_n - eq_n),
        (1.0 / 12.0) * (ax_w + dg_w - eq_w),
        0.25 * (even[7] - even[9] - flux[0] * speed[1]),
        0.25 * (even[11] - even[13] - flux[0] * speed[2]),
        0.25 * (even[15] - even[17] - flux[1] * speed[2]),
    ]
    base_axis = 11.0 * d_e + 4.0 * d_eps
    base_diag = -8.0 * d_e - d_eps
    base = [None] * 19
    base[0] = f[0] + (30.0 * d_e - 12.0 * d_eps)
    rest = base_axis - 2.0 * d_pn
    for q, change, skew in (
        (1, base_axis + 4.0 * d_pn, axis_odd[0]),
        (3, rest + 2.0 * d_pw, axis_odd[1]),
        (5, rest - 2.0 * d_pw, axis_odd[2]),
    ):
        base[q] = f[q] + (change + skew)
        base[q + 1] = f[q + 1] + (change - skew)
    rest = base_diag - d_pn
    for q, change, one, two in (
        (7, rest - d_pw, up[0], down[1]),
        (11, rest + d_pw, down[0], up[2]),
        (15, base_diag + 2.0 * d_pn, up[1], down[2]),
    ):
        same, other = one + two, one - two
        base[q] = f[q] + (change - same)
        base[q + 1] = f[q + 1] + (change + same)
        base[q + 2] = f[q + 2] + (change - other)
        base[q + 3] = f[q + 3] + (change + other)
    return base, shear


def shear_changes(shear, rate):
    n, w, xy, xz, yz = [rate * part for part in shear]
    lean = n + w
    tilt = n - w
    twice = n + n
    changes = [None] * 19
    changes[1] = changes[2] = -twice
    changes[3] = changes[4] = tilt
    changes[5] = changes[6] = lean
    changes[7] = changes[8] = -(lean + xy)
    changes[9] = changes[10] = xy - lean
    changes[11] = changes[12] = -(tilt + xz)
    changes[13] = changes[14] = xz - tilt
    changes[15] = changes[16] = twice - yz
    changes[17] = changes[18] = twice + yz
    return changes


def relax_rate(eddy, size):
    return 1.0 / (0.5 + 3.0 * (base_visc + eddy * size))


BEFORE = [q for q in range(19) if VELOCITIES[q][1] > 0]
AFTER = [q for q in range(19) if VELOCITIES[q][1] < 0]
RISING = [q for q in range(19) if VELOCITIES[q][2] > 0]
FALLING = [q for q in range(19) if VELOCITIES[q][2] < 0]
FIRST = 8


def ready_kernel(pops, first, second, after_this, base_ref, shear_ref, edge_ref, edge_shear):
    depth, width = pops.shape[1:3]
    rows = [
        below_above("cross", first[q].astype(jnp.float32), second[q].astype(jnp.float32))
        for q in range(19)
    ]
    for side, wanted in enumerate((BEFORE, AFTER)):
        base, shear = relax_parts([pair[side] for pair in rows])
        for index, q in enumerate(wanted):
            edge_ref[side, index] = base[q]
        for k in range(5):
            edge_shear[side, k] = shear[k]

    def plane(z, carry):
        for half in range(width // 16):
            rows = pl.ds(16 * half, 16)
            base, shear = relax_parts([pops[q, z, rows, :].astype(jnp.float32) for q in range(19)])
            for q in range(19):
                base_ref[q, z, rows, :] = base[q]
            for k in range(5):
                shear_ref[k, z, rows, :] = shear[k]
        return carry

    lax.fori_loop(0, depth, plane, 0)


def ready(populations, before, after, after_this):
    _, depth, width, lanes = populations.shape
    return pl.pallas_call(
        ready_kernel,
        out_shape=(
            full((19, depth, width, lanes), jnp.float32),
            full((5, depth, width, lanes), jnp.float32),
            full((2, 5, depth, lanes), jnp.float32),
            full((2, 5, depth, lanes), jnp.float32),
        ),
        in_specs=in_vmem(3) + [pl.BlockSpec(memory_space=pl.ANY)],
        out_specs=tuple(in_vmem(4)),
        compiler_params=params(),
        cost_estimate=cost(2.5),
        name="ready",
    )(populations, before, after, after_this)


def table_rows(table, at, low_at, flux):
    for dim in range(3):
        coarse, fine = split(flux[dim])
        table[at, dim * LANES : (dim + 1) * LANES] = coarse
        table[low_at, dim * LANES : (dim + 1) * LANES] = fine


def add_flux(flux, q, moved):
    for dim in range(3):
        sign = VELOCITIES[q][dim]
        if sign:
            flux[dim] = flux[dim] + moved if sign > 0 else flux[dim] - moved


def marker_force(table, picks, lanes, weights, taps):
    lane_of = lax.broadcasted_iota(jnp.int32, (LANES, lanes[0].shape[1]), 0)
    picked = lax.dot_general(
        table,
        jnp.concatenate(picks, axis=1),
        (((0,), (0,)), ((), ())),
        preferred_element_type=jnp.float32,
    )
    markers = lanes[0].shape[1]
    force = [0.0, 0.0, 0.0]
    for tap, (lane, weight) in enumerate(zip(lanes, weights)):
        mask = jnp.where(lane_of == lane, -weight, 0.0)
        at = slice(tap * markers, (tap + 1) * markers)
        for dim in range(3):
            force[dim] = force[dim] + picked[dim * LANES : (dim + 1) * LANES, at] * mask
        if (tap + 1) % taps == 0:
            yield [jnp.sum(part, axis=0, keepdims=True) for part in force]
            force = [0.0, 0.0, 0.0]


def step_kernel(
    base_ref,
    shear_ref,
    edge_ref,
    edge_shear,
    sums_ref,
    mag_in_ref,
    mag_out_ref,
    cell_ref,
    weight_ref,
    segment_ref,
    note_first,
    note_second,
    next_hbm,
    eddy_ref,
    partial_ref,
    first_ref,
    second_ref,
    post,
    nexts,
    table,
    face_table,
    faces,
    eddy,
    line,
    out_sems,
):
    depth, width = shear_ref.shape[1:3]
    lines = width + 2
    part = depth // 4
    eddy[...] = jnp.zeros_like(eddy)
    eddy[pl.ds(OWN - TOP - 1, lines), :] = jnp.maximum(
        sums_ref[pl.ds(0, lines), :] / (sums_ref[pl.ds(lines, lines), :] + eps_sum), 0.0
    )
    eddy_ref[...] = eddy[pl.ds(OWN - TOP, width), :]

    for side, (wanted, row, place) in enumerate(
        ((BEFORE, OWN - TOP - 1, FIRST - 1), (AFTER, OWN - TOP + width, FIRST + width))
    ):
        for z in range(depth):
            if z == 0:
                size = mag_out_ref[1, pl.ds(row, 1), :]
            elif z == depth - 1:
                size = mag_out_ref[6, pl.ds(row, 1), :]
            else:
                size = mag_in_ref[z - 1, pl.ds(row, 1), :]
            line[pl.ds(z, 1), :] = size
        rate = relax_rate(eddy[pl.ds(row, 1), :], line[...])
        changes = shear_changes([edge_shear[side, k] for k in range(5)], rate)
        for index, q in enumerate(wanted):
            out = edge_ref[side, index] + changes[q]
            for z in range(depth):
                post[q, z, pl.ds(place, 1), :] = out[z : z + 1]

    def collide(z, size_ref, at):
        for half in range(width // 16):
            rows = pl.ds(16 * half, 16)
            around = pl.ds(OWN - TOP + 16 * half, 16)
            rate = relax_rate(eddy[around, :], size_ref[at, around, :])
            changes = shear_changes([shear_ref[k, z, rows, :] for k in range(5)], rate)
            for q in range(19):
                value = base_ref[q, z, rows, :]
                if q:
                    value = value + changes[q]
                post[q, z, pl.ds(FIRST + 16 * half, 16), :] = value

    def inner(z, carry):
        collide(z, mag_in_ref, z - 1)
        return carry

    collide(0, mag_out_ref, 1)
    collide(depth - 1, mag_out_ref, 6)
    lax.fori_loop(1, depth - 1, inner, 0)

    def shifted(q, z, half):
        shift_x, shift_y, _ = VELOCITIES[q]
        piece = post[q, z, pl.ds(FIRST + 16 * half - shift_y, 16), :]
        if shift_x:
            piece = minus(piece) if shift_x > 0 else plus(piece)
        return piece.astype(jnp.bfloat16)

    def run(z, leave_out=()):
        for half in range(width // 16):
            flux = [0.0, 0.0, 0.0]
            for q in range(19):
                if q in leave_out:
                    continue
                moved = shifted(q, z - VELOCITIES[q][2], half)
                nexts[q, z, pl.ds(16 * half, 16), :] = moved
                if q:
                    add_flux(flux, q, moved.astype(jnp.float32))
            row = pl.multiple_of(z * width + 16 * half, 16)
            low_row = pl.multiple_of((depth + z) * width + 16 * half, 16)
            table_rows(table, pl.ds(row, 16), pl.ds(low_row, 16), flux)

    def run_inner(z, carry):
        run(z)
        return carry

    for side, (wanted, z) in enumerate(((RISING, depth - 1), (FALLING, 0))):
        for half in range(width // 16):
            rows = pl.ds(16 * half, 16)
            flux = [0.0, 0.0, 0.0]
            for index, q in enumerate(wanted):
                moved = shifted(q, z, half)
                faces[side, index, rows, :] = moved
                add_flux(flux, q, moved.astype(jnp.float32))
            row = side * width + 16 * half
            table_rows(face_table, pl.ds(row, 16), pl.ds(2 * width + row, 16), flux)
    send_pair("span", faces[0], faces[1], first_ref, second_ref)

    outs = []
    for index in range(4):
        start, stop = index * part, (index + 1) * part
        if index == 0:
            run(0, RISING)
            start += 1
        if index == 3:
            run(depth - 1, FALLING)
            stop -= 1
        lax.fori_loop(start, stop, run_inner, 0)
        place = pl.ds(index * part, part)
        outs.append(
            pltpu.make_async_copy(nexts.at[:, place], next_hbm.at[:, place], out_sems.at[index])
        )
        outs[-1].start()

    owners = partial_ref.shape[0]
    taps, markers = cell_ref.shape
    cells_all = depth * width
    note_below, note_above = below_above(
        "span", note_first[6].astype(jnp.int32), note_second[6].astype(jnp.int32)
    )

    def one_hot(rows, period, wanted):
        row_of = lax.broadcasted_iota(jnp.int32, (period, markers), 0)
        picks = []
        for tap in range(taps):
            hit = jnp.where(row_of == wanted[tap : tap + 1, :], 1.0, 0.0).astype(jnp.bfloat16)
            picks.append(jnp.concatenate([hit] * (rows // period), axis=0))
        return picks

    def row_lane(cells):
        return lax.shift_right_logical(cells, 7), lax.bitwise_and(cells, LANES - 1)

    def each(array):
        return [array[tap : tap + 1, :] for tap in range(taps)]

    row, lane = row_lane(cell_ref[...])
    forces = list(
        marker_force(
            table[...],
            one_hot(2 * cells_all, cells_all, row),
            each(lane),
            each(weight_ref[...]),
            taps,
        )
    )
    segments = [segment_ref[...]]
    picks, lanes, weights = [], [], []
    for side, note in enumerate((note_above, note_below)):
        row, lane = row_lane(note[:taps] + 2**15)
        row = row - side * (cells_all - width)
        inside = jnp.logical_and(row >= 0, row < width)
        picks += one_hot(4 * width, 2 * width, jnp.where(inside, row + side * width, -1))
        lanes += each(lane)
        weights += each(
            note[taps : 2 * taps].astype(jnp.float32) * 2.0**-16
            + note[2 * taps : 3 * taps].astype(jnp.float32) * 2.0**-31
        )
        segments.append(note[3 * taps : 3 * taps + 1])
    forces += list(marker_force(face_table[...], picks, lanes, weights, taps))

    owner_of = lax.broadcasted_iota(jnp.int32, (owners, markers), 0)
    place_of = lax.broadcasted_iota(jnp.int32, (SEG_DEV, markers), 0)
    mine, spread = [], []
    for force, segment in zip(forces, segments):
        hit = jnp.where(owner_of == lax.shift_right_logical(segment, 3), 1.0, 0.0)
        mine.append(hit.astype(jnp.bfloat16))
        place = place_of == lax.bitwise_and(segment, SEG_DEV - 1)
        spread.append(
            jnp.concatenate([jnp.where(place, part, 0.0) for part in force], axis=0)
        )
    mine, rest = jnp.concatenate(mine, axis=1), jnp.concatenate(spread, axis=1)
    rest = jnp.concatenate([rest, jnp.zeros((LANES - 3 * SEG_DEV, 3 * markers), jnp.float32)], axis=0)
    totals = 0.0
    for _ in range(3):
        coarse = rest.astype(jnp.bfloat16)
        rest = rest - coarse.astype(jnp.float32)
        totals = totals + lax.dot_general(
            mine, coarse, (((1,), (1,)), ((), ())), preferred_element_type=jnp.float32
        )
    partial_ref[:, 0, :] = totals
    for copy in outs:
        copy.wait()


def step(parts, sums, mag_in, mag_out, cells, weights, segments, notes, owners):
    _, depth, width, lanes = parts[0].shape
    face = full((5, width, lanes), jnp.bfloat16)
    return pl.pallas_call(
        step_kernel,
        out_shape=(
            full((19, depth, width, lanes), jnp.bfloat16),
            full((width, lanes), jnp.float32),
            full((owners, 1, lanes), jnp.float32),
            face,
            face,
        ),
        in_specs=in_vmem(12),
        out_specs=(pl.BlockSpec(memory_space=pl.ANY),) + tuple(in_vmem(4)),
        scratch_shapes=[
            pltpu.VMEM((19, depth, FIRST + width + 8, lanes), jnp.float32),
            pltpu.VMEM((19, depth, width, lanes), jnp.bfloat16),
            pltpu.VMEM((2 * depth * width, 3 * lanes), jnp.bfloat16),
            pltpu.VMEM((4 * width, 3 * lanes), jnp.bfloat16),
            pltpu.VMEM((2, 5, width, lanes), jnp.bfloat16),
            pltpu.VMEM((EXT, lanes), jnp.float32),
            pltpu.VMEM((depth, lanes), jnp.float32),
            pltpu.SemaphoreType.DMA((4,)),
        ],
        compiler_params=params(),
        cost_estimate=cost(5),
        name="step",
    )(*parts, sums, mag_in, mag_out, cells, weights, segments, *notes)


def arrive_kernel(next_in, first, second, arrived_hbm, next_hbm, force_ref, arrived, sems):
    depth = next_hbm.shape[1]
    odd = is_odd("span")
    shares = pltpu.make_async_copy(arrived_hbm, arrived, sems.at[10])
    shares.start()

    def place(below, above):
        copies = []
        for source, wanted, z in ((below, RISING, 0), (above, FALLING, depth - 1)):
            for index, q in enumerate(wanted):
                copies.append(
                    pltpu.make_async_copy(source.at[index], next_hbm.at[q, z], sems.at[len(copies)])
                )
                copies[-1].start()
        for copy in copies:
            copy.wait()

    @pl.when(odd)
    def _():
        place(first, second)

    @pl.when(jnp.logical_not(odd))
    def _():
        place(second, first)

    shares.wait()
    total = jnp.sum(arrived[:, 0, :], axis=0, keepdims=True)
    for dim in range(3):
        force_ref[pl.ds(dim, 1), :] = total[:, dim * SEG_DEV : (dim + 1) * SEG_DEV]


def arrive(populations_next, first, second, arrived):
    hbm = pl.BlockSpec(memory_space=pl.ANY)
    return pl.pallas_call(
        arrive_kernel,
        out_shape=(
            full(populations_next.shape, jnp.bfloat16),
            full((3, SEG_DEV), jnp.float32),
        ),
        in_specs=[hbm] + in_vmem(2) + [hbm],
        out_specs=(hbm, in_vmem(1)[0]),
        input_output_aliases={0: 0},
        scratch_shapes=[
            pltpu.VMEM(arrived.shape, jnp.float32),
            pltpu.SemaphoreType.DMA((11,)),
        ],
        compiler_params=params(),
        cost_estimate=cost(0.5),
        name="arrive",
    )(populations_next, first, second, arrived)


def local(populations, cell_index, marker_weight, segment_id):
    owners = lax.axis_size("span") * lax.axis_size("cross")
    cells, weights, segments = cell_index.T, marker_weight.T, segment_id[None, :]
    vel, *lines = block_moments(populations)
    lines = swap(*lines, "cross")
    planes = swap(*edge_planes(vel, *lines, cells, weights, segments), "span")
    partial, mag_in = inner_sums(vel, *lines)
    faces = swap(*face_rows(populations, partial), "cross")
    sums, mag_out = outer_sums(vel, *lines, *planes, partial)
    parts = ready(populations, *faces, sums)
    count = lax.axis_size("span")
    if count & (count - 1):
        sums = lax.psum(sums, "span")
    else:
        distance = 1
        while distance < count:
            pairs = [(i, i ^ distance) for i in range(count)]
            sums = sums + lax.ppermute(sums, "span", pairs)
            distance *= 2
    moved, eddy_coeff, packed, *leaving = step(
        parts, sums, mag_in, mag_out, cells, weights, segments, planes, owners
    )
    arrived = lax.all_to_all(packed, ("span", "cross"), 0, 0)
    populations_next, segment_force = arrive(moved, *swap(*leaving, "span"), arrived)
    return (populations_next, eddy_coeff, segment_force)


def solution(mesh):
    in_specs = (
        P(None, "span", "cross", None),
        P(("span", "cross"), None),
        P(("span", "cross"), None),
        P(("span", "cross")),
    )
    out_specs = (P(None, "span", "cross", None), P("cross", None), P(None, ("span", "cross")))
    return jax.shard_map(local, mesh=mesh, in_specs=in_specs, out_specs=out_specs, check_vma=False)
```

profile of v0, /device:TPU:0, one launch (start us, length us, event | category | flops | bytes accessed | tf_op | source)
XLA Modules:
  0.0 51.7 jit_solution(7538380670808082672)
XLA Ops:
  0.6 1.7 %copy-done = bf16[19,16,32,128]{3,2,1,0:T(8,128)(2,1)S(1)} copy-done((bf16[19,16,32,128]{3,2,1,0:T(8,128)(2,1)S(1)}, bf16[19,16,32,128]{3,2,1,0:T(8,128)(2,1)}, u32[]{:S(2)}) %copy-start) | copy-done | bytes 2490392
  2.3 0.7 %moments.1 = (f32[3,16,32,128]{3,2,1,0:T(8,128)S(1)}, s16[9,16,128]{2,1,0:T(8,128)(2,1)S(1)}, s16[9,16,128]{2,1,0:T(8,128)(2,1)S(1)}) custom-call(bf16[19,16,32,128]{3,2,1,0:T(8,128)(2,1)S(1)} %copy-done), custom_call_target="tpu_custom_call" | custom-call | bytes 3600000 | tf_op jit(solution)/shard_map/moments/pallas_call | solution.py:150
  3.1 0.5 %collective-permute-start = (s16[9,16,128]{2,1,0:T(8,128)(2,1)S(1)}, s16[9,16,128]{2,1,0:T(8,128)(2,1)S(1)}, u32[]{:S(2)}, u32[]{:S(2)}) collective-permute-start(s16[9,16,128]{2,1,0:T(8,128)(2,1)S(1)} %get-tuple-element.26), channel_id=1, source_target_pairs={{0,1},{1,0},{2,3},{3,2},{4,5},{5,4},{6,7},{7,6},{8,9},{9,8},{10,11... | collective-permute-start | bytes 110600 | tf_op jit(solution)/shard_map/ppermute | solution.py:50
  3.6 2.6 %collective-permute-start.1 = (s16[9,16,128]{2,1,0:T(8,128)(2,1)S(1)}, s16[9,16,128]{2,1,0:T(8,128)(2,1)S(1)}, u32[]{:S(2)}, u32[]{:S(2)}) collective-permute-start(s16[9,16,128]{2,1,0:T(8,128)(2,1)S(1)} %get-tuple-element.27), channel_id=1, source_target_pairs={{0,3},{1,2},{2,1},{3,0},{4,7},{5,6},{6,5},{7,4},{8,11},{9,10},{10,... | collective-permute-start | bytes 110600 | tf_op jit(solution)/shard_map/ppermute | solution.py:50
  6.2 0.0 collective-permute-done.low_ref
  6.2 1.8 %collective-permute-done.1.high_ref = s16[9,16,128]{2,1,0:T(8,128)(2,1)S(1)} collective-permute-done((s16[9,16,128]{2,1,0:T(8,128)(2,1)S(1)}, s16[9,16,128]{2,1,0:T(8,128)(2,1)S(1)}, u32[]{:S(2)}, u32[]{:S(2)}) %collective-permute-start.1) | collective-permute-done | bytes 36896 | tf_op jit(solution)/shard_map/ppermute | solution.py:50
  8.0 0.1 edges.1
  8.1 1.6 %collective-permute-start.4 = (s16[7,40,128]{2,1,0:T(8,128)(2,1)S(1)}, s16[7,40,128]{2,1,0:T(8,128)(2,1)S(1)}, u32[]{:S(2)}, u32[]{:S(2)}) collective-permute-start(s16[7,40,128]{2,1,0:T(8,128)(2,1)S(1)} %get-tuple-element.31), channel_id=1, source_target_pairs={{0,4},{4,0},{8,12},{12,8},{16,20},{20,16},{24,28},{28,24},{1,5},{5... | collective-permute-start | bytes 215048 | tf_op jit(solution)/shard_map/ppermute | solution.py:50
  9.8 3.6 %collective-permute-start.5 = (s16[7,40,128]{2,1,0:T(8,128)(2,1)S(1)}, s16[7,40,128]{2,1,0:T(8,128)(2,1)S(1)}, u32[]{:S(2)}, u32[]{:S(2)}) collective-permute-start(s16[7,40,128]{2,1,0:T(8,128)(2,1)S(1)} %get-tuple-element.32), channel_id=1, source_target_pairs={{0,28},{4,8},{8,4},{12,16},{16,12},{20,24},{24,20},{28,0},{1,29},{... | collective-permute-start | bytes 215048 | tf_op jit(solution)/shard_map/ppermute | solution.py:50
  13.3 3.3 %inner_sums.1 = (f32[2,40,128]{2,1,0:T(8,128)S(1)}, f32[14,40,128]{2,1,0:T(8,128)S(1)}) custom-call(f32[3,16,32,128]{3,2,1,0:T(8,128)S(1)} %get-tuple-element.25.vel_ref, s16[9,16,128]{2,1,0:T(8,128)(2,1)S(1)} %collective-permute-done.low_ref, s16[9,16,128]{2,1,0:T(8,128)(2,1)S(1)} %collective-permute-done.1.high_ref), custom_call_target="tpu_custom_call" | custom-call | bytes 18000000 | tf_op jit(solution)/shard_map/inner_sums/pallas_call | solution.py:373
  16.6 0.0 collective-permute-done.4.first_ref.note_first
  16.6 0.2 collective-permute-done.5.second_ref.note_second
  16.8 1.4 %outer_sums.1 = (f32[72,128]{1,0:T(8,128)S(1)}, f32[8,40,128]{2,1,0:T(8,128)S(1)}) custom-call(f32[3,16,32,128]{3,2,1,0:T(8,128)S(1)} %get-tuple-element.25.vel_ref, s16[9,16,128]{2,1,0:T(8,128)(2,1)S(1)} %collective-permute-done.low_ref, s16[9,16,128]{2,1,0:T(8,128)(2,1)S(1)} %collective-permute-done.1.high_ref, ...), custom_call_target="tpu_custom_call" | custom-call | bytes 7200000 | tf_op jit(solution)/shard_map/outer_sums/pallas_call | solution.py:431
  18.2 0.1 collective-permute-start.6
  18.3 0.3 face_rows.1
  18.6 0.1 collective-permute-start.2
  18.7 1.6 %collective-permute-start.3 = (bf16[19,16,128]{2,1,0:T(8,128)(2,1)S(1)}, bf16[19,16,128]{2,1,0:T(8,128)(2,1)S(1)}, u32[]{:S(2)}, u32[]{:S(2)}) collective-permute-start(bf16[19,16,128]{2,1,0:T(8,128)(2,1)S(1)} %get-tuple-element.30), channel_id=1, source_target_pairs={{0,3},{1,2},{2,1},{3,0},{4,7},{5,6},{6,5},{7,4},{8,11},{9,10},{10,... | collective-permute-start | bytes 233480 | tf_op jit(solution)/shard_map/ppermute | solution.py:50
  20.3 1.9 %collective-permute-done.6 = f32[72,128]{1,0:T(8,128)S(1)} collective-permute-done((f32[72,128]{1,0:T(8,128)S(1)}, f32[72,128]{1,0:T(8,128)S(1)}, u32[]{:S(2)}, u32[]{:S(2)}) %collective-permute-start.6) | collective-permute-done | bytes 36896 | tf_op jit(solution)/shard_map/ppermute | solution.py:944
  22.2 0.0 collective-permute-start.7
  22.2 3.9 %collective-permute-done.7 = f32[72,128]{1,0:T(8,128)S(1)} collective-permute-done((f32[72,128]{1,0:T(8,128)S(1)}, f32[72,128]{1,0:T(8,128)S(1)}, u32[]{:S(2)}, u32[]{:S(2)}) %collective-permute-start.7) | collective-permute-done | bytes 36896 | tf_op jit(solution)/shard_map/ppermute | solution.py:944
  26.2 0.8 %collective-permute-start.8 = (f32[72,128]{1,0:T(8,128)S(1)}, f32[72,128]{1,0:T(8,128)S(1)}, u32[]{:S(2)}, u32[]{:S(2)}) collective-permute-start(f32[72,128]{1,0:T(8,128)S(1)} %add.10), channel_id=1, source_target_pairs={{0,16},{4,20},{8,24},{12,28},{16,0},{20,4},{24,8},{28,12},{1,17},{... | collective-permute-start | bytes 110600 | tf_op jit(solution)/shard_map/ppermute | solution.py:944
  27.0 0.0 collective-permute-done.2.first
  27.0 0.0 collective-permute-done.3.second
  27.0 2.1 %ready.1 = (f32[19,16,32,128]{3,2,1,0:T(8,128)S(1)}, f32[5,16,32,128]{3,2,1,0:T(8,128)S(1)}, f32[2,5,16,128]{3,2,1,0:T(8,128)S(1)}, f32[2,5,16,128]{3,2,1,0:T(8,128)S(1)}) custom-call(bf16[19,16,32,128]{3,2,1,0:T(8,128)(2,1)S(1)} %copy-done.1, bf16[19,16,128]{2,1,0:T(8,128)(2,1)S(1)} %collective-permute-done.2.first, ...), custom_call_target="tpu_custom_call" | custom-call | bytes 9000000 | tf_op jit(solution)/shard_map/ready/pallas_call | solution.py:598
  29.1 2.0 %collective-permute-done.8 = f32[72,128]{1,0:T(8,128)S(1)} collective-permute-done((f32[72,128]{1,0:T(8,128)S(1)}, f32[72,128]{1,0:T(8,128)S(1)}, u32[]{:S(2)}, u32[]{:S(2)}) %collective-permute-start.8) | collective-permute-done | bytes 36896 | tf_op jit(solution)/shard_map/ppermute | solution.py:944
  31.1 5.1 %step.1 = (bf16[19,16,32,128]{3,2,1,0:T(8,128)(2,1)}, f32[32,128]{1,0:T(8,128)}, f32[32,1,128]{2,1,0:T(1,128)S(1)}, bf16[5,32,128]{2,1,0:T(8,128)(2,1)S(1)}, bf16[5,32,128]{2,1,0:T(8,128)(2,1)S(1)}) custom-call(f32[19,16,32,128]{3,2,1,0:T(8,128)S(1)} %get-tuple-element.34.base_ref, f32[5,16,32,128]{3,2,1,0:T(8,128)S(1)} %get-tuple-element.35.shear_ref, ...), custom_call_target="tpu_custom_call" | custom-call | bytes 18000000 | tf_op jit(solution)/shard_map/step/pallas_call | solution.py:848
  36.2 0.2 collective-permute-start.9
  36.3 3.6 %collective-permute-start.10 = (bf16[5,32,128]{2,1,0:T(8,128)(2,1)S(1)}, bf16[5,32,128]{2,1,0:T(8,128)(2,1)S(1)}, u32[]{:S(2)}, u32[]{:S(2)}) collective-permute-start(bf16[5,32,128]{2,1,0:T(8,128)(2,1)S(1)} %get-tuple-element.42), channel_id=1, source_target_pairs={{0,28},{4,8},{8,4},{12,16},{16,12},{20,24},{24,20},{28,0},{1,29},{... | collective-permute-start | bytes 122888 | tf_op jit(solution)/shard_map/ppermute | solution.py:50
  39.9 10.4 %all_to_all.5.arrived_hbm = f32[32,1,128]{2,1,0:T(1,128)S(1)} all-to-all(f32[32,1,128]{2,1,0:T(1,128)S(1)} %get-tuple-element.43), channel_id=1, replica_groups=mesh['span'=8,'cross'=4] {'span','cross'}, dimensions={0} | all-to-all | bytes 32768 | tf_op jit(solution)/shard_map/all_to_all | solution.py:949
  50.3 0.0 collective-permute-done.9.first
  50.3 0.0 collective-permute-done.10.second
  50.3 1.4 %arrive.1 = (bf16[19,16,32,128]{3,2,1,0:T(8,128)(2,1)}, f32[3,8]{1,0:T(4,128)}) custom-call(bf16[19,16,32,128]{3,2,1,0:T(8,128)(2,1)} %get-tuple-element.40.next_in, bf16[5,32,128]{2,1,0:T(8,128)(2,1)S(1)} %collective-permute-done.9.first, bf16[5,32,128]{2,1,0:T(8,128)(2,1)S(1)} %collective-permute-done.10.second, ...), custom_call_target="tpu_custom_call", output_to_operand_aliasing={{0}: (0, {})} | custom-call | bytes 1800000 | tf_op jit(solution)/shard_map/arrive/pallas_call | solution.py:908
  (12 shorter events, 0.0 us)
Async XLA Ops:
  0.6 1.7 %copy-start = (bf16[19,16,32,128]{3,2,1,0:T(8,128)(2,1)S(1)}, bf16[19,16,32,128]{3,2,1,0:T(8,128)(2,1)}, u32[]{:S(2)}) copy-start(bf16[19,16,32,128]{3,2,1,0:T(8,128)(2,1)} %pops.5) | copy-start | bytes 7471108
  2.3 5.7 %copy-start.2 = (s32[128,8]{0,1:T(8,128)S(1)}, s32[128,8]{0,1:T(8,128)}, u32[]{:S(2)}) copy-start(s32[128,8]{0,1:T(8,128)} %param.5) | copy-start | bytes 12292
  2.3 5.7 %copy-start.3 = (f32[128,8]{0,1:T(8,128)S(1)}, f32[128,8]{0,1:T(8,128)}, u32[]{:S(2)}) copy-start(f32[128,8]{0,1:T(8,128)} %param.6) | copy-start | bytes 12292
  2.3 5.7 %copy-start.4 = (s32[128]{0:T(128)S(1)}, s32[128]{0:T(128)}, u32[]{:S(2)}) copy-start(s32[128]{0:T(128)} %param.7) | copy-start | bytes 1540
  2.3 15.9 %copy-start.1 = (bf16[19,16,32,128]{3,2,1,0:T(8,128)(2,1)S(1)}, bf16[19,16,32,128]{3,2,1,0:T(8,128)(2,1)}, u32[]{:S(2)}) copy-start(bf16[19,16,32,128]{3,2,1,0:T(8,128)(2,1)} %pops.5) | copy-start | bytes 7471108
  3.1 3.2 %collective-permute-start = (s16[9,16,128]{2,1,0:T(8,128)(2,1)S(1)}, s16[9,16,128]{2,1,0:T(8,128)(2,1)S(1)}, u32[]{:S(2)}, u32[]{:S(2)}) collective-permute-start(s16[9,16,128]{2,1,0:T(8,128)(2,1)S(1)} %get-tuple-element.26), channel_id=1, source_target_pairs={{0,1},{1,0},{2,3},{3,2},{4,5},{5,4},{6,7},{7,6},{8,9},{9,8},{10,11... | collective-permute-start | bytes 110600 | tf_op jit(solution)/shard_map/ppermute | solution.py:50
  3.6 4.4 %collective-permute-start.1 = (s16[9,16,128]{2,1,0:T(8,128)(2,1)S(1)}, s16[9,16,128]{2,1,0:T(8,128)(2,1)S(1)}, u32[]{:S(2)}, u32[]{:S(2)}) collective-permute-start(s16[9,16,128]{2,1,0:T(8,128)(2,1)S(1)} %get-tuple-element.27), channel_id=1, source_target_pairs={{0,3},{1,2},{2,1},{3,0},{4,7},{5,6},{6,5},{7,4},{8,11},{9,10},{10,... | collective-permute-start | bytes 110600 | tf_op jit(solution)/shard_map/ppermute | solution.py:50
  8.1 8.4 %collective-permute-start.4 = (s16[7,40,128]{2,1,0:T(8,128)(2,1)S(1)}, s16[7,40,128]{2,1,0:T(8,128)(2,1)S(1)}, u32[]{:S(2)}, u32[]{:S(2)}) collective-permute-start(s16[7,40,128]{2,1,0:T(8,128)(2,1)S(1)} %get-tuple-element.31), channel_id=1, source_target_pairs={{0,4},{4,0},{8,12},{12,8},{16,20},{20,16},{24,28},{28,24},{1,5},{5... | collective-permute-start | bytes 215048 | tf_op jit(solution)/shard_map/ppermute | solution.py:50
  9.8 7.0 %collective-permute-start.5 = (s16[7,40,128]{2,1,0:T(8,128)(2,1)S(1)}, s16[7,40,128]{2,1,0:T(8,128)(2,1)S(1)}, u32[]{:S(2)}, u32[]{:S(2)}) collective-permute-start(s16[7,40,128]{2,1,0:T(8,128)(2,1)S(1)} %get-tuple-element.32), channel_id=1, source_target_pairs={{0,28},{4,8},{8,4},{12,16},{16,12},{20,24},{24,20},{28,0},{1,29},{... | collective-permute-start | bytes 215048 | tf_op jit(solution)/shard_map/ppermute | solution.py:50
  18.2 4.0 %collective-permute-start.6 = (f32[72,128]{1,0:T(8,128)S(1)}, f32[72,128]{1,0:T(8,128)S(1)}, u32[]{:S(2)}, u32[]{:S(2)}) collective-permute-start(f32[72,128]{1,0:T(8,128)S(1)} %get-tuple-element.33.after_this), channel_id=1, source_target_pairs={{0,4},{4,0},{8,12},{12,8},{16,20},{20,16},{24,28},{28,24},{1,5},{5... | collective-permute-start | bytes 110600 | tf_op jit(solution)/shard_map/ppermute | solution.py:944
  18.6 8.4 %collective-permute-start.2 = (bf16[19,16,128]{2,1,0:T(8,128)(2,1)S(1)}, bf16[19,16,128]{2,1,0:T(8,128)(2,1)S(1)}, u32[]{:S(2)}, u32[]{:S(2)}) collective-permute-start(bf16[19,16,128]{2,1,0:T(8,128)(2,1)S(1)} %get-tuple-element.29), channel_id=1, source_target_pairs={{0,1},{1,0},{2,3},{3,2},{4,5},{5,4},{6,7},{7,6},{8,9},{9,8},{10,11... | collective-permute-start | bytes 233480 | tf_op jit(solution)/shard_map/ppermute | solution.py:50
  18.7 8.3 %collective-permute-start.3 = (bf16[19,16,128]{2,1,0:T(8,128)(2,1)S(1)}, bf16[19,16,128]{2,1,0:T(8,128)(2,1)S(1)}, u32[]{:S(2)}, u32[]{:S(2)}) collective-permute-start(bf16[19,16,128]{2,1,0:T(8,128)(2,1)S(1)} %get-tuple-element.30), channel_id=1, source_target_pairs={{0,3},{1,2},{2,1},{3,0},{4,7},{5,6},{6,5},{7,4},{8,11},{9,10},{10,... | collective-permute-start | bytes 233480 | tf_op jit(solution)/shard_map/ppermute | solution.py:50
  22.2 4.0 %collective-permute-start.7 = (f32[72,128]{1,0:T(8,128)S(1)}, f32[72,128]{1,0:T(8,128)S(1)}, u32[]{:S(2)}, u32[]{:S(2)}) collective-permute-start(f32[72,128]{1,0:T(8,128)S(1)} %add.9), channel_id=1, source_target_pairs={{0,8},{4,12},{8,0},{12,4},{16,24},{20,28},{24,16},{28,20},{1,9},{5... | collective-permute-start | bytes 110600 | tf_op jit(solution)/shard_map/ppermute | solution.py:944
  26.2 4.9 %collective-permute-start.8 = (f32[72,128]{1,0:T(8,128)S(1)}, f32[72,128]{1,0:T(8,128)S(1)}, u32[]{:S(2)}, u32[]{:S(2)}) collective-permute-start(f32[72,128]{1,0:T(8,128)S(1)} %add.10), channel_id=1, source_target_pairs={{0,16},{4,20},{8,24},{12,28},{16,0},{20,4},{24,8},{28,12},{1,17},{... | collective-permute-start | bytes 110600 | tf_op jit(solution)/shard_map/ppermute | solution.py:944
  36.2 14.2 %collective-permute-start.9 = (bf16[5,32,128]{2,1,0:T(8,128)(2,1)S(1)}, bf16[5,32,128]{2,1,0:T(8,128)(2,1)S(1)}, u32[]{:S(2)}, u32[]{:S(2)}) collective-permute-start(bf16[5,32,128]{2,1,0:T(8,128)(2,1)S(1)} %get-tuple-element.41), channel_id=1, source_target_pairs={{0,4},{4,0},{8,12},{12,8},{16,20},{20,16},{24,28},{28,24},{1,5},{5... | collective-permute-start | bytes 122888 | tf_op jit(solution)/shard_map/ppermute | solution.py:50
  36.3 14.0 %collective-permute-start.10 = (bf16[5,32,128]{2,1,0:T(8,128)(2,1)S(1)}, bf16[5,32,128]{2,1,0:T(8,128)(2,1)S(1)}, u32[]{:S(2)}, u32[]{:S(2)}) collective-permute-start(bf16[5,32,128]{2,1,0:T(8,128)(2,1)S(1)} %get-tuple-element.42), channel_id=1, source_target_pairs={{0,28},{4,8},{8,4},{12,16},{16,12},{20,24},{24,20},{28,0},{1,29},{... | collective-permute-start | bytes 122888 | tf_op jit(solution)/shard_map/ppermute | solution.py:50
where the time goes:
time: 51.9 us; the launch traced here: 51.7 us
  starting transfers between devices  14.7 us (28%)
  Pallas kernels  14.4 us (28%)
  blocking collectives  10.4 us (20%)
  waiting for transfers between devices  9.83 us (19%)
  local copies, waits for them, and re-layouts  1.71 us (3%)
  between operations  0.74 us (1%)
    ppermute x8, starting transfers between devices, swap(): return (lax.ppermute(first, axis, near), lax.ppermute(second, axis, other))  13.8 us
    all_to_all x1, blocking collectives, local(): arrived = lax.all_to_all(packed, ('span', 'cross'), 0, 0)  10.4 us
    ppermute x3, waiting for transfers between devices, local(): sums = sums + lax.ppermute(sums, 'span', pairs)  7.87 us
    pallas_call x1, Pallas kernels, step(): pl.pallas_call(step_kernel, out_shape=(full((19, depth, width, lanes), jn...  5.08 us
    pallas_call x1, Pallas kernels, inner_sums(): pl.pallas_call(inner_kernel, out_shape=(full((2, EXT, LANES), jnp.float32...  3.25 us
    pallas_call x1, Pallas kernels, ready(): pl.pallas_call(ready_kernel, out_shape=(full((19, depth, width, lanes), j...  2.06 us
    ppermute x8, waiting for transfers between devices, swap(): return (lax.ppermute(first, axis, near), lax.ppermute(second, axis, other))  1.96 us
    unnamed x10, local copies, waits for them, and re-layouts  1.71 us
  transfers between devices with their start and end apart: 11, of which 5 were waited for; matrix products, arithmetic and copies ran while one was open for 0% of the time, Pallas kernels for 11%

commit v1 on v0

--- a/solution.py
+++ b/solution.py
@@ -111,6 +111,20 @@
 def split(value):
     high = value.astype(jnp.bfloat16)
     return high, (value - high.astype(jnp.float32)).astype(jnp.bfloat16)
+
+
+def plane_loop(start, stop, body, carry, most):
+    count = stop - start
+    step = max(size for size in range(1, most + 1) if count % size == 0)
+
+    def block(index, carry):
+        for shift in range(step):
+            carry = body(start + index * step + shift, carry)
+        return carry
+
+    if count == step:
+        return block(0, carry)
+    return lax.fori_loop(0, count // step, block, carry)
 
 
 def moments_kernel(pops, vel_ref, first, second, rows):
@@ -140,7 +154,7 @@
                         rows[1, dim * HALO + k, pl.ds(z, 1), :] = speed[15 - k : 16 - k]
         return carry
 
-    lax.fori_loop(0, depth, plane, 0)
+    plane_loop(0, depth, plane, 0, 4)
     send_pair("cross", encode(rows[1]), encode(rows[0]), first, second)
 
 
@@ -174,6 +188,8 @@
 
 
 TALL = 40
+FREE = [(slot, row) for slot in (1, 3, 5) for row in (0, 37, 38, 39)]
+FREE += [(slot, row) for slot in (0, 2, 4) for row in (38, 39)]
 
 
 def edges_kernel(
@@ -188,19 +204,15 @@
     rows,
     planes,
     note,
-    coded,
 ):
     depth, width = vel_ref.shape[1:3]
     taps = cell_ref.shape[0]
     decode_rows(low_ref, high_ref, rows)
-    fixed = weight_ref[...] * 2.0**16
-    coarse = jnp.round(fixed)
-    note[...] = jnp.zeros_like(note)
     note[pl.ds(0, taps), :] = cell_ref[...].astype(jnp.float32) - 2.0**15
-    note[pl.ds(taps, taps), :] = coarse
-    note[pl.ds(2 * taps, taps), :] = jnp.round((fixed - coarse) * 2.0**15)
-    note[pl.ds(3 * taps, 1), :] = segment_ref[...].astype(jnp.float32)
-    for side, pair in enumerate(((0, 1), (depth - 1, depth - 2))):
+    note[pl.ds(taps, taps), :] = weight_ref[...] * 2.0**17 - 2.0**14
+    note[pl.ds(2 * taps, 1), :] = segment_ref[...].astype(jnp.float32)
+    coded = []
+    for pair in ((0, 1), (depth - 1, depth - 2)):
         planes[...] = jnp.zeros_like(planes)
         for dim in range(3):
             for index, z in enumerate(pair):
@@ -210,13 +222,30 @@
                     line = pl.ds(z, 1)
                     planes[slot, pl.ds(HALO - 1 - k, 1), :] = rows[0, dim * HALO + k, line, :]
                     planes[slot, pl.ds(HALO + width + k, 1), :] = rows[1, dim * HALO + k, line, :]
-        coded[side, pl.ds(0, 6)] = encode(planes[...])
-        coded[side, 6] = note[...].astype(jnp.int32).astype(jnp.int16)
+        for index in range(2 * taps + 1):
+            slot, row = FREE[index]
+            planes[slot, pl.ds(row, 1), :] = note[pl.ds(index, 1), :] * STEP
+        coded.append(encode(planes[...]))
     send_pair("span", coded[1], coded[0], first, second)
 
 
+def free_rows(first, second, start, count):
+    picked = []
+    for message in (first, second):
+        picked.append(
+            jnp.concatenate(
+                [
+                    message[slot].astype(jnp.int32)[row : row + 1]
+                    for slot, row in FREE[start : start + count]
+                ],
+                axis=0,
+            )
+        )
+    return below_above("span", *picked)
+
+
 def edge_planes(vel, low, high, cells, weights, segments):
-    pair = full((7, TALL, LANES), jnp.int16)
+    pair = full((6, TALL, LANES), jnp.int16)
     return pl.pallas_call(
         edges_kernel,
         out_shape=(pair, pair),
@@ -225,27 +254,12 @@
         scratch_shapes=[
             pltpu.VMEM((2, 3 * HALO, vel.shape[1], LANES), jnp.float32),
             pltpu.VMEM((6, TALL, LANES), jnp.float32),
-            pltpu.VMEM((TALL, LANES), jnp.float32),
-            pltpu.VMEM((2, 7, TALL, LANES), jnp.int16),
+            pltpu.VMEM((2 * cells.shape[0] + 8, LANES), jnp.float32),
         ],
         compiler_params=params(),
         cost_estimate=cost(0.2),
         name="edges",
     )(vel, low, high, cells, weights, segments)
-
-
-def plane_loop(start, stop, body, carry, most):
-    count = stop - start
-    step = max(size for size in range(1, most + 1) if count % size == 0)
-
-    def block(index, carry):
-        for shift in range(step):
-            carry = body(start + index * step + shift, carry)
-        return carry
-
-    if count == step:
-        return block(0, carry)
-    return lax.fori_loop(0, count // step, block, carry)
 
 
 def strain_parts(ref, p, row, before, here, after):
@@ -349,7 +363,7 @@
         place_plane(ext, p, vel_ref, rows, p)
         return carry
 
-    lax.fori_loop(0, depth, assemble, 0)
+    plane_loop(0, depth, assemble, 0, 4)
     acc_ref[...] = jnp.zeros_like(acc_ref)
 
     def store_mag(p, row, size):
@@ -404,9 +418,7 @@
     depth, width = vel_ref.shape[1:3]
     decode_rows(low_ref, high_ref, rows)
     acc[...] = partial_ref[...]
-    below, above = below_above(
-        "span", decode(first_ref[pl.ds(0, 6)]), decode(second_ref[pl.ds(0, 6)])
-    )
+    below, above = below_above("span", decode(first_ref[...]), decode(second_ref[...]))
     for side, (message, places, start) in enumerate(
         ((below, (1, 0), 0), (above, (4, 5), depth - 4))
     ):
@@ -454,7 +466,7 @@
             rows[1, q, pl.ds(z, 1), :] = high[15:]
         return carry
 
-    lax.fori_loop(0, depth, plane, 0)
+    plane_loop(0, depth, plane, 0, 4)
     send_pair(
         "cross", rows[1].astype(jnp.bfloat16), rows[0].astype(jnp.bfloat16), first, second
     )
@@ -590,7 +602,7 @@
                 shear_ref[k, z, rows, :] = shear[k]
         return carry
 
-    lax.fori_loop(0, depth, plane, 0)
+    plane_loop(0, depth, plane, 0, 4)
 
 
 def ready(populations, before, after, after_this):
@@ -717,7 +729,7 @@
 
     collide(0, mag_out_ref, 1)
     collide(depth - 1, mag_out_ref, 6)
-    lax.fori_loop(1, depth - 1, inner, 0)
+    plane_loop(1, depth - 1, inner, 0, 7)
 
     def shifted(q, z, half):
         shift_x, shift_y, _ = VELOCITIES[q]
@@ -765,7 +777,7 @@
         if index == 3:
             run(depth - 1, FALLING)
             stop -= 1
-        lax.fori_loop(start, stop, run_inner, 0)
+        plane_loop(start, stop, run_inner, 0, 4)
         place = pl.ds(index * part, part)
         outs.append(
             pltpu.make_async_copy(nexts.at[:, place], next_hbm.at[:, place], out_sems.at[index])
@@ -775,9 +787,7 @@
     owners = partial_ref.shape[0]
     taps, markers = cell_ref.shape
     cells_all = depth * width
-    note_below, note_above = below_above(
-        "span", note_first[6].astype(jnp.int32), note_second[6].astype(jnp.int32)
-    )
+    note_below, note_above = free_rows(note_first, note_second, 0, 2 * taps + 1)
 
     def one_hot(rows, period, wanted):
         row_of = lax.broadcasted_iota(jnp.int32, (period, markers), 0)
@@ -812,10 +822,9 @@
         picks += one_hot(4 * width, 2 * width, jnp.where(inside, row + side * width, -1))
         lanes += each(lane)
         weights += each(
-            note[taps : 2 * taps].astype(jnp.float32) * 2.0**-16
-            + note[2 * taps : 3 * taps].astype(jnp.float32) * 2.0**-31
+            (note[taps : 2 * taps].astype(jnp.float32) + 2.0**14) * 2.0**-17
         )
-        segments.append(note[3 * taps : 3 * taps + 1])
+        segments.append(note[2 * taps : 2 * taps + 1])
     forces += list(marker_force(face_table[...], picks, lanes, weights, taps))
 
     owner_of = lax.broadcasted_iota(jnp.int32, (owners, markers), 0)

time: 51.9 us -> 50.7 us (0.977)
  Pallas kernels: 14.4 us -> 13.1 us
    pallas_call x1, Pallas kernels: 5.08 us -> 4.08 us  [step(): pl.pallas_call(step_kernel, out_shape=(full((19, depth, width, lanes), jn...]
where the time goes in v1:
time: 50.7 us; the launch traced here: 50.5 us
  starting transfers between devices  14.6 us (29%)
  Pallas kernels  13.1 us (26%)
  blocking collectives  10.4 us (21%)
  waiting for transfers between devices  9.89 us (20%)
  local copies, waits for them, and re-layouts  1.71 us (3%)
  between operations  0.74 us (1%)
    ppermute x8, starting transfers between devices, swap(): return (lax.ppermute(first, axis, near), lax.ppermute(second, axis, other))  13.8 us
    all_to_all x1, blocking collectives, local(): arrived = lax.all_to_all(packed, ('span', 'cross'), 0, 0)  10.4 us
    ppermute x3, waiting for transfers between devices, local(): sums = sums + lax.ppermute(sums, 'span', pairs)  8.01 us
    pallas_call x1, Pallas kernels, step(): pl.pallas_call(step_kernel, out_shape=(full((19, depth, width, lanes), jn...  4.08 us
    pallas_call x1, Pallas kernels, inner_sums(): pl.pallas_call(inner_kernel, out_shape=(full((2, EXT, LANES), jnp.float32...  3.23 us
    pallas_call x1, Pallas kernels, ready(): pl.pallas_call(ready_kernel, out_shape=(full((19, depth, width, lanes), j...  1.98 us
    ppermute x8, waiting for transfers between devices, swap(): return (lax.ppermute(first, axis, near), lax.ppermute(second, axis, other))  1.88 us
    unnamed x10, local copies, waits for them, and re-layouts  1.71 us
  transfers between devices with their start and end apart: 11, of which 5 were waited for; matrix products, arithmetic and copies ran while one was open for 0% of the time, Pallas kernels for 11%

profile of v1, /device:TPU:0, one launch (start us, length us, event | category | flops | bytes accessed | tf_op | source)
XLA Modules:
  0.0 50.5 jit_solution(11889788792051659677)
XLA Ops:
  0.6 1.7 %copy-done = bf16[19,16,32,128]{3,2,1,0:T(8,128)(2,1)S(1)} copy-done((bf16[19,16,32,128]{3,2,1,0:T(8,128)(2,1)S(1)}, bf16[19,16,32,128]{3,2,1,0:T(8,128)(2,1)}, u32[]{:S(2)}) %copy-start) | copy-done | bytes 2490392
  2.3 0.6 %moments.1 = (f32[3,16,32,128]{3,2,1,0:T(8,128)S(1)}, s16[9,16,128]{2,1,0:T(8,128)(2,1)S(1)}, s16[9,16,128]{2,1,0:T(8,128)(2,1)S(1)}) custom-call(bf16[19,16,32,128]{3,2,1,0:T(8,128)(2,1)S(1)} %copy-done), custom_call_target="tpu_custom_call" | custom-call | bytes 3600000 | tf_op jit(solution)/shard_map/moments/pallas_call | solution.py:164
  3.0 0.5 %collective-permute-start = (s16[9,16,128]{2,1,0:T(8,128)(2,1)S(1)}, s16[9,16,128]{2,1,0:T(8,128)(2,1)S(1)}, u32[]{:S(2)}, u32[]{:S(2)}) collective-permute-start(s16[9,16,128]{2,1,0:T(8,128)(2,1)S(1)} %get-tuple-element.26), channel_id=1, source_target_pairs={{0,1},{1,0},{2,3},{3,2},{4,5},{5,4},{6,7},{7,6},{8,9},{9,8},{10,11... | collective-permute-start | bytes 110600 | tf_op jit(solution)/shard_map/ppermute | solution.py:50
  3.5 2.6 %collective-permute-start.1 = (s16[9,16,128]{2,1,0:T(8,128)(2,1)S(1)}, s16[9,16,128]{2,1,0:T(8,128)(2,1)S(1)}, u32[]{:S(2)}, u32[]{:S(2)}) collective-permute-start(s16[9,16,128]{2,1,0:T(8,128)(2,1)S(1)} %get-tuple-element.27), channel_id=1, source_target_pairs={{0,3},{1,2},{2,1},{3,0},{4,7},{5,6},{6,5},{7,4},{8,11},{9,10},{10,... | collective-permute-start | bytes 110600 | tf_op jit(solution)/shard_map/ppermute | solution.py:50
  6.1 0.0 collective-permute-done.low_ref
  6.1 1.8 %collective-permute-done.1.high_ref = s16[9,16,128]{2,1,0:T(8,128)(2,1)S(1)} collective-permute-done((s16[9,16,128]{2,1,0:T(8,128)(2,1)S(1)}, s16[9,16,128]{2,1,0:T(8,128)(2,1)S(1)}, u32[]{:S(2)}, u32[]{:S(2)}) %collective-permute-start.1) | collective-permute-done | bytes 36896 | tf_op jit(solution)/shard_map/ppermute | solution.py:50
  7.9 0.1 edges.1
  8.0 1.6 %collective-permute-start.4 = (s16[6,40,128]{2,1,0:T(8,128)(2,1)S(1)}, s16[6,40,128]{2,1,0:T(8,128)(2,1)S(1)}, u32[]{:S(2)}, u32[]{:S(2)}) collective-permute-start(s16[6,40,128]{2,1,0:T(8,128)(2,1)S(1)} %get-tuple-element.31), channel_id=1, source_target_pairs={{0,4},{4,0},{8,12},{12,8},{16,20},{20,16},{24,28},{28,24},{1,5},{5... | collective-permute-start | bytes 184328 | tf_op jit(solution)/shard_map/ppermute | solution.py:50
  9.6 3.6 %collective-permute-start.5 = (s16[6,40,128]{2,1,0:T(8,128)(2,1)S(1)}, s16[6,40,128]{2,1,0:T(8,128)(2,1)S(1)}, u32[]{:S(2)}, u32[]{:S(2)}) collective-permute-start(s16[6,40,128]{2,1,0:T(8,128)(2,1)S(1)} %get-tuple-element.32), channel_id=1, source_target_pairs={{0,28},{4,8},{8,4},{12,16},{16,12},{20,24},{24,20},{28,0},{1,29},{... | collective-permute-start | bytes 184328 | tf_op jit(solution)/shard_map/ppermute | solution.py:50
  13.2 3.2 %inner_sums.1 = (f32[2,40,128]{2,1,0:T(8,128)S(1)}, f32[14,40,128]{2,1,0:T(8,128)S(1)}) custom-call(f32[3,16,32,128]{3,2,1,0:T(8,128)S(1)} %get-tuple-element.25.vel_ref, s16[9,16,128]{2,1,0:T(8,128)(2,1)S(1)} %collective-permute-done.low_ref, s16[9,16,128]{2,1,0:T(8,128)(2,1)S(1)} %collective-permute-done.1.high_ref), custom_call_target="tpu_custom_call" | custom-call | bytes 18000000 | tf_op jit(solution)/shard_map/inner_sums/pallas_call | solution.py:387
  16.4 0.0 collective-permute-done.4.first_ref.note_first
  16.4 0.1 collective-permute-done.5.second_ref.note_second
  16.5 1.4 %outer_sums.1 = (f32[72,128]{1,0:T(8,128)S(1)}, f32[8,40,128]{2,1,0:T(8,128)S(1)}) custom-call(f32[3,16,32,128]{3,2,1,0:T(8,128)S(1)} %get-tuple-element.25.vel_ref, s16[9,16,128]{2,1,0:T(8,128)(2,1)S(1)} %collective-permute-done.low_ref, s16[9,16,128]{2,1,0:T(8,128)(2,1)S(1)} %collective-permute-done.1.high_ref, ...), custom_call_target="tpu_custom_call" | custom-call | bytes 7200000 | tf_op jit(solution)/shard_map/outer_sums/pallas_call | solution.py:443
  18.0 0.1 collective-permute-start.6
  18.1 0.2 face_rows.1
  18.3 0.1 collective-permute-start.2
  18.4 1.6 %collective-permute-start.3 = (bf16[19,16,128]{2,1,0:T(8,128)(2,1)S(1)}, bf16[19,16,128]{2,1,0:T(8,128)(2,1)S(1)}, u32[]{:S(2)}, u32[]{:S(2)}) collective-permute-start(bf16[19,16,128]{2,1,0:T(8,128)(2,1)S(1)} %get-tuple-element.30), channel_id=1, source_target_pairs={{0,3},{1,2},{2,1},{3,0},{4,7},{5,6},{6,5},{7,4},{8,11},{9,10},{10,... | collective-permute-start | bytes 233480 | tf_op jit(solution)/shard_map/ppermute | solution.py:50
  20.0 2.0 %collective-permute-done.6 = f32[72,128]{1,0:T(8,128)S(1)} collective-permute-done((f32[72,128]{1,0:T(8,128)S(1)}, f32[72,128]{1,0:T(8,128)S(1)}, u32[]{:S(2)}, u32[]{:S(2)}) %collective-permute-start.6) | collective-permute-done | bytes 36896 | tf_op jit(solution)/shard_map/ppermute | solution.py:953
  22.0 0.0 collective-permute-start.7
  22.0 3.9 %collective-permute-done.7 = f32[72,128]{1,0:T(8,128)S(1)} collective-permute-done((f32[72,128]{1,0:T(8,128)S(1)}, f32[72,128]{1,0:T(8,128)S(1)}, u32[]{:S(2)}, u32[]{:S(2)}) %collective-permute-start.7) | collective-permute-done | bytes 36896 | tf_op jit(solution)/shard_map/ppermute | solution.py:953
  26.0 0.8 %collective-permute-start.8 = (f32[72,128]{1,0:T(8,128)S(1)}, f32[72,128]{1,0:T(8,128)S(1)}, u32[]{:S(2)}, u32[]{:S(2)}) collective-permute-start(f32[72,128]{1,0:T(8,128)S(1)} %add.10), channel_id=1, source_target_pairs={{0,16},{4,20},{8,24},{12,28},{16,0},{20,4},{24,8},{28,12},{1,17},{... | collective-permute-start | bytes 110600 | tf_op jit(solution)/shard_map/ppermute | solution.py:953
  26.8 0.0 collective-permute-done.2.first
  26.8 0.0 collective-permute-done.3.second
  26.8 2.0 %ready.1 = (f32[19,16,32,128]{3,2,1,0:T(8,128)S(1)}, f32[5,16,32,128]{3,2,1,0:T(8,128)S(1)}, f32[2,5,16,128]{3,2,1,0:T(8,128)S(1)}, f32[2,5,16,128]{3,2,1,0:T(8,128)S(1)}) custom-call(bf16[19,16,32,128]{3,2,1,0:T(8,128)(2,1)S(1)} %copy-done.1, bf16[19,16,128]{2,1,0:T(8,128)(2,1)S(1)} %collective-permute-done.2.first, ...), custom_call_target="tpu_custom_call" | custom-call | bytes 9000000 | tf_op jit(solution)/shard_map/ready/pallas_call | solution.py:610
  28.8 2.1 %collective-permute-done.8 = f32[72,128]{1,0:T(8,128)S(1)} collective-permute-done((f32[72,128]{1,0:T(8,128)S(1)}, f32[72,128]{1,0:T(8,128)S(1)}, u32[]{:S(2)}, u32[]{:S(2)}) %collective-permute-start.8) | collective-permute-done | bytes 36896 | tf_op jit(solution)/shard_map/ppermute | solution.py:953
  30.8 4.1 %step.1 = (bf16[19,16,32,128]{3,2,1,0:T(8,128)(2,1)}, f32[32,128]{1,0:T(8,128)}, f32[32,1,128]{2,1,0:T(1,128)S(1)}, bf16[5,32,128]{2,1,0:T(8,128)(2,1)S(1)}, bf16[5,32,128]{2,1,0:T(8,128)(2,1)S(1)}) custom-call(f32[19,16,32,128]{3,2,1,0:T(8,128)S(1)} %get-tuple-element.34.base_ref, f32[5,16,32,128]{3,2,1,0:T(8,128)S(1)} %get-tuple-element.35.shear_ref, ...), custom_call_target="tpu_custom_call" | custom-call | bytes 18000000 | tf_op jit(solution)/shard_map/step/pallas_call | solution.py:857
  34.9 0.1 collective-permute-start.9
  35.0 3.6 %collective-permute-start.10 = (bf16[5,32,128]{2,1,0:T(8,128)(2,1)S(1)}, bf16[5,32,128]{2,1,0:T(8,128)(2,1)S(1)}, u32[]{:S(2)}, u32[]{:S(2)}) collective-permute-start(bf16[5,32,128]{2,1,0:T(8,128)(2,1)S(1)} %get-tuple-element.42), channel_id=1, source_target_pairs={{0,28},{4,8},{8,4},{12,16},{16,12},{20,24},{24,20},{28,0},{1,29},{... | collective-permute-start | bytes 122888 | tf_op jit(solution)/shard_map/ppermute | solution.py:50
  38.6 10.4 %all_to_all.5.arrived_hbm = f32[32,1,128]{2,1,0:T(1,128)S(1)} all-to-all(f32[32,1,128]{2,1,0:T(1,128)S(1)} %get-tuple-element.43), channel_id=1, replica_groups=mesh['span'=8,'cross'=4] {'span','cross'}, dimensions={0} | all-to-all | bytes 32768 | tf_op jit(solution)/shard_map/all_to_all | solution.py:958
  49.1 0.0 collective-permute-done.9.first
  49.1 0.0 collective-permute-done.10.second
  49.1 1.4 %arrive.1 = (bf16[19,16,32,128]{3,2,1,0:T(8,128)(2,1)}, f32[3,8]{1,0:T(4,128)}) custom-call(bf16[19,16,32,128]{3,2,1,0:T(8,128)(2,1)} %get-tuple-element.40.next_in, bf16[5,32,128]{2,1,0:T(8,128)(2,1)S(1)} %collective-permute-done.9.first, bf16[5,32,128]{2,1,0:T(8,128)(2,1)S(1)} %collective-permute-done.10.second, ...), custom_call_target="tpu_custom_call", output_to_operand_aliasing={{0}: (0, {})} | custom-call | bytes 1800000 | tf_op jit(solution)/shard_map/arrive/pallas_call | solution.py:917
  (12 shorter events, 0.0 us)
Async XLA Ops:
  0.6 1.7 %copy-start = (bf16[19,16,32,128]{3,2,1,0:T(8,128)(2,1)S(1)}, bf16[19,16,32,128]{3,2,1,0:T(8,128)(2,1)}, u32[]{:S(2)}) copy-start(bf16[19,16,32,128]{3,2,1,0:T(8,128)(2,1)} %pops.5) | copy-start | bytes 7471108
  2.3 5.5 %copy-start.2 = (s32[128,8]{0,1:T(8,128)S(1)}, s32[128,8]{0,1:T(8,128)}, u32[]{:S(2)}) copy-start(s32[128,8]{0,1:T(8,128)} %param.5) | copy-start | bytes 12292
  2.3 5.5 %copy-start.3 = (f32[128,8]{0,1:T(8,128)S(1)}, f32[128,8]{0,1:T(8,128)}, u32[]{:S(2)}) copy-start(f32[128,8]{0,1:T(8,128)} %param.6) | copy-start | bytes 12292
  2.3 5.5 %copy-start.4 = (s32[128]{0:T(128)S(1)}, s32[128]{0:T(128)}, u32[]{:S(2)}) copy-start(s32[128]{0:T(128)} %param.7) | copy-start | bytes 1540
  2.3 15.7 %copy-start.1 = (bf16[19,16,32,128]{3,2,1,0:T(8,128)(2,1)S(1)}, bf16[19,16,32,128]{3,2,1,0:T(8,128)(2,1)}, u32[]{:S(2)}) copy-start(bf16[19,16,32,128]{3,2,1,0:T(8,128)(2,1)} %pops.5) | copy-start | bytes 7471108
  3.0 3.2 %collective-permute-start = (s16[9,16,128]{2,1,0:T(8,128)(2,1)S(1)}, s16[9,16,128]{2,1,0:T(8,128)(2,1)S(1)}, u32[]{:S(2)}, u32[]{:S(2)}) collective-permute-start(s16[9,16,128]{2,1,0:T(8,128)(2,1)S(1)} %get-tuple-element.26), channel_id=1, source_target_pairs={{0,1},{1,0},{2,3},{3,2},{4,5},{5,4},{6,7},{7,6},{8,9},{9,8},{10,11... | collective-permute-start | bytes 110600 | tf_op jit(solution)/shard_map/ppermute | solution.py:50
  3.5 4.4 %collective-permute-start.1 = (s16[9,16,128]{2,1,0:T(8,128)(2,1)S(1)}, s16[9,16,128]{2,1,0:T(8,128)(2,1)S(1)}, u32[]{:S(2)}, u32[]{:S(2)}) collective-permute-start(s16[9,16,128]{2,1,0:T(8,128)(2,1)S(1)} %get-tuple-element.27), channel_id=1, source_target_pairs={{0,3},{1,2},{2,1},{3,0},{4,7},{5,6},{6,5},{7,4},{8,11},{9,10},{10,... | collective-permute-start | bytes 110600 | tf_op jit(solution)/shard_map/ppermute | solution.py:50
  8.0 8.4 %collective-permute-start.4 = (s16[6,40,128]{2,1,0:T(8,128)(2,1)S(1)}, s16[6,40,128]{2,1,0:T(8,128)(2,1)S(1)}, u32[]{:S(2)}, u32[]{:S(2)}) collective-permute-start(s16[6,40,128]{2,1,0:T(8,128)(2,1)S(1)} %get-tuple-element.31), channel_id=1, source_target_pairs={{0,4},{4,0},{8,12},{12,8},{16,20},{20,16},{24,28},{28,24},{1,5},{5... | collective-permute-start | bytes 184328 | tf_op jit(solution)/shard_map/ppermute | solution.py:50
  9.6 6.9 %collective-permute-start.5 = (s16[6,40,128]{2,1,0:T(8,128)(2,1)S(1)}, s16[6,40,128]{2,1,0:T(8,128)(2,1)S(1)}, u32[]{:S(2)}, u32[]{:S(2)}) collective-permute-start(s16[6,40,128]{2,1,0:T(8,128)(2,1)S(1)} %get-tuple-element.32), channel_id=1, source_target_pairs={{0,28},{4,8},{8,4},{12,16},{16,12},{20,24},{24,20},{28,0},{1,29},{... | collective-permute-start | bytes 184328 | tf_op jit(solution)/shard_map/ppermute | solution.py:50
  18.0 4.0 %collective-permute-start.6 = (f32[72,128]{1,0:T(8,128)S(1)}, f32[72,128]{1,0:T(8,128)S(1)}, u32[]{:S(2)}, u32[]{:S(2)}) collective-permute-start(f32[72,128]{1,0:T(8,128)S(1)} %get-tuple-element.33.after_this), channel_id=1, source_target_pairs={{0,4},{4,0},{8,12},{12,8},{16,20},{20,16},{24,28},{28,24},{1,5},{5... | collective-permute-start | bytes 110600 | tf_op jit(solution)/shard_map/ppermute | solution.py:953
  18.3 8.5 %collective-permute-start.2 = (bf16[19,16,128]{2,1,0:T(8,128)(2,1)S(1)}, bf16[19,16,128]{2,1,0:T(8,128)(2,1)S(1)}, u32[]{:S(2)}, u32[]{:S(2)}) collective-permute-start(bf16[19,16,128]{2,1,0:T(8,128)(2,1)S(1)} %get-tuple-element.29), channel_id=1, source_target_pairs={{0,1},{1,0},{2,3},{3,2},{4,5},{5,4},{6,7},{7,6},{8,9},{9,8},{10,11... | collective-permute-start | bytes 233480 | tf_op jit(solution)/shard_map/ppermute | solution.py:50
  18.4 8.4 %collective-permute-start.3 = (bf16[19,16,128]{2,1,0:T(8,128)(2,1)S(1)}, bf16[19,16,128]{2,1,0:T(8,128)(2,1)S(1)}, u32[]{:S(2)}, u32[]{:S(2)}) collective-permute-start(bf16[19,16,128]{2,1,0:T(8,128)(2,1)S(1)} %get-tuple-element.30), channel_id=1, source_target_pairs={{0,3},{1,2},{2,1},{3,0},{4,7},{5,6},{6,5},{7,4},{8,11},{9,10},{10,... | collective-permute-start | bytes 233480 | tf_op jit(solution)/shard_map/ppermute | solution.py:50
  22.0 4.0 %collective-permute-start.7 = (f32[72,128]{1,0:T(8,128)S(1)}, f32[72,128]{1,0:T(8,128)S(1)}, u32[]{:S(2)}, u32[]{:S(2)}) collective-permute-start(f32[72,128]{1,0:T(8,128)S(1)} %add.9), channel_id=1, source_target_pairs={{0,8},{4,12},{8,0},{12,4},{16,24},{20,28},{24,16},{28,20},{1,9},{5... | collective-permute-start | bytes 110600 | tf_op jit(solution)/shard_map/ppermute | solution.py:953
  26.0 4.9 %collective-permute-start.8 = (f32[72,128]{1,0:T(8,128)S(1)}, f32[72,128]{1,0:T(8,128)S(1)}, u32[]{:S(2)}, u32[]{:S(2)}) collective-permute-start(f32[72,128]{1,0:T(8,128)S(1)} %add.10), channel_id=1, source_target_pairs={{0,16},{4,20},{8,24},{12,28},{16,0},{20,4},{24,8},{28,12},{1,17},{... | collective-permute-start | bytes 110600 | tf_op jit(solution)/shard_map/ppermute | solution.py:953
  34.9 14.1 %collective-permute-start.9 = (bf16[5,32,128]{2,1,0:T(8,128)(2,1)S(1)}, bf16[5,32,128]{2,1,0:T(8,128)(2,1)S(1)}, u32[]{:S(2)}, u32[]{:S(2)}) collective-permute-start(bf16[5,32,128]{2,1,0:T(8,128)(2,1)S(1)} %get-tuple-element.41), channel_id=1, source_target_pairs={{0,4},{4,0},{8,12},{12,8},{16,20},{20,16},{24,28},{28,24},{1,5},{5... | collective-permute-start | bytes 122888 | tf_op jit(solution)/shard_map/ppermute | solution.py:50
  35.0 14.0 %collective-permute-start.10 = (bf16[5,32,128]{2,1,0:T(8,128)(2,1)S(1)}, bf16[5,32,128]{2,1,0:T(8,128)(2,1)S(1)}, u32[]{:S(2)}, u32[]{:S(2)}) collective-permute-start(bf16[5,32,128]{2,1,0:T(8,128)(2,1)S(1)} %get-tuple-element.42), channel_id=1, source_target_pairs={{0,28},{4,8},{8,4},{12,16},{16,12},{20,24},{24,20},{28,0},{1,29},{... | collective-permute-start | bytes 122888 | tf_op jit(solution)/shard_map/ppermute | solution.py:50

commit v2 on v1

--- a/solution.py
+++ b/solution.py
@@ -408,12 +408,14 @@
     partial_ref,
     sums_ref,
     mag_ref,
+    words_ref,
     ext,
     hat,
     zsum,
     zvel,
     rows,
     acc,
+    stage,
 ):
     depth, width = vel_ref.shape[1:3]
     decode_rows(low_ref, high_ref, rows)
@@ -436,23 +438,92 @@
     sums_ref[...] = jnp.zeros_like(sums_ref)
     for index in range(2):
         sums_ref[pl.ds(index * lines, lines), :] = acc[index, pl.ds(OWN - TOP - 1, lines), :]
+    stage[...] = jnp.zeros_like(stage)
+    words = pack(*[acc[index, pl.ds(OWN - TOP - 1, lines), :] for index in range(2)])
+    store_words(words, stage, words_ref)
 
 
 def outer_sums(vel, low, high, below, above, partial):
     depth, width = vel.shape[1:3]
+    words = -(-3 * (width + 2) // 8) * 8
     return pl.pallas_call(
         outer_kernel,
         out_shape=(
             full((-(-2 * (width + 2) // 8) * 8, LANES), jnp.float32),
             full((8, EXT, LANES), jnp.float32),
+            full((words, LANES), jnp.int16),
         ),
         in_specs=in_vmem(6),
-        out_specs=tuple(in_vmem(2)),
-        scratch_shapes=model_scratch(6, depth) + [pltpu.VMEM((2, EXT, LANES), jnp.float32)],
+        out_specs=tuple(in_vmem(3)),
+        scratch_shapes=model_scratch(6, depth) + [
+            pltpu.VMEM((2, EXT, LANES), jnp.float32),
+            pltpu.VMEM((words, LANES), jnp.float32),
+        ],
         compiler_params=params(),
         cost_estimate=cost(2),
         name="outer_sums",
     )(vel, low, high, below, above, partial)
+
+
+def to_code(value):
+    size = jnp.clip(jnp.abs(value), 2.0**-63, 2.0**63)
+    steps = jnp.round((jnp.log(size) * 1.4426950408889634 + 64.0) * 2.0**16).astype(jnp.int32)
+    return jnp.where(value < 0.0, steps + 2**23, steps)
+
+
+def from_code(code):
+    steps = lax.bitwise_and(code, 2**23 - 1).astype(jnp.float32)
+    size = jnp.exp((steps * 2.0**-16 - 64.0) * 0.6931471805599453)
+    return jnp.where(code >= 2**23, -size, size)
+
+
+def pack(lm, mm):
+    lm, mm = to_code(lm), to_code(mm)
+    low = lax.bitwise_and(lm, 255) * 256 + lax.bitwise_and(mm, 255)
+    words = [lax.shift_right_logical(lm, 8), lax.shift_right_logical(mm, 8), low]
+    return [(word - 2**15).astype(jnp.float32) for word in words]
+
+
+def unpack(words):
+    lm, mm, low = [word + 2**15 for word in words]
+    return (
+        from_code(lm * 256 + lax.shift_right_logical(low, 8)),
+        from_code(mm * 256 + lax.bitwise_and(low, 255)),
+    )
+
+
+def store_words(words, stage, out):
+    lines = words[0].shape[0]
+    for index, word in enumerate(words):
+        stage[pl.ds(index * lines, lines), :] = word
+    out[...] = stage[...].astype(jnp.int32).astype(jnp.int16)
+
+
+def combine_kernel(lines, own, other, out, stage):
+    total = (0.0, 0.0)
+    for message in (own, other):
+        stage[...] = message[...].astype(jnp.int32).astype(jnp.float32)
+        words = [stage[pl.ds(index * lines, lines), :].astype(jnp.int32) for index in range(3)]
+        total = [before + value for before, value in zip(total, unpack(words))]
+    if out.dtype == jnp.int16:
+        store_words(pack(*total), stage, out)
+    else:
+        out[...] = jnp.zeros_like(out)
+        for index in range(2):
+            out[pl.ds(index * lines, lines), :] = total[index]
+
+
+def combine(own, other, lines, like):
+    return pl.pallas_call(
+        functools.partial(combine_kernel, lines),
+        out_shape=full(like.shape, like.dtype),
+        in_specs=in_vmem(2),
+        out_specs=in_vmem(1)[0],
+        scratch_shapes=[pltpu.VMEM(own.shape, jnp.float32)],
+        compiler_params=params(),
+        cost_estimate=cost(0.1),
+        name="combine",
+    )(own, other)
 
 
 def rows_kernel(pops, after_this, first, second, rows):
@@ -941,17 +1012,20 @@
     planes = swap(*edge_planes(vel, *lines, cells, weights, segments), "span")
     partial, mag_in = inner_sums(vel, *lines)
     faces = swap(*face_rows(populations, partial), "cross")
-    sums, mag_out = outer_sums(vel, *lines, *planes, partial)
+    sums, mag_out, words = outer_sums(vel, *lines, *planes, partial)
     parts = ready(populations, *faces, sums)
     count = lax.axis_size("span")
     if count & (count - 1):
         sums = lax.psum(sums, "span")
     else:
         distance = 1
+        lines = populations.shape[2] + 2
         while distance < count:
             pairs = [(i, i ^ distance) for i in range(count)]
-            sums = sums + lax.ppermute(sums, "span", pairs)
+            other = lax.ppermute(words, "span", pairs)
             distance *= 2
+            words = combine(words, other, lines, words if distance < count else sums)
+        sums = words
     moved, eddy_coeff, packed, *leaving = step(
         parts, sums, mag_in, mag_out, cells, weights, segments, planes, owners
     )

time: 50.7 us -> 50.5 us (level)
  no operation moved by 1% of the time
where the time goes in v2:
time: 50.5 us; the launch traced here: 50.4 us
  starting transfers between devices  14.8 us (29%)
  Pallas kernels  13.4 us (27%)
  blocking collectives  10.2 us (20%)
  waiting for transfers between devices  9.55 us (19%)
  local copies, waits for them, and re-layouts  1.71 us (3%)
  between operations  0.75 us (1%)
    ppermute x8, starting transfers between devices, swap(): return (lax.ppermute(first, axis, near), lax.ppermute(second, axis, other))  13.8 us
    all_to_all x1, blocking collectives, local(): arrived = lax.all_to_all(packed, ('span', 'cross'), 0, 0)  10.2 us
    ppermute x3, waiting for transfers between devices, local(): other = lax.ppermute(words, 'span', pairs)  7.67 us
    pallas_call x1, Pallas kernels, step(): pl.pallas_call(step_kernel, out_shape=(full((19, depth, width, lanes), jn...  4.09 us
    pallas_call x1, Pallas kernels, inner_sums(): pl.pallas_call(inner_kernel, out_shape=(full((2, EXT, LANES), jnp.float32...  3.23 us
    pallas_call x1, Pallas kernels, ready(): pl.pallas_call(ready_kernel, out_shape=(full((19, depth, width, lanes), j...  1.99 us
    ppermute x8, waiting for transfers between devices, swap(): return (lax.ppermute(first, axis, near), lax.ppermute(second, axis, other))  1.88 us
    unnamed x10, local copies, waits for them, and re-layouts  1.71 us
  transfers between devices with their start and end apart: 11, of which 5 were waited for; matrix products, arithmetic and copies ran while one was open for 0% of the time, Pallas kernels for 11%

profile of v2, /device:TPU:0, one launch (start us, length us, event | category | flops | bytes accessed | tf_op | source)
XLA Modules:
  0.0 50.4 jit_solution(14807298411085562977)
XLA Ops:
  0.6 1.7 %copy-done = bf16[19,16,32,128]{3,2,1,0:T(8,128)(2,1)S(1)} copy-done((bf16[19,16,32,128]{3,2,1,0:T(8,128)(2,1)S(1)}, bf16[19,16,32,128]{3,2,1,0:T(8,128)(2,1)}, u32[]{:S(2)}) %copy-start) | copy-done | bytes 2490392
  2.3 0.6 %moments.1 = (f32[3,16,32,128]{3,2,1,0:T(8,128)S(1)}, s16[9,16,128]{2,1,0:T(8,128)(2,1)S(1)}, s16[9,16,128]{2,1,0:T(8,128)(2,1)S(1)}) custom-call(bf16[19,16,32,128]{3,2,1,0:T(8,128)(2,1)S(1)} %copy-done), custom_call_target="tpu_custom_call" | custom-call | bytes 3600000 | tf_op jit(solution)/shard_map/moments/pallas_call | solution.py:164
  3.0 0.5 %collective-permute-start = (s16[9,16,128]{2,1,0:T(8,128)(2,1)S(1)}, s16[9,16,128]{2,1,0:T(8,128)(2,1)S(1)}, u32[]{:S(2)}, u32[]{:S(2)}) collective-permute-start(s16[9,16,128]{2,1,0:T(8,128)(2,1)S(1)} %get-tuple-element.27), channel_id=1, source_target_pairs={{0,1},{1,0},{2,3},{3,2},{4,5},{5,4},{6,7},{7,6},{8,9},{9,8},{10,11... | collective-permute-start | bytes 110600 | tf_op jit(solution)/shard_map/ppermute | solution.py:50
  3.5 2.6 %collective-permute-start.1 = (s16[9,16,128]{2,1,0:T(8,128)(2,1)S(1)}, s16[9,16,128]{2,1,0:T(8,128)(2,1)S(1)}, u32[]{:S(2)}, u32[]{:S(2)}) collective-permute-start(s16[9,16,128]{2,1,0:T(8,128)(2,1)S(1)} %get-tuple-element.28), channel_id=1, source_target_pairs={{0,3},{1,2},{2,1},{3,0},{4,7},{5,6},{6,5},{7,4},{8,11},{9,10},{10,... | collective-permute-start | bytes 110600 | tf_op jit(solution)/shard_map/ppermute | solution.py:50
  6.1 0.0 collective-permute-done.low_ref
  6.1 1.8 %collective-permute-done.1.high_ref = s16[9,16,128]{2,1,0:T(8,128)(2,1)S(1)} collective-permute-done((s16[9,16,128]{2,1,0:T(8,128)(2,1)S(1)}, s16[9,16,128]{2,1,0:T(8,128)(2,1)S(1)}, u32[]{:S(2)}, u32[]{:S(2)}) %collective-permute-start.1) | collective-permute-done | bytes 36896 | tf_op jit(solution)/shard_map/ppermute | solution.py:50
  7.9 0.1 edges.1
  8.0 1.6 %collective-permute-start.4 = (s16[6,40,128]{2,1,0:T(8,128)(2,1)S(1)}, s16[6,40,128]{2,1,0:T(8,128)(2,1)S(1)}, u32[]{:S(2)}, u32[]{:S(2)}) collective-permute-start(s16[6,40,128]{2,1,0:T(8,128)(2,1)S(1)} %get-tuple-element.32), channel_id=1, source_target_pairs={{0,4},{4,0},{8,12},{12,8},{16,20},{20,16},{24,28},{28,24},{1,5},{5... | collective-permute-start | bytes 184328 | tf_op jit(solution)/shard_map/ppermute | solution.py:50
  9.6 3.6 %collective-permute-start.5 = (s16[6,40,128]{2,1,0:T(8,128)(2,1)S(1)}, s16[6,40,128]{2,1,0:T(8,128)(2,1)S(1)}, u32[]{:S(2)}, u32[]{:S(2)}) collective-permute-start(s16[6,40,128]{2,1,0:T(8,128)(2,1)S(1)} %get-tuple-element.33), channel_id=1, source_target_pairs={{0,28},{4,8},{8,4},{12,16},{16,12},{20,24},{24,20},{28,0},{1,29},{... | collective-permute-start | bytes 184328 | tf_op jit(solution)/shard_map/ppermute | solution.py:50
  13.2 3.2 %inner_sums.1 = (f32[2,40,128]{2,1,0:T(8,128)S(1)}, f32[14,40,128]{2,1,0:T(8,128)S(1)}) custom-call(f32[3,16,32,128]{3,2,1,0:T(8,128)S(1)} %get-tuple-element.26.vel_ref, s16[9,16,128]{2,1,0:T(8,128)(2,1)S(1)} %collective-permute-done.low_ref, s16[9,16,128]{2,1,0:T(8,128)(2,1)S(1)} %collective-permute-done.1.high_ref), custom_call_target="tpu_custom_call" | custom-call | bytes 18000000 | tf_op jit(solution)/shard_map/inner_sums/pallas_call | solution.py:387
  16.4 0.1 collective-permute-done.5.second_ref.note_second
  16.5 1.5 %outer_sums.1 = (f32[72,128]{1,0:T(8,128)S(1)}, f32[8,40,128]{2,1,0:T(8,128)S(1)}, s16[104,128]{1,0:T(8,128)(2,1)S(1)}) custom-call(f32[3,16,32,128]{3,2,1,0:T(8,128)S(1)} %get-tuple-element.26.vel_ref, s16[9,16,128]{2,1,0:T(8,128)(2,1)S(1)} %collective-permute-done.low_ref, s16[9,16,128]{2,1,0:T(8,128)(2,1)S(1)} %collective-permute-done.1.high_ref, ...), custom_call_target="tpu_custom_call" | custom-call | bytes 7200000 | tf_op jit(solution)/shard_map/outer_sums/pallas_call | solution.py:449
  18.0 0.1 collective-permute-start.6
  18.1 0.2 face_rows.1
  18.3 0.1 collective-permute-start.2
  18.4 1.6 %collective-permute-start.3 = (bf16[19,16,128]{2,1,0:T(8,128)(2,1)S(1)}, bf16[19,16,128]{2,1,0:T(8,128)(2,1)S(1)}, u32[]{:S(2)}, u32[]{:S(2)}) collective-permute-start(bf16[19,16,128]{2,1,0:T(8,128)(2,1)S(1)} %get-tuple-element.31), channel_id=1, source_target_pairs={{0,3},{1,2},{2,1},{3,0},{4,7},{5,6},{6,5},{7,4},{8,11},{9,10},{10,... | collective-permute-start | bytes 233480 | tf_op jit(solution)/shard_map/ppermute | solution.py:50
  20.0 1.9 %collective-permute-done.6.other = s16[104,128]{1,0:T(8,128)(2,1)S(1)} collective-permute-done((s16[104,128]{1,0:T(8,128)(2,1)S(1)}, s16[104,128]{1,0:T(8,128)(2,1)S(1)}, u32[]{:S(2)}, u32[]{:S(2)}) %collective-permute-start.6) | collective-permute-done | bytes 26656 | tf_op jit(solution)/shard_map/ppermute | solution.py:1025
  21.9 0.1 combine.3.own
  22.0 0.1 collective-permute-start.7
  22.1 3.8 %collective-permute-done.7.other = s16[104,128]{1,0:T(8,128)(2,1)S(1)} collective-permute-done((s16[104,128]{1,0:T(8,128)(2,1)S(1)}, s16[104,128]{1,0:T(8,128)(2,1)S(1)}, u32[]{:S(2)}, u32[]{:S(2)}) %collective-permute-start.7) | collective-permute-done | bytes 26656 | tf_op jit(solution)/shard_map/ppermute | solution.py:1025
  25.9 0.1 combine.4.own
  26.0 0.9 %collective-permute-start.8 = (s16[104,128]{1,0:T(8,128)(2,1)S(1)}, s16[104,128]{1,0:T(8,128)(2,1)S(1)}, u32[]{:S(2)}, u32[]{:S(2)}) collective-permute-start(s16[104,128]{1,0:T(8,128)(2,1)S(1)} %combine.4.own), channel_id=1, source_target_pairs={{0,16},{4,20},{8,24},{12,28},{16,0},{20,4},{24,8},{28,12},{1,17},{... | collective-permute-start | bytes 79880 | tf_op jit(solution)/shard_map/ppermute | solution.py:1025
  26.9 0.0 collective-permute-done.2.first
  26.9 0.0 collective-permute-done.3.second
  26.9 2.0 %ready.1 = (f32[19,16,32,128]{3,2,1,0:T(8,128)S(1)}, f32[5,16,32,128]{3,2,1,0:T(8,128)S(1)}, f32[2,5,16,128]{3,2,1,0:T(8,128)S(1)}, f32[2,5,16,128]{3,2,1,0:T(8,128)S(1)}) custom-call(bf16[19,16,32,128]{3,2,1,0:T(8,128)(2,1)S(1)} %copy-done.1, bf16[19,16,128]{2,1,0:T(8,128)(2,1)S(1)} %collective-permute-done.2.first, ...), custom_call_target="tpu_custom_call" | custom-call | bytes 9000000 | tf_op jit(solution)/shard_map/ready/pallas_call | solution.py:681
  28.9 1.9 %collective-permute-done.8.other = s16[104,128]{1,0:T(8,128)(2,1)S(1)} collective-permute-done((s16[104,128]{1,0:T(8,128)(2,1)S(1)}, s16[104,128]{1,0:T(8,128)(2,1)S(1)}, u32[]{:S(2)}, u32[]{:S(2)}) %collective-permute-start.8) | collective-permute-done | bytes 26656 | tf_op jit(solution)/shard_map/ppermute | solution.py:1025
  30.8 0.1 combine.5.sums_ref
  30.9 4.1 %step.1 = (bf16[19,16,32,128]{3,2,1,0:T(8,128)(2,1)}, f32[32,128]{1,0:T(8,128)}, f32[32,1,128]{2,1,0:T(1,128)S(1)}, bf16[5,32,128]{2,1,0:T(8,128)(2,1)S(1)}, bf16[5,32,128]{2,1,0:T(8,128)(2,1)S(1)}) custom-call(f32[19,16,32,128]{3,2,1,0:T(8,128)S(1)} %get-tuple-element.35.base_ref, f32[5,16,32,128]{3,2,1,0:T(8,128)S(1)} %get-tuple-element.36.shear_ref, ...), custom_call_target="tpu_custom_call" | custom-call | bytes 18000000 | tf_op jit(solution)/shard_map/step/pallas_call | solution.py:928
  35.0 0.2 collective-permute-start.9
  35.2 3.6 %collective-permute-start.10 = (bf16[5,32,128]{2,1,0:T(8,128)(2,1)S(1)}, bf16[5,32,128]{2,1,0:T(8,128)(2,1)S(1)}, u32[]{:S(2)}, u32[]{:S(2)}) collective-permute-start(bf16[5,32,128]{2,1,0:T(8,128)(2,1)S(1)} %get-tuple-element.44), channel_id=1, source_target_pairs={{0,28},{4,8},{8,4},{12,16},{16,12},{20,24},{24,20},{28,0},{1,29},{... | collective-permute-start | bytes 122888 | tf_op jit(solution)/shard_map/ppermute | solution.py:50
  38.8 10.2 %all_to_all.5.arrived_hbm = f32[32,1,128]{2,1,0:T(1,128)S(1)} all-to-all(f32[32,1,128]{2,1,0:T(1,128)S(1)} %get-tuple-element.45), channel_id=1, replica_groups=mesh['span'=8,'cross'=4] {'span','cross'}, dimensions={0} | all-to-all | bytes 32768 | tf_op jit(solution)/shard_map/all_to_all | solution.py:1032
  48.9 1.4 %arrive.1 = (bf16[19,16,32,128]{3,2,1,0:T(8,128)(2,1)}, f32[3,8]{1,0:T(4,128)}) custom-call(bf16[19,16,32,128]{3,2,1,0:T(8,128)(2,1)} %get-tuple-element.42.next_in, bf16[5,32,128]{2,1,0:T(8,128)(2,1)S(1)} %collective-permute-done.9.first, bf16[5,32,128]{2,1,0:T(8,128)(2,1)S(1)} %collective-permute-done.10.second, ...), custom_call_target="tpu_custom_call", output_to_operand_aliasing={{0}: (0, {})} | custom-call | bytes 1800000 | tf_op jit(solution)/shard_map/arrive/pallas_call | solution.py:988
  (12 shorter events, 0.0 us)
Async XLA Ops:
  0.6 1.7 %copy-start = (bf16[19,16,32,128]{3,2,1,0:T(8,128)(2,1)S(1)}, bf16[19,16,32,128]{3,2,1,0:T(8,128)(2,1)}, u32[]{:S(2)}) copy-start(bf16[19,16,32,128]{3,2,1,0:T(8,128)(2,1)} %pops.5) | copy-start | bytes 7471108
  2.3 5.5 %copy-start.2 = (s32[128,8]{0,1:T(8,128)S(1)}, s32[128,8]{0,1:T(8,128)}, u32[]{:S(2)}) copy-start(s32[128,8]{0,1:T(8,128)} %param.5) | copy-start | bytes 12292
  2.3 5.5 %copy-start.3 = (f32[128,8]{0,1:T(8,128)S(1)}, f32[128,8]{0,1:T(8,128)}, u32[]{:S(2)}) copy-start(f32[128,8]{0,1:T(8,128)} %param.6) | copy-start | bytes 12292
  2.3 5.5 %copy-start.4 = (s32[128]{0:T(128)S(1)}, s32[128]{0:T(128)}, u32[]{:S(2)}) copy-start(s32[128]{0:T(128)} %param.7) | copy-start | bytes 1540
  2.3 15.7 %copy-start.1 = (bf16[19,16,32,128]{3,2,1,0:T(8,128)(2,1)S(1)}, bf16[19,16,32,128]{3,2,1,0:T(8,128)(2,1)}, u32[]{:S(2)}) copy-start(bf16[19,16,32,128]{3,2,1,0:T(8,128)(2,1)} %pops.5) | copy-start | bytes 7471108
  3.0 3.2 %collective-permute-start = (s16[9,16,128]{2,1,0:T(8,128)(2,1)S(1)}, s16[9,16,128]{2,1,0:T(8,128)(2,1)S(1)}, u32[]{:S(2)}, u32[]{:S(2)}) collective-permute-start(s16[9,16,128]{2,1,0:T(8,128)(2,1)S(1)} %get-tuple-element.27), channel_id=1, source_target_pairs={{0,1},{1,0},{2,3},{3,2},{4,5},{5,4},{6,7},{7,6},{8,9},{9,8},{10,11... | collective-permute-start | bytes 110600 | tf_op jit(solution)/shard_map/ppermute | solution.py:50
  3.5 4.4 %collective-permute-start.1 = (s16[9,16,128]{2,1,0:T(8,128)(2,1)S(1)}, s16[9,16,128]{2,1,0:T(8,128)(2,1)S(1)}, u32[]{:S(2)}, u32[]{:S(2)}) collective-permute-start(s16[9,16,128]{2,1,0:T(8,128)(2,1)S(1)} %get-tuple-element.28), channel_id=1, source_target_pairs={{0,3},{1,2},{2,1},{3,0},{4,7},{5,6},{6,5},{7,4},{8,11},{9,10},{10,... | collective-permute-start | bytes 110600 | tf_op jit(solution)/shard_map/ppermute | solution.py:50
  8.0 8.4 %collective-permute-start.4 = (s16[6,40,128]{2,1,0:T(8,128)(2,1)S(1)}, s16[6,40,128]{2,1,0:T(8,128)(2,1)S(1)}, u32[]{:S(2)}, u32[]{:S(2)}) collective-permute-start(s16[6,40,128]{2,1,0:T(8,128)(2,1)S(1)} %get-tuple-element.32), channel_id=1, source_target_pairs={{0,4},{4,0},{8,12},{12,8},{16,20},{20,16},{24,28},{28,24},{1,5},{5... | collective-permute-start | bytes 184328 | tf_op jit(solution)/shard_map/ppermute | solution.py:50
  9.6 6.9 %collective-permute-start.5 = (s16[6,40,128]{2,1,0:T(8,128)(2,1)S(1)}, s16[6,40,128]{2,1,0:T(8,128)(2,1)S(1)}, u32[]{:S(2)}, u32[]{:S(2)}) collective-permute-start(s16[6,40,128]{2,1,0:T(8,128)(2,1)S(1)} %get-tuple-element.33), channel_id=1, source_target_pairs={{0,28},{4,8},{8,4},{12,16},{16,12},{20,24},{24,20},{28,0},{1,29},{... | collective-permute-start | bytes 184328 | tf_op jit(solution)/shard_map/ppermute | solution.py:50
  18.0 3.9 %collective-permute-start.6 = (s16[104,128]{1,0:T(8,128)(2,1)S(1)}, s16[104,128]{1,0:T(8,128)(2,1)S(1)}, u32[]{:S(2)}, u32[]{:S(2)}) collective-permute-start(s16[104,128]{1,0:T(8,128)(2,1)S(1)} %get-tuple-element.39.own), channel_id=1, source_target_pairs={{0,4},{4,0},{8,12},{12,8},{16,20},{20,16},{24,28},{28,24},{1,5},{5... | collective-permute-start | bytes 79880 | tf_op jit(solution)/shard_map/ppermute | solution.py:1025
  18.3 8.6 %collective-permute-start.2 = (bf16[19,16,128]{2,1,0:T(8,128)(2,1)S(1)}, bf16[19,16,128]{2,1,0:T(8,128)(2,1)S(1)}, u32[]{:S(2)}, u32[]{:S(2)}) collective-permute-start(bf16[19,16,128]{2,1,0:T(8,128)(2,1)S(1)} %get-tuple-element.30), channel_id=1, source_target_pairs={{0,1},{1,0},{2,3},{3,2},{4,5},{5,4},{6,7},{7,6},{8,9},{9,8},{10,11... | collective-permute-start | bytes 233480 | tf_op jit(solution)/shard_map/ppermute | solution.py:50
  18.4 8.5 %collective-permute-start.3 = (bf16[19,16,128]{2,1,0:T(8,128)(2,1)S(1)}, bf16[19,16,128]{2,1,0:T(8,128)(2,1)S(1)}, u32[]{:S(2)}, u32[]{:S(2)}) collective-permute-start(bf16[19,16,128]{2,1,0:T(8,128)(2,1)S(1)} %get-tuple-element.31), channel_id=1, source_target_pairs={{0,3},{1,2},{2,1},{3,0},{4,7},{5,6},{6,5},{7,4},{8,11},{9,10},{10,... | collective-permute-start | bytes 233480 | tf_op jit(solution)/shard_map/ppermute | solution.py:50
  22.0 3.9 %collective-permute-start.7 = (s16[104,128]{1,0:T(8,128)(2,1)S(1)}, s16[104,128]{1,0:T(8,128)(2,1)S(1)}, u32[]{:S(2)}, u32[]{:S(2)}) collective-permute-start(s16[104,128]{1,0:T(8,128)(2,1)S(1)} %combine.3.own), channel_id=1, source_target_pairs={{0,8},{4,12},{8,0},{12,4},{16,24},{20,28},{24,16},{28,20},{1,9},{5... | collective-permute-start | bytes 79880 | tf_op jit(solution)/shard_map/ppermute | solution.py:1025
  26.0 4.8 %collective-permute-start.8 = (s16[104,128]{1,0:T(8,128)(2,1)S(1)}, s16[104,128]{1,0:T(8,128)(2,1)S(1)}, u32[]{:S(2)}, u32[]{:S(2)}) collective-permute-start(s16[104,128]{1,0:T(8,128)(2,1)S(1)} %combine.4.own), channel_id=1, source_target_pairs={{0,16},{4,20},{8,24},{12,28},{16,0},{20,4},{24,8},{28,12},{1,17},{... | collective-permute-start | bytes 79880 | tf_op jit(solution)/shard_map/ppermute | solution.py:1025
  35.0 13.9 %collective-permute-start.9 = (bf16[5,32,128]{2,1,0:T(8,128)(2,1)S(1)}, bf16[5,32,128]{2,1,0:T(8,128)(2,1)S(1)}, u32[]{:S(2)}, u32[]{:S(2)}) collective-permute-start(bf16[5,32,128]{2,1,0:T(8,128)(2,1)S(1)} %get-tuple-element.43), channel_id=1, source_target_pairs={{0,4},{4,0},{8,12},{12,8},{16,20},{20,16},{24,28},{28,24},{1,5},{5... | collective-permute-start | bytes 122888 | tf_op jit(solution)/shard_map/ppermute | solution.py:50
  35.2 13.8 %collective-permute-start.10 = (bf16[5,32,128]{2,1,0:T(8,128)(2,1)S(1)}, bf16[5,32,128]{2,1,0:T(8,128)(2,1)S(1)}, u32[]{:S(2)}, u32[]{:S(2)}) collective-permute-start(bf16[5,32,128]{2,1,0:T(8,128)(2,1)S(1)} %get-tuple-element.44), channel_id=1, source_target_pairs={{0,28},{4,8},{8,4},{12,16},{16,12},{20,24},{24,20},{28,0},{1,29},{... | collective-permute-start | bytes 122888 | tf_op jit(solution)/shard_map/ppermute | solution.py:50

commit v3 on v1

--- a/solution.py
+++ b/solution.py
@@ -188,29 +188,11 @@
 
 
 TALL = 40
-FREE = [(slot, row) for slot in (1, 3, 5) for row in (0, 37, 38, 39)]
-FREE += [(slot, row) for slot in (0, 2, 4) for row in (38, 39)]
-
-
-def edges_kernel(
-    vel_ref,
-    low_ref,
-    high_ref,
-    cell_ref,
-    weight_ref,
-    segment_ref,
-    first,
-    second,
-    rows,
-    planes,
-    note,
-):
+
+
+def edges_kernel(vel_ref, low_ref, high_ref, first, second, rows, planes):
     depth, width = vel_ref.shape[1:3]
-    taps = cell_ref.shape[0]
     decode_rows(low_ref, high_ref, rows)
-    note[pl.ds(0, taps), :] = cell_ref[...].astype(jnp.float32) - 2.0**15
-    note[pl.ds(taps, taps), :] = weight_ref[...] * 2.0**17 - 2.0**14
-    note[pl.ds(2 * taps, 1), :] = segment_ref[...].astype(jnp.float32)
     coded = []
     for pair in ((0, 1), (depth - 1, depth - 2)):
         planes[...] = jnp.zeros_like(planes)
@@ -222,44 +204,25 @@
                     line = pl.ds(z, 1)
                     planes[slot, pl.ds(HALO - 1 - k, 1), :] = rows[0, dim * HALO + k, line, :]
                     planes[slot, pl.ds(HALO + width + k, 1), :] = rows[1, dim * HALO + k, line, :]
-        for index in range(2 * taps + 1):
-            slot, row = FREE[index]
-            planes[slot, pl.ds(row, 1), :] = note[pl.ds(index, 1), :] * STEP
         coded.append(encode(planes[...]))
     send_pair("span", coded[1], coded[0], first, second)
 
 
-def free_rows(first, second, start, count):
-    picked = []
-    for message in (first, second):
-        picked.append(
-            jnp.concatenate(
-                [
-                    message[slot].astype(jnp.int32)[row : row + 1]
-                    for slot, row in FREE[start : start + count]
-                ],
-                axis=0,
-            )
-        )
-    return below_above("span", *picked)
-
-
-def edge_planes(vel, low, high, cells, weights, segments):
+def edge_planes(vel, low, high):
     pair = full((6, TALL, LANES), jnp.int16)
     return pl.pallas_call(
         edges_kernel,
         out_shape=(pair, pair),
-        in_specs=in_vmem(6),
+        in_specs=in_vmem(3),
         out_specs=tuple(in_vmem(2)),
         scratch_shapes=[
             pltpu.VMEM((2, 3 * HALO, vel.shape[1], LANES), jnp.float32),
             pltpu.VMEM((6, TALL, LANES), jnp.float32),
-            pltpu.VMEM((2 * cells.shape[0] + 8, LANES), jnp.float32),
         ],
         compiler_params=params(),
         cost_estimate=cost(0.2),
         name="edges",
-    )(vel, low, high, cells, weights, segments)
+    )(vel, low, high)
 
 
 def strain_parts(ref, p, row, before, here, after):
@@ -406,6 +369,7 @@
     first_ref,
     second_ref,
     partial_ref,
+    after_this,
     sums_ref,
     mag_ref,
     ext,
@@ -438,7 +402,7 @@
         sums_ref[pl.ds(index * lines, lines), :] = acc[index, pl.ds(OWN - TOP - 1, lines), :]
 
 
-def outer_sums(vel, low, high, below, above, partial):
+def outer_sums(vel, low, high, below, above, partial, after_this):
     depth, width = vel.shape[1:3]
     return pl.pallas_call(
         outer_kernel,
@@ -446,13 +410,13 @@
             full((-(-2 * (width + 2) // 8) * 8, LANES), jnp.float32),
             full((8, EXT, LANES), jnp.float32),
         ),
-        in_specs=in_vmem(6),
+        in_specs=in_vmem(6) + [pl.BlockSpec(memory_space=pl.ANY)],
         out_specs=tuple(in_vmem(2)),
         scratch_shapes=model_scratch(6, depth) + [pltpu.VMEM((2, EXT, LANES), jnp.float32)],
         compiler_params=params(),
         cost_estimate=cost(2),
         name="outer_sums",
-    )(vel, low, high, below, above, partial)
+    )(vel, low, high, below, above, partial, after_this)
 
 
 def rows_kernel(pops, after_this, first, second, rows):
@@ -623,6 +587,53 @@
     )(populations, before, after, after_this)
 
 
+PART_STEP = 2.0**-13
+ACTING = (0, 1, 3, 4)
+
+
+def leaving_kernel(pops, first, second, after_this, out_first, out_second, stage):
+    depth, width = pops.shape[1:3]
+    rows = [
+        below_above("cross", first[q].astype(jnp.float32), second[q].astype(jnp.float32))
+        for q in range(19)
+    ]
+    halo = [relax_parts([pair[side] for pair in rows]) for side in range(2)]
+    coded = []
+    for wanted, z in ((FALLING, 0), (RISING, depth - 1)):
+        stage[...] = jnp.zeros_like(stage)
+        for half in range(width // 16):
+            at = pl.ds(16 * half, 16)
+            base, shear = relax_parts([pops[q, z, at, :].astype(jnp.float32) for q in range(19)])
+            for index, q in enumerate(wanted):
+                stage[index, at, :] = base[q]
+            for index, k in enumerate(ACTING):
+                stage[5 + index, at, :] = 2.0 * shear[k]
+        for side, (base, shear) in enumerate(halo):
+            at = pl.ds(width + side, 1)
+            for index, q in enumerate(wanted):
+                stage[index, at, :] = base[q][z : z + 1]
+            for index, k in enumerate(ACTING):
+                stage[5 + index, at, :] = 2.0 * shear[k][z : z + 1]
+        coded.append(
+            jnp.round(stage[...] * (1.0 / PART_STEP)).astype(jnp.int32).astype(jnp.int16)
+        )
+    send_pair("span", coded[1], coded[0], out_first, out_second)
+
+
+def leaving(populations, first, second, after_this):
+    part = full((9, TALL, LANES), jnp.int16)
+    return pl.pallas_call(
+        leaving_kernel,
+        out_shape=(part, part),
+        in_specs=in_vmem(3) + [pl.BlockSpec(memory_space=pl.ANY)],
+        out_specs=tuple(in_vmem(2)),
+        scratch_shapes=[pltpu.VMEM((9, TALL, LANES), jnp.float32)],
+        compiler_params=params(),
+        cost_estimate=cost(0.5),
+        name="leaving",
+    )(populations, first, second, after_this)
+
+
 def table_rows(table, at, low_at, flux):
     for dim in range(3):
         coarse, fine = split(flux[dim])
@@ -637,7 +648,7 @@
             flux[dim] = flux[dim] + moved if sign > 0 else flux[dim] - moved
 
 
-def marker_force(table, picks, lanes, weights, taps):
+def marker_force(table, picks, lanes, weights):
     lane_of = lax.broadcasted_iota(jnp.int32, (LANES, lanes[0].shape[1]), 0)
     picked = lax.dot_general(
         table,
@@ -652,9 +663,7 @@
         at = slice(tap * markers, (tap + 1) * markers)
         for dim in range(3):
             force[dim] = force[dim] + picked[dim * LANES : (dim + 1) * LANES, at] * mask
-        if (tap + 1) % taps == 0:
-            yield [jnp.sum(part, axis=0, keepdims=True) for part in force]
-            force = [0.0, 0.0, 0.0]
+    return [jnp.sum(part, axis=0, keepdims=True) for part in force]
 
 
 def step_kernel(
@@ -668,18 +677,15 @@
     cell_ref,
     weight_ref,
     segment_ref,
-    note_first,
-    note_second,
+    part_first,
+    part_second,
     next_hbm,
     eddy_ref,
     partial_ref,
-    first_ref,
-    second_ref,
     post,
     nexts,
     table,
-    face_table,
-    faces,
+    arrived,
     eddy,
     line,
     out_sems,
@@ -709,7 +715,25 @@
         for index, q in enumerate(wanted):
             out = edge_ref[side, index] + changes[q]
             for z in range(depth):
-                post[q, z, pl.ds(place, 1), :] = out[z : z + 1]
+                post[q, z + 1, pl.ds(place, 1), :] = out[z : z + 1]
+
+    parts = [
+        message[...].astype(jnp.int32).astype(jnp.float32) for message in (part_first, part_second)
+    ]
+    arrived[0], arrived[1] = below_above("span", *parts)
+    for side, (wanted, p, slot) in enumerate(((RISING, 0, 0), (FALLING, depth + 1, 7))):
+        pieces = [(16 * half, 16, OWN - TOP + 16 * half, FIRST + 16 * half, wanted) for half in range(width // 16)]
+        pieces.append((width, 1, OWN - TOP - 1, FIRST - 1, BEFORE))
+        pieces.append((width + 1, 1, OWN - TOP + width, FIRST + width, AFTER))
+        for start, count, around, place, needed in pieces:
+            at, around = pl.ds(start, count), pl.ds(around, count)
+            rate = relax_rate(eddy[around, :], mag_out_ref[slot, around, :])
+            n, w, xz, yz = [arrived[side, 5 + k, at, :] * (0.5 * PART_STEP) for k in range(4)]
+            changes = shear_changes([n, w, jnp.zeros_like(n), xz, yz], rate)
+            for index, q in enumerate(wanted):
+                if q in needed:
+                    value = arrived[side, index, at, :] * PART_STEP + changes[q]
+                    post[q, p, pl.ds(place, count), :] = value
 
     def collide(z, size_ref, at):
         for half in range(width // 16):
@@ -721,7 +745,7 @@
                 value = base_ref[q, z, rows, :]
                 if q:
                     value = value + changes[q]
-                post[q, z, pl.ds(FIRST + 16 * half, 16), :] = value
+                post[q, z + 1, pl.ds(FIRST + 16 * half, 16), :] = value
 
     def inner(z, carry):
         collide(z, mag_in_ref, z - 1)
@@ -733,17 +757,15 @@
 
     def shifted(q, z, half):
         shift_x, shift_y, _ = VELOCITIES[q]
-        piece = post[q, z, pl.ds(FIRST + 16 * half - shift_y, 16), :]
+        piece = post[q, z + 1, pl.ds(FIRST + 16 * half - shift_y, 16), :]
         if shift_x:
             piece = minus(piece) if shift_x > 0 else plus(piece)
         return piece.astype(jnp.bfloat16)
 
-    def run(z, leave_out=()):
+    def run(z, carry):
         for half in range(width // 16):
             flux = [0.0, 0.0, 0.0]
             for q in range(19):
-                if q in leave_out:
-                    continue
                 moved = shifted(q, z - VELOCITIES[q][2], half)
                 nexts[q, z, pl.ds(16 * half, 16), :] = moved
                 if q:
@@ -751,33 +773,12 @@
             row = pl.multiple_of(z * width + 16 * half, 16)
             low_row = pl.multiple_of((depth + z) * width + 16 * half, 16)
             table_rows(table, pl.ds(row, 16), pl.ds(low_row, 16), flux)
-
-    def run_inner(z, carry):
-        run(z)
         return carry
-
-    for side, (wanted, z) in enumerate(((RISING, depth - 1), (FALLING, 0))):
-        for half in range(width // 16):
-            rows = pl.ds(16 * half, 16)
-            flux = [0.0, 0.0, 0.0]
-            for index, q in enumerate(wanted):
-                moved = shifted(q, z, half)
-                faces[side, index, rows, :] = moved
-                add_flux(flux, q, moved.astype(jnp.float32))
-            row = side * width + 16 * half
-            table_rows(face_table, pl.ds(row, 16), pl.ds(2 * width + row, 16), flux)
-    send_pair("span", faces[0], faces[1], first_ref, second_ref)
 
     outs = []
     for index in range(4):
         start, stop = index * part, (index + 1) * part
-        if index == 0:
-            run(0, RISING)
-            start += 1
-        if index == 3:
-            run(depth - 1, FALLING)
-            stop -= 1
-        plane_loop(start, stop, run_inner, 0, 4)
+        plane_loop(start, stop, run, 0, 4)
         place = pl.ds(index * part, part)
         outs.append(
             pltpu.make_async_copy(nexts.at[:, place], next_hbm.at[:, place], out_sems.at[index])
@@ -787,8 +788,6 @@
     owners = partial_ref.shape[0]
     taps, markers = cell_ref.shape
     cells_all = depth * width
-    note_below, note_above = free_rows(note_first, note_second, 0, 2 * taps + 1)
-
     def one_hot(rows, period, wanted):
         row_of = lax.broadcasted_iota(jnp.int32, (period, markers), 0)
         picks = []
@@ -804,41 +803,22 @@
         return [array[tap : tap + 1, :] for tap in range(taps)]
 
     row, lane = row_lane(cell_ref[...])
-    forces = list(
-        marker_force(
-            table[...],
-            one_hot(2 * cells_all, cells_all, row),
-            each(lane),
-            each(weight_ref[...]),
-            taps,
-        )
+    force = marker_force(
+        table[...],
+        one_hot(2 * cells_all, cells_all, row),
+        each(lane),
+        each(weight_ref[...]),
     )
-    segments = [segment_ref[...]]
-    picks, lanes, weights = [], [], []
-    for side, note in enumerate((note_above, note_below)):
-        row, lane = row_lane(note[:taps] + 2**15)
-        row = row - side * (cells_all - width)
-        inside = jnp.logical_and(row >= 0, row < width)
-        picks += one_hot(4 * width, 2 * width, jnp.where(inside, row + side * width, -1))
-        lanes += each(lane)
-        weights += each(
-            (note[taps : 2 * taps].astype(jnp.float32) + 2.0**14) * 2.0**-17
-        )
-        segments.append(note[2 * taps : 2 * taps + 1])
-    forces += list(marker_force(face_table[...], picks, lanes, weights, taps))
 
     owner_of = lax.broadcasted_iota(jnp.int32, (owners, markers), 0)
     place_of = lax.broadcasted_iota(jnp.int32, (SEG_DEV, markers), 0)
-    mine, spread = [], []
-    for force, segment in zip(forces, segments):
-        hit = jnp.where(owner_of == lax.shift_right_logical(segment, 3), 1.0, 0.0)
-        mine.append(hit.astype(jnp.bfloat16))
-        place = place_of == lax.bitwise_and(segment, SEG_DEV - 1)
-        spread.append(
-            jnp.concatenate([jnp.where(place, part, 0.0) for part in force], axis=0)
-        )
-    mine, rest = jnp.concatenate(mine, axis=1), jnp.concatenate(spread, axis=1)
-    rest = jnp.concatenate([rest, jnp.zeros((LANES - 3 * SEG_DEV, 3 * markers), jnp.float32)], axis=0)
+    segment = segment_ref[...]
+    mine = jnp.where(owner_of == lax.shift_right_logical(segment, 3), 1.0, 0.0)
+    mine = mine.astype(jnp.bfloat16)
+    place = place_of == lax.bitwise_and(segment, SEG_DEV - 1)
+    rest = [jnp.where(place, part, 0.0) for part in force]
+    rest.append(jnp.zeros((LANES - 3 * SEG_DEV, markers), jnp.float32))
+    rest = jnp.concatenate(rest, axis=0)
     totals = 0.0
     for _ in range(3):
         coarse = rest.astype(jnp.bfloat16)
@@ -851,26 +831,22 @@
         copy.wait()
 
 
-def step(parts, sums, mag_in, mag_out, cells, weights, segments, notes, owners):
+def step(parts, sums, mag_in, mag_out, cells, weights, segments, messages, owners):
     _, depth, width, lanes = parts[0].shape
-    face = full((5, width, lanes), jnp.bfloat16)
     return pl.pallas_call(
         step_kernel,
         out_shape=(
             full((19, depth, width, lanes), jnp.bfloat16),
             full((width, lanes), jnp.float32),
             full((owners, 1, lanes), jnp.float32),
-            face,
-            face,
         ),
         in_specs=in_vmem(12),
-        out_specs=(pl.BlockSpec(memory_space=pl.ANY),) + tuple(in_vmem(4)),
+        out_specs=(pl.BlockSpec(memory_space=pl.ANY),) + tuple(in_vmem(2)),
         scratch_shapes=[
-            pltpu.VMEM((19, depth, FIRST + width + 8, lanes), jnp.float32),
+            pltpu.VMEM((19, depth + 2, FIRST + width + 8, lanes), jnp.float32),
             pltpu.VMEM((19, depth, width, lanes), jnp.bfloat16),
             pltpu.VMEM((2 * depth * width, 3 * lanes), jnp.bfloat16),
-            pltpu.VMEM((4 * width, 3 * lanes), jnp.bfloat16),
-            pltpu.VMEM((2, 5, width, lanes), jnp.bfloat16),
+            pltpu.VMEM((2, 9, TALL, lanes), jnp.float32),
             pltpu.VMEM((EXT, lanes), jnp.float32),
             pltpu.VMEM((depth, lanes), jnp.float32),
             pltpu.SemaphoreType.DMA((4,)),
@@ -878,59 +854,23 @@
         compiler_params=params(),
         cost_estimate=cost(5),
         name="step",
-    )(*parts, sums, mag_in, mag_out, cells, weights, segments, *notes)
-
-
-def arrive_kernel(next_in, first, second, arrived_hbm, next_hbm, force_ref, arrived, sems):
-    depth = next_hbm.shape[1]
-    odd = is_odd("span")
-    shares = pltpu.make_async_copy(arrived_hbm, arrived, sems.at[10])
-    shares.start()
-
-    def place(below, above):
-        copies = []
-        for source, wanted, z in ((below, RISING, 0), (above, FALLING, depth - 1)):
-            for index, q in enumerate(wanted):
-                copies.append(
-                    pltpu.make_async_copy(source.at[index], next_hbm.at[q, z], sems.at[len(copies)])
-                )
-                copies[-1].start()
-        for copy in copies:
-            copy.wait()
-
-    @pl.when(odd)
-    def _():
-        place(first, second)
-
-    @pl.when(jnp.logical_not(odd))
-    def _():
-        place(second, first)
-
-    shares.wait()
-    total = jnp.sum(arrived[:, 0, :], axis=0, keepdims=True)
+    )(*parts, sums, mag_in, mag_out, cells, weights, segments, *messages)
+
+
+def finish_kernel(arrived_ref, out_ref):
+    total = jnp.sum(arrived_ref[:, 0, :], axis=0, keepdims=True)
     for dim in range(3):
-        force_ref[pl.ds(dim, 1), :] = total[:, dim * SEG_DEV : (dim + 1) * SEG_DEV]
-
-
-def arrive(populations_next, first, second, arrived):
-    hbm = pl.BlockSpec(memory_space=pl.ANY)
+        out_ref[pl.ds(dim, 1), :] = total[:, dim * SEG_DEV : (dim + 1) * SEG_DEV]
+
+
+def finish(arrived):
     return pl.pallas_call(
-        arrive_kernel,
-        out_shape=(
-            full(populations_next.shape, jnp.bfloat16),
-            full((3, SEG_DEV), jnp.float32),
-        ),
-        in_specs=[hbm] + in_vmem(2) + [hbm],
-        out_specs=(hbm, in_vmem(1)[0]),
-        input_output_aliases={0: 0},
-        scratch_shapes=[
-            pltpu.VMEM(arrived.shape, jnp.float32),
-            pltpu.SemaphoreType.DMA((11,)),
-        ],
-        compiler_params=params(),
-        cost_estimate=cost(0.5),
-        name="arrive",
-    )(populations_next, first, second, arrived)
+        finish_kernel,
+        out_shape=full((3, SEG_DEV), jnp.float32),
+        in_specs=in_vmem(1),
+        out_specs=in_vmem(1)[0],
+        name="finish",
+    )(arrived)
 
 
 def local(populations, cell_index, marker_weight, segment_id):
@@ -938,26 +878,32 @@
     cells, weights, segments = cell_index.T, marker_weight.T, segment_id[None, :]
     vel, *lines = block_moments(populations)
     lines = swap(*lines, "cross")
-    planes = swap(*edge_planes(vel, *lines, cells, weights, segments), "span")
+    planes = swap(*edge_planes(vel, *lines), "span")
     partial, mag_in = inner_sums(vel, *lines)
-    faces = swap(*face_rows(populations, partial), "cross")
-    sums, mag_out = outer_sums(vel, *lines, *planes, partial)
+    faces = face_rows(populations, partial)
+    sums, mag_out = outer_sums(vel, *lines, *planes, partial, faces[0])
+    faces = swap(*faces, "cross")
+    messages = leaving(populations, *faces, sums)
     parts = ready(populations, *faces, sums)
     count = lax.axis_size("span")
     if count & (count - 1):
         sums = lax.psum(sums, "span")
+        messages = swap(*messages, "span")
     else:
         distance = 1
         while distance < count:
             pairs = [(i, i ^ distance) for i in range(count)]
             sums = sums + lax.ppermute(sums, "span", pairs)
+            if distance == 1:
+                arriving = swap(*messages, "span")
+                sums, _ = lax.optimization_barrier((sums, messages))
             distance *= 2
-    moved, eddy_coeff, packed, *leaving = step(
-        parts, sums, mag_in, mag_out, cells, weights, segments, planes, owners
+        messages = arriving
+    populations_next, eddy_coeff, packed = step(
+        parts, sums, mag_in, mag_out, cells, weights, segments, messages, owners
     )
     arrived = lax.all_to_all(packed, ("span", "cross"), 0, 0)
-    populations_next, segment_force = arrive(moved, *swap(*leaving, "span"), arrived)
-    return (populations_next, eddy_coeff, segment_force)
+    return (populations_next, eddy_coeff, finish(arrived))
 
 
 def solution(mesh):

time: 50.7 us -> 48.9 us (0.964)
  waiting for transfers between devices: 9.89 us -> 8.68 us
    ppermute x3, waiting for transfers between devices: 8.01 us -> 5.52 us  [local(): sums = sums + lax.ppermute(sums, 'span', pairs)]
    ppermute x8, starting transfers between devices: 13.8 us -> 12.5 us  [swap(): return (lax.ppermute(first, axis, near), lax.ppermute(second, axis, other))]
    ppermute x8, waiting for transfers between devices: 1.88 us -> 3.16 us  [swap(): return (lax.ppermute(first, axis, near), lax.ppermute(second, axis, other))]
    ppermute x3, starting transfers between devices: 0.86 us -> 1.7 us  [local(): sums = sums + lax.ppermute(sums, 'span', pairs)]
    pallas_call x1, Pallas kernels: 4.08 us -> 3.57 us  [step(): pl.pallas_call(step_kernel, out_shape=(full((19, depth, width, lanes), jn...]
    pallas_call x2 -> x3, Pallas kernels: 1.55 us -> 1.84 us  [the longest x1 1.38 us: finish(): pl.pallas_call(finish_kernel, out_shape=full((3, SEG_DEV), jnp.float32),...]
  transfers between devices with their start and end apart: 11 -> 11, of which waited for: 5 -> 4; matrix products, arithmetic and copies ran while one was open for 0% -> 0% of each run, Pallas kernels for 11% -> 15%
where the time goes in v3:
time: 48.9 us; the launch traced here: 48.7 us
  starting transfers between devices  14.2 us (29%)
  Pallas kernels  12.9 us (26%)
  blocking collectives  10.4 us (21%)
  waiting for transfers between devices  8.68 us (18%)
  local copies, waits for them, and re-layouts  1.72 us (4%)
  between operations  0.77 us (2%)
    ppermute x8, starting transfers between devices, swap(): return (lax.ppermute(first, axis, near), lax.ppermute(second, axis, other))  12.5 us
    all_to_all x1, blocking collectives, local(): arrived = lax.all_to_all(packed, ('span', 'cross'), 0, 0)  10.4 us
    ppermute x3, waiting for transfers between devices, local(): sums = sums + lax.ppermute(sums, 'span', pairs)  5.52 us
    pallas_call x1, Pallas kernels, step(): pl.pallas_call(step_kernel, out_shape=(full((19, depth, width, lanes), jn...  3.57 us
    pallas_call x1, Pallas kernels, inner_sums(): pl.pallas_call(inner_kernel, out_shape=(full((2, EXT, LANES), jnp.float32...  3.23 us
    ppermute x8, waiting for transfers between devices, swap(): return (lax.ppermute(first, axis, near), lax.ppermute(second, axis, other))  3.16 us
    pallas_call x1, Pallas kernels, ready(): pl.pallas_call(ready_kernel, out_shape=(full((19, depth, width, lanes), j...  1.99 us
    unnamed x10, local copies, waits for them, and re-layouts  1.72 us
  transfers between devices with their start and end apart: 11, of which 4 were waited for; matrix products, arithmetic and copies ran while one was open for 0% of the time, Pallas kernels for 15%

profile of v3, /device:TPU:0, one launch (start us, length us, event | category | flops | bytes accessed | tf_op | source)
XLA Modules:
  0.0 48.7 jit_solution(8902066991684160067)
XLA Ops:
  0.6 1.7 %copy-done = bf16[19,16,32,128]{3,2,1,0:T(8,128)(2,1)S(1)} copy-done((bf16[19,16,32,128]{3,2,1,0:T(8,128)(2,1)S(1)}, bf16[19,16,32,128]{3,2,1,0:T(8,128)(2,1)}, u32[]{:S(2)}) %copy-start) | copy-done | bytes 2490392
  2.3 0.6 %moments.1 = (f32[3,16,32,128]{3,2,1,0:T(8,128)S(1)}, s16[9,16,128]{2,1,0:T(8,128)(2,1)S(1)}, s16[9,16,128]{2,1,0:T(8,128)(2,1)S(1)}) custom-call(bf16[19,16,32,128]{3,2,1,0:T(8,128)(2,1)S(1)} %copy-done), custom_call_target="tpu_custom_call" | custom-call | bytes 3600000 | tf_op jit(solution)/shard_map/moments/pallas_call | solution.py:164
  2.9 0.5 %collective-permute-start = (s16[9,16,128]{2,1,0:T(8,128)(2,1)S(1)}, s16[9,16,128]{2,1,0:T(8,128)(2,1)S(1)}, u32[]{:S(2)}, u32[]{:S(2)}) collective-permute-start(s16[9,16,128]{2,1,0:T(8,128)(2,1)S(1)} %get-tuple-element.25), channel_id=1, source_target_pairs={{0,1},{1,0},{2,3},{3,2},{4,5},{5,4},{6,7},{7,6},{8,9},{9,8},{10,11... | collective-permute-start | bytes 110600 | tf_op jit(solution)/shard_map/ppermute | solution.py:50
  3.5 2.6 %collective-permute-start.1 = (s16[9,16,128]{2,1,0:T(8,128)(2,1)S(1)}, s16[9,16,128]{2,1,0:T(8,128)(2,1)S(1)}, u32[]{:S(2)}, u32[]{:S(2)}) collective-permute-start(s16[9,16,128]{2,1,0:T(8,128)(2,1)S(1)} %get-tuple-element.26), channel_id=1, source_target_pairs={{0,3},{1,2},{2,1},{3,0},{4,7},{5,6},{6,5},{7,4},{8,11},{9,10},{10,... | collective-permute-start | bytes 110600 | tf_op jit(solution)/shard_map/ppermute | solution.py:50
  6.1 0.0 collective-permute-done.low_ref
  6.1 1.8 %collective-permute-done.1.high_ref = s16[9,16,128]{2,1,0:T(8,128)(2,1)S(1)} collective-permute-done((s16[9,16,128]{2,1,0:T(8,128)(2,1)S(1)}, s16[9,16,128]{2,1,0:T(8,128)(2,1)S(1)}, u32[]{:S(2)}, u32[]{:S(2)}) %collective-permute-start.1) | collective-permute-done | bytes 36896 | tf_op jit(solution)/shard_map/ppermute | solution.py:50
  7.9 0.1 edges.1
  8.0 1.6 %collective-permute-start.4 = (s16[6,40,128]{2,1,0:T(8,128)(2,1)S(1)}, s16[6,40,128]{2,1,0:T(8,128)(2,1)S(1)}, u32[]{:S(2)}, u32[]{:S(2)}) collective-permute-start(s16[6,40,128]{2,1,0:T(8,128)(2,1)S(1)} %get-tuple-element.30), channel_id=1, source_target_pairs={{0,4},{4,0},{8,12},{12,8},{16,20},{20,16},{24,28},{28,24},{1,5},{5... | collective-permute-start | bytes 184328 | tf_op jit(solution)/shard_map/ppermute | solution.py:50
  9.6 3.6 %collective-permute-start.5 = (s16[6,40,128]{2,1,0:T(8,128)(2,1)S(1)}, s16[6,40,128]{2,1,0:T(8,128)(2,1)S(1)}, u32[]{:S(2)}, u32[]{:S(2)}) collective-permute-start(s16[6,40,128]{2,1,0:T(8,128)(2,1)S(1)} %get-tuple-element.31), channel_id=1, source_target_pairs={{0,28},{4,8},{8,4},{12,16},{16,12},{20,24},{24,20},{28,0},{1,29},{... | collective-permute-start | bytes 184328 | tf_op jit(solution)/shard_map/ppermute | solution.py:50
  13.2 3.2 %inner_sums.1 = (f32[2,40,128]{2,1,0:T(8,128)S(1)}, f32[14,40,128]{2,1,0:T(8,128)S(1)}) custom-call(f32[3,16,32,128]{3,2,1,0:T(8,128)S(1)} %get-tuple-element.24.vel_ref, s16[9,16,128]{2,1,0:T(8,128)(2,1)S(1)} %collective-permute-done.low_ref, s16[9,16,128]{2,1,0:T(8,128)(2,1)S(1)} %collective-permute-done.1.high_ref), custom_call_target="tpu_custom_call" | custom-call | bytes 18000000 | tf_op jit(solution)/shard_map/inner_sums/pallas_call | solution.py:350
  16.4 0.2 face_rows.1
  16.6 1.1 %collective-permute-start.3 = (bf16[19,16,128]{2,1,0:T(8,128)(2,1)S(1)}, bf16[19,16,128]{2,1,0:T(8,128)(2,1)S(1)}, u32[]{:S(2)}, u32[]{:S(2)}) collective-permute-start(bf16[19,16,128]{2,1,0:T(8,128)(2,1)S(1)} %get-tuple-element.29), channel_id=1, source_target_pairs={{0,3},{1,2},{2,1},{3,0},{4,7},{5,6},{6,5},{7,4},{8,11},{9,10},{10,... | collective-permute-start | bytes 233480 | tf_op jit(solution)/shard_map/ppermute | solution.py:50
  17.7 0.6 %collective-permute-start.2 = (bf16[19,16,128]{2,1,0:T(8,128)(2,1)S(1)}, bf16[19,16,128]{2,1,0:T(8,128)(2,1)S(1)}, u32[]{:S(2)}, u32[]{:S(2)}) collective-permute-start(bf16[19,16,128]{2,1,0:T(8,128)(2,1)S(1)} %get-tuple-element.28.after_this), channel_id=1, source_target_pairs={{0,1},{1,0},{2,3},{3,2},{4,5},{5,4},{6,7},{7,6},{8,9},{9,8},{10,11... | collective-permute-start | bytes 233480 | tf_op jit(solution)/shard_map/ppermute | solution.py:50
  18.3 1.4 %outer_sums.1 = (f32[72,128]{1,0:T(8,128)S(1)}, f32[8,40,128]{2,1,0:T(8,128)S(1)}) custom-call(f32[3,16,32,128]{3,2,1,0:T(8,128)S(1)} %get-tuple-element.24.vel_ref, s16[9,16,128]{2,1,0:T(8,128)(2,1)S(1)} %collective-permute-done.low_ref, s16[9,16,128]{2,1,0:T(8,128)(2,1)S(1)} %collective-permute-done.1.high_ref, ...), custom_call_target="tpu_custom_call" | custom-call | bytes 7200000 | tf_op jit(solution)/shard_map/outer_sums/pallas_call | solution.py:407
  19.8 0.0 copy-start.3
  19.8 0.0 copy-start.4
  19.8 0.1 collective-permute-start.6
  19.9 1.4 %collective-permute-done.3.second = bf16[19,16,128]{2,1,0:T(8,128)(2,1)S(1)} collective-permute-done((bf16[19,16,128]{2,1,0:T(8,128)(2,1)S(1)}, bf16[19,16,128]{2,1,0:T(8,128)(2,1)S(1)}, u32[]{:S(2)}, u32[]{:S(2)}) %collective-permute-start.3) | collective-permute-done | bytes 77856 | tf_op jit(solution)/shard_map/ppermute | solution.py:50
  21.3 0.0 collective-permute-done.2.first
  21.3 0.3 leaving.1
  21.6 0.7 %collective-permute-start.9 = (s16[9,40,128]{2,1,0:T(8,128)(2,1)S(1)}, s16[9,40,128]{2,1,0:T(8,128)(2,1)S(1)}, u32[]{:S(2)}, u32[]{:S(2)}) collective-permute-start(s16[9,40,128]{2,1,0:T(8,128)(2,1)S(1)} %get-tuple-element.37), channel_id=1, source_target_pairs={{0,4},{4,0},{8,12},{12,8},{16,20},{20,16},{24,28},{28,24},{1,5},{5... | collective-permute-start | bytes 276488 | tf_op jit(solution)/shard_map/ppermute | solution.py:50
  22.3 1.7 %collective-permute-start.10 = (s16[9,40,128]{2,1,0:T(8,128)(2,1)S(1)}, s16[9,40,128]{2,1,0:T(8,128)(2,1)S(1)}, u32[]{:S(2)}, u32[]{:S(2)}) collective-permute-start(s16[9,40,128]{2,1,0:T(8,128)(2,1)S(1)} %get-tuple-element.38), channel_id=1, source_target_pairs={{0,28},{4,8},{8,4},{12,16},{16,12},{20,24},{24,20},{28,0},{1,29},{... | collective-permute-start | bytes 276488 | tf_op jit(solution)/shard_map/ppermute | solution.py:50
  24.1 1.2 %collective-permute-start.7 = (f32[72,128]{1,0:T(8,128)S(1)}, f32[72,128]{1,0:T(8,128)S(1)}, u32[]{:S(2)}, u32[]{:S(2)}) collective-permute-start(f32[72,128]{1,0:T(8,128)S(1)} %add.9), channel_id=1, source_target_pairs={{0,8},{4,12},{8,0},{12,4},{16,24},{20,28},{24,16},{28,20},{1,9},{5... | collective-permute-start | bytes 110600 | tf_op jit(solution)/shard_map/ppermute | solution.py:896
  25.3 3.1 %collective-permute-done.7 = f32[72,128]{1,0:T(8,128)S(1)} collective-permute-done((f32[72,128]{1,0:T(8,128)S(1)}, f32[72,128]{1,0:T(8,128)S(1)}, u32[]{:S(2)}, u32[]{:S(2)}) %collective-permute-start.7) | collective-permute-done | bytes 36896 | tf_op jit(solution)/shard_map/ppermute | solution.py:896
  28.4 0.4 collective-permute-start.8
  28.8 2.0 %ready.1 = (f32[19,16,32,128]{3,2,1,0:T(8,128)S(1)}, f32[5,16,32,128]{3,2,1,0:T(8,128)S(1)}, f32[2,5,16,128]{3,2,1,0:T(8,128)S(1)}, f32[2,5,16,128]{3,2,1,0:T(8,128)S(1)}) custom-call(bf16[19,16,32,128]{3,2,1,0:T(8,128)(2,1)S(1)} %copy-done.1, bf16[19,16,128]{2,1,0:T(8,128)(2,1)S(1)} %collective-permute-done.2.first, ...), custom_call_target="tpu_custom_call" | custom-call | bytes 9000000 | tf_op jit(solution)/shard_map/ready/pallas_call | solution.py:574
  30.8 2.4 %collective-permute-done.8 = f32[72,128]{1,0:T(8,128)S(1)} collective-permute-done((f32[72,128]{1,0:T(8,128)S(1)}, f32[72,128]{1,0:T(8,128)S(1)}, u32[]{:S(2)}, u32[]{:S(2)}) %collective-permute-start.8) | collective-permute-done | bytes 36896 | tf_op jit(solution)/shard_map/ppermute | solution.py:896
  33.2 0.0 collective-permute-done.9.part_first
  33.2 0.0 collective-permute-done.10.part_second
  33.3 3.6 %step.1 = (bf16[19,16,32,128]{3,2,1,0:T(8,128)(2,1)}, f32[32,128]{1,0:T(8,128)}, f32[32,1,128]{2,1,0:T(1,128)S(1)}) custom-call(f32[19,16,32,128]{3,2,1,0:T(8,128)S(1)} %get-tuple-element.33.base_ref, f32[5,16,32,128]{3,2,1,0:T(8,128)S(1)} %get-tuple-element.34.shear_ref, f32[2,5,16,128]{3,2,1,0:T(8,128)S(1)} %get-tuple-element.35.edge_ref, ...), custom_call_target="tpu_custom_call" | custom-call | bytes 18000000 | tf_op jit(solution)/shard_map/step/pallas_call | solution.py:836
  36.9 10.4 %all_to_all.5.arrived_ref = f32[32,1,128]{2,1,0:T(1,128)} all-to-all(f32[32,1,128]{2,1,0:T(1,128)S(1)} %get-tuple-element.44), channel_id=1, replica_groups=mesh['span'=8,'cross'=4] {'span','cross'}, dimensions={0} | all-to-all | bytes 32768 | tf_op jit(solution)/shard_map/all_to_all | solution.py:905
  47.3 1.4 %finish.1 = f32[3,8]{1,0:T(4,128)} custom-call(f32[32,1,128]{2,1,0:T(1,128)} %all_to_all.5.arrived_ref), custom_call_target="tpu_custom_call" | custom-call | tf_op jit(solution)/shard_map/finish/pallas_call | solution.py:867
  (13 shorter events, 0.0 us)
Async XLA Ops:
  0.6 1.7 %copy-start = (bf16[19,16,32,128]{3,2,1,0:T(8,128)(2,1)S(1)}, bf16[19,16,32,128]{3,2,1,0:T(8,128)(2,1)}, u32[]{:S(2)}) copy-start(bf16[19,16,32,128]{3,2,1,0:T(8,128)(2,1)} %pops.7) | copy-start | bytes 7471108
  2.3 14.1 %copy-start.1 = (bf16[19,16,32,128]{3,2,1,0:T(8,128)(2,1)S(1)}, bf16[19,16,32,128]{3,2,1,0:T(8,128)(2,1)}, u32[]{:S(2)}) copy-start(bf16[19,16,32,128]{3,2,1,0:T(8,128)(2,1)} %pops.7) | copy-start | bytes 7471108
  2.9 3.2 %collective-permute-start = (s16[9,16,128]{2,1,0:T(8,128)(2,1)S(1)}, s16[9,16,128]{2,1,0:T(8,128)(2,1)S(1)}, u32[]{:S(2)}, u32[]{:S(2)}) collective-permute-start(s16[9,16,128]{2,1,0:T(8,128)(2,1)S(1)} %get-tuple-element.25), channel_id=1, source_target_pairs={{0,1},{1,0},{2,3},{3,2},{4,5},{5,4},{6,7},{7,6},{8,9},{9,8},{10,11... | collective-permute-start | bytes 110600 | tf_op jit(solution)/shard_map/ppermute | solution.py:50
  3.5 4.4 %collective-permute-start.1 = (s16[9,16,128]{2,1,0:T(8,128)(2,1)S(1)}, s16[9,16,128]{2,1,0:T(8,128)(2,1)S(1)}, u32[]{:S(2)}, u32[]{:S(2)}) collective-permute-start(s16[9,16,128]{2,1,0:T(8,128)(2,1)S(1)} %get-tuple-element.26), channel_id=1, source_target_pairs={{0,3},{1,2},{2,1},{3,0},{4,7},{5,6},{6,5},{7,4},{8,11},{9,10},{10,... | collective-permute-start | bytes 110600 | tf_op jit(solution)/shard_map/ppermute | solution.py:50
  8.0 10.4 %collective-permute-start.4 = (s16[6,40,128]{2,1,0:T(8,128)(2,1)S(1)}, s16[6,40,128]{2,1,0:T(8,128)(2,1)S(1)}, u32[]{:S(2)}, u32[]{:S(2)}) collective-permute-start(s16[6,40,128]{2,1,0:T(8,128)(2,1)S(1)} %get-tuple-element.30), channel_id=1, source_target_pairs={{0,4},{4,0},{8,12},{12,8},{16,20},{20,16},{24,28},{28,24},{1,5},{5... | collective-permute-start | bytes 184328 | tf_op jit(solution)/shard_map/ppermute | solution.py:50
  9.6 8.7 %collective-permute-start.5 = (s16[6,40,128]{2,1,0:T(8,128)(2,1)S(1)}, s16[6,40,128]{2,1,0:T(8,128)(2,1)S(1)}, u32[]{:S(2)}, u32[]{:S(2)}) collective-permute-start(s16[6,40,128]{2,1,0:T(8,128)(2,1)S(1)} %get-tuple-element.31), channel_id=1, source_target_pairs={{0,28},{4,8},{8,4},{12,16},{16,12},{20,24},{24,20},{28,0},{1,29},{... | collective-permute-start | bytes 184328 | tf_op jit(solution)/shard_map/ppermute | solution.py:50
  16.6 4.6 %collective-permute-start.3 = (bf16[19,16,128]{2,1,0:T(8,128)(2,1)S(1)}, bf16[19,16,128]{2,1,0:T(8,128)(2,1)S(1)}, u32[]{:S(2)}, u32[]{:S(2)}) collective-permute-start(bf16[19,16,128]{2,1,0:T(8,128)(2,1)S(1)} %get-tuple-element.29), channel_id=1, source_target_pairs={{0,3},{1,2},{2,1},{3,0},{4,7},{5,6},{6,5},{7,4},{8,11},{9,10},{10,... | collective-permute-start | bytes 233480 | tf_op jit(solution)/shard_map/ppermute | solution.py:50
  17.7 3.6 %collective-permute-start.2 = (bf16[19,16,128]{2,1,0:T(8,128)(2,1)S(1)}, bf16[19,16,128]{2,1,0:T(8,128)(2,1)S(1)}, u32[]{:S(2)}, u32[]{:S(2)}) collective-permute-start(bf16[19,16,128]{2,1,0:T(8,128)(2,1)S(1)} %get-tuple-element.28.after_this), channel_id=1, source_target_pairs={{0,1},{1,0},{2,3},{3,2},{4,5},{5,4},{6,7},{7,6},{8,9},{9,8},{10,11... | collective-permute-start | bytes 233480 | tf_op jit(solution)/shard_map/ppermute | solution.py:50
  19.8 13.5 %copy-start.2 = (s32[128,8]{0,1:T(8,128)S(1)}, s32[128,8]{0,1:T(8,128)}, u32[]{:S(2)}) copy-start(s32[128,8]{0,1:T(8,128)} %param.5) | copy-start | bytes 12292
  19.8 13.5 %copy-start.3 = (f32[128,8]{0,1:T(8,128)S(1)}, f32[128,8]{0,1:T(8,128)}, u32[]{:S(2)}) copy-start(f32[128,8]{0,1:T(8,128)} %param.6) | copy-start | bytes 12292
  19.8 13.5 %copy-start.4 = (s32[128]{0:T(128)S(1)}, s32[128]{0:T(128)}, u32[]{:S(2)}) copy-start(s32[128]{0:T(128)} %param.7) | copy-start | bytes 1540
  19.8 4.3 %collective-permute-start.6 = (f32[72,128]{1,0:T(8,128)S(1)}, f32[72,128]{1,0:T(8,128)S(1)}, u32[]{:S(2)}, u32[]{:S(2)}) collective-permute-start(f32[72,128]{1,0:T(8,128)S(1)} %get-tuple-element.32.after_this), channel_id=1, source_target_pairs={{0,4},{4,0},{8,12},{12,8},{16,20},{20,16},{24,28},{28,24},{1,5},{5... | collective-permute-start | bytes 110600 | tf_op jit(solution)/shard_map/ppermute | solution.py:896
  21.6 11.6 %collective-permute-start.9 = (s16[9,40,128]{2,1,0:T(8,128)(2,1)S(1)}, s16[9,40,128]{2,1,0:T(8,128)(2,1)S(1)}, u32[]{:S(2)}, u32[]{:S(2)}) collective-permute-start(s16[9,40,128]{2,1,0:T(8,128)(2,1)S(1)} %get-tuple-element.37), channel_id=1, source_target_pairs={{0,4},{4,0},{8,12},{12,8},{16,20},{20,16},{24,28},{28,24},{1,5},{5... | collective-permute-start | bytes 276488 | tf_op jit(solution)/shard_map/ppermute | solution.py:50
  22.3 10.9 %collective-permute-start.10 = (s16[9,40,128]{2,1,0:T(8,128)(2,1)S(1)}, s16[9,40,128]{2,1,0:T(8,128)(2,1)S(1)}, u32[]{:S(2)}, u32[]{:S(2)}) collective-permute-start(s16[9,40,128]{2,1,0:T(8,128)(2,1)S(1)} %get-tuple-element.38), channel_id=1, source_target_pairs={{0,28},{4,8},{8,4},{12,16},{16,12},{20,24},{24,20},{28,0},{1,29},{... | collective-permute-start | bytes 276488 | tf_op jit(solution)/shard_map/ppermute | solution.py:50
  24.1 4.3 %collective-permute-start.7 = (f32[72,128]{1,0:T(8,128)S(1)}, f32[72,128]{1,0:T(8,128)S(1)}, u32[]{:S(2)}, u32[]{:S(2)}) collective-permute-start(f32[72,128]{1,0:T(8,128)S(1)} %add.9), channel_id=1, source_target_pairs={{0,8},{4,12},{8,0},{12,4},{16,24},{20,28},{24,16},{28,20},{1,9},{5... | collective-permute-start | bytes 110600 | tf_op jit(solution)/shard_map/ppermute | solution.py:896
  28.4 4.9 %collective-permute-start.8 = (f32[72,128]{1,0:T(8,128)S(1)}, f32[72,128]{1,0:T(8,128)S(1)}, u32[]{:S(2)}, u32[]{:S(2)}) collective-permute-start(f32[72,128]{1,0:T(8,128)S(1)} %add.10), channel_id=1, source_target_pairs={{0,16},{4,20},{8,24},{12,28},{16,0},{20,4},{24,8},{28,12},{1,17},{... | collective-permute-start | bytes 110600 | tf_op jit(solution)/shard_map/ppermute | solution.py:896

commit v4 on v3

--- a/solution.py
+++ b/solution.py
@@ -587,7 +587,7 @@
     )(populations, before, after, after_this)
 
 
-PART_STEP = 2.0**-13
+PART_STEP = 1.0 / 11500.0
 ACTING = (0, 1, 3, 4)
 
 
@@ -605,13 +605,13 @@
             at = pl.ds(16 * half, 16)
             base, shear = relax_parts([pops[q, z, at, :].astype(jnp.float32) for q in range(19)])
             for index, q in enumerate(wanted):
-                stage[index, at, :] = base[q]
+                stage[index, at, :] = base[q] - 0.5
             for index, k in enumerate(ACTING):
                 stage[5 + index, at, :] = 2.0 * shear[k]
         for side, (base, shear) in enumerate(halo):
             at = pl.ds(width + side, 1)
             for index, q in enumerate(wanted):
-                stage[index, at, :] = base[q][z : z + 1]
+                stage[index, at, :] = base[q][z : z + 1] - 0.5
             for index, k in enumerate(ACTING):
                 stage[5 + index, at, :] = 2.0 * shear[k][z : z + 1]
         coded.append(
@@ -648,19 +648,49 @@
             flux[dim] = flux[dim] + moved if sign > 0 else flux[dim] - moved
 
 
-def marker_force(table, picks, lanes, weights):
-    lane_of = lax.broadcasted_iota(jnp.int32, (LANES, lanes[0].shape[1]), 0)
+def picks_kernel(cell_ref, weight_ref, after_this, pick_ref, mask_ref):
+    taps, markers = cell_ref.shape
+    cells_all = pick_ref.shape[0] // 2
+    row_of = lax.broadcasted_iota(jnp.int32, (cells_all, markers), 0)
+    lane_of = lax.broadcasted_iota(jnp.int32, (LANES, markers), 0)
+    for tap in range(taps):
+        cell = cell_ref[pl.ds(tap, 1), :]
+        at = pl.ds(tap * markers, markers)
+        hit = jnp.where(row_of == lax.shift_right_logical(cell, 7), 1.0, 0.0)
+        hit = hit.astype(jnp.bfloat16)
+        pick_ref[pl.ds(0, cells_all), at] = hit
+        pick_ref[pl.ds(cells_all, cells_all), at] = hit
+        lane = lax.bitwise_and(cell, LANES - 1)
+        mask_ref[:, at] = jnp.where(lane_of == lane, -weight_ref[pl.ds(tap, 1), :], 0.0)
+
+
+def marker_picks(cells, weights, after_this, rows):
+    taps, markers = cells.shape
+    return pl.pallas_call(
+        picks_kernel,
+        out_shape=(
+            full((2 * rows, taps * markers), jnp.bfloat16),
+            full((LANES, taps * markers), jnp.float32),
+        ),
+        in_specs=in_vmem(2) + [pl.BlockSpec(memory_space=pl.ANY)],
+        out_specs=tuple(in_vmem(2)),
+        compiler_params=params(),
+        cost_estimate=cost(0.7),
+        name="picks",
+    )(cells, weights, after_this)
+
+
+def marker_force(table, pick_ref, mask_ref, markers):
     picked = lax.dot_general(
-        table,
-        jnp.concatenate(picks, axis=1),
+        table[...],
+        pick_ref[...],
         (((0,), (0,)), ((), ())),
         preferred_element_type=jnp.float32,
     )
-    markers = lanes[0].shape[1]
     force = [0.0, 0.0, 0.0]
-    for tap, (lane, weight) in enumerate(zip(lanes, weights)):
-        mask = jnp.where(lane_of == lane, -weight, 0.0)
-        at = slice(tap * markers, (tap + 1) * markers)
+    for start in range(0, pick_ref.shape[1], markers):
+        at = slice(start, start + markers)
+        mask = mask_ref[:, pl.ds(start, markers)]
         for dim in range(3):
             force[dim] = force[dim] + picked[dim * LANES : (dim + 1) * LANES, at] * mask
     return [jnp.sum(part, axis=0, keepdims=True) for part in force]
@@ -674,8 +704,8 @@
     sums_ref,
     mag_in_ref,
     mag_out_ref,
-    cell_ref,
-    weight_ref,
+    pick_ref,
+    mask_ref,
     segment_ref,
     part_first,
     part_second,
@@ -732,7 +762,7 @@
             changes = shear_changes([n, w, jnp.zeros_like(n), xz, yz], rate)
             for index, q in enumerate(wanted):
                 if q in needed:
-                    value = arrived[side, index, at, :] * PART_STEP + changes[q]
+                    value = (arrived[side, index, at, :] * PART_STEP + 0.5) + changes[q]
                     post[q, p, pl.ds(place, count), :] = value
 
     def collide(z, size_ref, at):
@@ -786,29 +816,8 @@
         outs[-1].start()
 
     owners = partial_ref.shape[0]
-    taps, markers = cell_ref.shape
-    cells_all = depth * width
-    def one_hot(rows, period, wanted):
-        row_of = lax.broadcasted_iota(jnp.int32, (period, markers), 0)
-        picks = []
-        for tap in range(taps):
-            hit = jnp.where(row_of == wanted[tap : tap + 1, :], 1.0, 0.0).astype(jnp.bfloat16)
-            picks.append(jnp.concatenate([hit] * (rows // period), axis=0))
-        return picks
-
-    def row_lane(cells):
-        return lax.shift_right_logical(cells, 7), lax.bitwise_and(cells, LANES - 1)
-
-    def each(array):
-        return [array[tap : tap + 1, :] for tap in range(taps)]
-
-    row, lane = row_lane(cell_ref[...])
-    force = marker_force(
-        table[...],
-        one_hot(2 * cells_all, cells_all, row),
-        each(lane),
-        each(weight_ref[...]),
-    )
+    markers = segment_ref.shape[1]
+    force = marker_force(table, pick_ref, mask_ref, markers)
 
     owner_of = lax.broadcasted_iota(jnp.int32, (owners, markers), 0)
     place_of = lax.broadcasted_iota(jnp.int32, (SEG_DEV, markers), 0)
@@ -831,7 +840,7 @@
         copy.wait()
 
 
-def step(parts, sums, mag_in, mag_out, cells, weights, segments, messages, owners):
+def step(parts, sums, mag_in, mag_out, picks, segments, messages, owners):
     _, depth, width, lanes = parts[0].shape
     return pl.pallas_call(
         step_kernel,
@@ -854,7 +863,7 @@
         compiler_params=params(),
         cost_estimate=cost(5),
         name="step",
-    )(*parts, sums, mag_in, mag_out, cells, weights, segments, *messages)
+    )(*parts, sums, mag_in, mag_out, *picks, segments, *messages)
 
 
 def finish_kernel(arrived_ref, out_ref):
@@ -883,24 +892,30 @@
     faces = face_rows(populations, partial)
     sums, mag_out = outer_sums(vel, *lines, *planes, partial, faces[0])
     faces = swap(*faces, "cross")
-    messages = leaving(populations, *faces, sums)
     parts = ready(populations, *faces, sums)
+    flat_rows = populations.shape[1] * populations.shape[2]
     count = lax.axis_size("span")
     if count & (count - 1):
+        arriving = swap(*leaving(populations, *faces, sums), "span")
+        picks = marker_picks(cells, weights, sums, flat_rows)
         sums = lax.psum(sums, "span")
-        messages = swap(*messages, "span")
     else:
         distance = 1
+        messages = leaving(populations, *faces, sums)
         while distance < count:
             pairs = [(i, i ^ distance) for i in range(count)]
-            sums = sums + lax.ppermute(sums, "span", pairs)
+            other = lax.ppermute(sums, "span", pairs)
             if distance == 1:
                 arriving = swap(*messages, "span")
-                sums, _ = lax.optimization_barrier((sums, messages))
+                sums, _ = lax.optimization_barrier((sums + other, messages))
+                picks = marker_picks(cells, weights, sums, flat_rows)
+            elif distance == 2:
+                sums, picks = lax.optimization_barrier((sums + other, picks))
+            else:
+                sums = sums + other
             distance *= 2
-        messages = arriving
     populations_next, eddy_coeff, packed = step(
-        parts, sums, mag_in, mag_out, cells, weights, segments, messages, owners
+        parts, sums, mag_in, mag_out, picks, segments, arriving, owners
     )
     arrived = lax.all_to_all(packed, ("span", "cross"), 0, 0)
     return (populations_next, eddy_coeff, finish(arrived))

time: 48.9 us -> 49 us (level)
  waiting for transfers between devices: 8.68 us -> 8.12 us
  Pallas kernels: 12.9 us -> 13.4 us
    ppermute x3, waiting for transfers between devices: 5.52 us -> 4.93 us  [local(): other = lax.ppermute(sums, 'span', pairs)]
    pallas_call x0 -> x1, Pallas kernels: none -> 0.58 us  [marker_picks(): pl.pallas_call(picks_kernel, out_shape=(full((2 * rows, taps * markers),...]
  transfers between devices with their start and end apart: 11 -> 11, of which waited for: 4 -> 4; matrix products, arithmetic and copies ran while one was open for 0% -> 0% of each run, Pallas kernels for 15% -> 16%
where the time goes in v4:
time: 49 us; the launch traced here: 48.7 us
  starting transfers between devices  14.2 us (29%)
  Pallas kernels  13.4 us (27%)
  blocking collectives  10.6 us (22%)
  waiting for transfers between devices  8.12 us (17%)
  local copies, waits for them, and re-layouts  1.72 us (4%)
  between operations  0.77 us (2%)
    ppermute x8, starting transfers between devices, swap(): return (lax.ppermute(first, axis, near), lax.ppermute(second, axis, other))  12.4 us
    all_to_all x1, blocking collectives, local(): arrived = lax.all_to_all(packed, ('span', 'cross'), 0, 0)  10.6 us
    ppermute x3, waiting for transfers between devices, local(): other = lax.ppermute(sums, 'span', pairs)  4.93 us
    pallas_call x1, Pallas kernels, step(): pl.pallas_call(step_kernel, out_shape=(full((19, depth, width, lanes), jn...  3.48 us
    pallas_call x1, Pallas kernels, inner_sums(): pl.pallas_call(inner_kernel, out_shape=(full((2, EXT, LANES), jnp.float32...  3.23 us
    ppermute x8, waiting for transfers between devices, swap(): return (lax.ppermute(first, axis, near), lax.ppermute(second, axis, other))  3.19 us
    pallas_call x1, Pallas kernels, ready(): pl.pallas_call(ready_kernel, out_shape=(full((19, depth, width, lanes), j...  1.98 us
    ppermute x3, starting transfers between devices, local(): other = lax.ppermute(sums, 'span', pairs)  1.75 us
  transfers between devices with their start and end apart: 11, of which 4 were waited for; matrix products, arithmetic and copies ran while one was open for 0% of the time, Pallas kernels for 16%

profile of v4, /device:TPU:0, one launch (start us, length us, event | category | flops | bytes accessed | tf_op | source)
XLA Modules:
  0.0 48.7 jit_solution(10783453407465036753)
XLA Ops:
  0.6 1.7 %copy-done = bf16[19,16,32,128]{3,2,1,0:T(8,128)(2,1)S(1)} copy-done((bf16[19,16,32,128]{3,2,1,0:T(8,128)(2,1)S(1)}, bf16[19,16,32,128]{3,2,1,0:T(8,128)(2,1)}, u32[]{:S(2)}) %copy-start) | copy-done | bytes 2490392
  2.3 0.6 %moments.1 = (f32[3,16,32,128]{3,2,1,0:T(8,128)S(1)}, s16[9,16,128]{2,1,0:T(8,128)(2,1)S(1)}, s16[9,16,128]{2,1,0:T(8,128)(2,1)S(1)}) custom-call(bf16[19,16,32,128]{3,2,1,0:T(8,128)(2,1)S(1)} %copy-done), custom_call_target="tpu_custom_call" | custom-call | bytes 3600000 | tf_op jit(solution)/shard_map/moments/pallas_call | solution.py:164
  2.9 0.5 %collective-permute-start = (s16[9,16,128]{2,1,0:T(8,128)(2,1)S(1)}, s16[9,16,128]{2,1,0:T(8,128)(2,1)S(1)}, u32[]{:S(2)}, u32[]{:S(2)}) collective-permute-start(s16[9,16,128]{2,1,0:T(8,128)(2,1)S(1)} %get-tuple-element.30), channel_id=1, source_target_pairs={{0,1},{1,0},{2,3},{3,2},{4,5},{5,4},{6,7},{7,6},{8,9},{9,8},{10,11... | collective-permute-start | bytes 110600 | tf_op jit(solution)/shard_map/ppermute | solution.py:50
  3.5 2.6 %collective-permute-start.1 = (s16[9,16,128]{2,1,0:T(8,128)(2,1)S(1)}, s16[9,16,128]{2,1,0:T(8,128)(2,1)S(1)}, u32[]{:S(2)}, u32[]{:S(2)}) collective-permute-start(s16[9,16,128]{2,1,0:T(8,128)(2,1)S(1)} %get-tuple-element.31), channel_id=1, source_target_pairs={{0,3},{1,2},{2,1},{3,0},{4,7},{5,6},{6,5},{7,4},{8,11},{9,10},{10,... | collective-permute-start | bytes 110600 | tf_op jit(solution)/shard_map/ppermute | solution.py:50
  6.1 0.0 collective-permute-done.low_ref
  6.1 1.8 %collective-permute-done.1.high_ref = s16[9,16,128]{2,1,0:T(8,128)(2,1)S(1)} collective-permute-done((s16[9,16,128]{2,1,0:T(8,128)(2,1)S(1)}, s16[9,16,128]{2,1,0:T(8,128)(2,1)S(1)}, u32[]{:S(2)}, u32[]{:S(2)}) %collective-permute-start.1) | collective-permute-done | bytes 36896 | tf_op jit(solution)/shard_map/ppermute | solution.py:50
  7.9 0.1 edges.1
  8.0 1.6 %collective-permute-start.4 = (s16[6,40,128]{2,1,0:T(8,128)(2,1)S(1)}, s16[6,40,128]{2,1,0:T(8,128)(2,1)S(1)}, u32[]{:S(2)}, u32[]{:S(2)}) collective-permute-start(s16[6,40,128]{2,1,0:T(8,128)(2,1)S(1)} %get-tuple-element.35), channel_id=1, source_target_pairs={{0,4},{4,0},{8,12},{12,8},{16,20},{20,16},{24,28},{28,24},{1,5},{5... | collective-permute-start | bytes 184328 | tf_op jit(solution)/shard_map/ppermute | solution.py:50
  9.6 3.6 %collective-permute-start.5 = (s16[6,40,128]{2,1,0:T(8,128)(2,1)S(1)}, s16[6,40,128]{2,1,0:T(8,128)(2,1)S(1)}, u32[]{:S(2)}, u32[]{:S(2)}) collective-permute-start(s16[6,40,128]{2,1,0:T(8,128)(2,1)S(1)} %get-tuple-element.36), channel_id=1, source_target_pairs={{0,28},{4,8},{8,4},{12,16},{16,12},{20,24},{24,20},{28,0},{1,29},{... | collective-permute-start | bytes 184328 | tf_op jit(solution)/shard_map/ppermute | solution.py:50
  13.2 3.2 %inner_sums.1 = (f32[2,40,128]{2,1,0:T(8,128)S(1)}, f32[14,40,128]{2,1,0:T(8,128)S(1)}) custom-call(f32[3,16,32,128]{3,2,1,0:T(8,128)S(1)} %get-tuple-element.29.vel_ref, s16[9,16,128]{2,1,0:T(8,128)(2,1)S(1)} %collective-permute-done.low_ref, s16[9,16,128]{2,1,0:T(8,128)(2,1)S(1)} %collective-permute-done.1.high_ref), custom_call_target="tpu_custom_call" | custom-call | bytes 18000000 | tf_op jit(solution)/shard_map/inner_sums/pallas_call | solution.py:350
  16.4 0.2 face_rows.1
  16.6 0.0 copy-start.2
  16.6 0.0 copy-start.3
  16.6 1.1 %collective-permute-start.3 = (bf16[19,16,128]{2,1,0:T(8,128)(2,1)S(1)}, bf16[19,16,128]{2,1,0:T(8,128)(2,1)S(1)}, u32[]{:S(2)}, u32[]{:S(2)}) collective-permute-start(bf16[19,16,128]{2,1,0:T(8,128)(2,1)S(1)} %get-tuple-element.34), channel_id=1, source_target_pairs={{0,3},{1,2},{2,1},{3,0},{4,7},{5,6},{6,5},{7,4},{8,11},{9,10},{10,... | collective-permute-start | bytes 233480 | tf_op jit(solution)/shard_map/ppermute | solution.py:50
  17.7 0.6 %collective-permute-start.2 = (bf16[19,16,128]{2,1,0:T(8,128)(2,1)S(1)}, bf16[19,16,128]{2,1,0:T(8,128)(2,1)S(1)}, u32[]{:S(2)}, u32[]{:S(2)}) collective-permute-start(bf16[19,16,128]{2,1,0:T(8,128)(2,1)S(1)} %get-tuple-element.33.after_this), channel_id=1, source_target_pairs={{0,1},{1,0},{2,3},{3,2},{4,5},{5,4},{6,7},{7,6},{8,9},{9,8},{10,11... | collective-permute-start | bytes 233480 | tf_op jit(solution)/shard_map/ppermute | solution.py:50
  18.3 0.0 collective-permute-done.4.first_ref
  18.3 0.0 collective-permute-done.5.second_ref
  18.4 1.4 %outer_sums.1 = (f32[72,128]{1,0:T(8,128)S(1)}, f32[8,40,128]{2,1,0:T(8,128)S(1)}) custom-call(f32[3,16,32,128]{3,2,1,0:T(8,128)S(1)} %get-tuple-element.29.vel_ref, s16[9,16,128]{2,1,0:T(8,128)(2,1)S(1)} %collective-permute-done.low_ref, s16[9,16,128]{2,1,0:T(8,128)(2,1)S(1)} %collective-permute-done.1.high_ref, ...), custom_call_target="tpu_custom_call" | custom-call | bytes 7200000 | tf_op jit(solution)/shard_map/outer_sums/pallas_call | solution.py:407
  19.8 0.1 collective-permute-start.6
  19.9 1.4 %collective-permute-done.3.second = bf16[19,16,128]{2,1,0:T(8,128)(2,1)S(1)} collective-permute-done((bf16[19,16,128]{2,1,0:T(8,128)(2,1)S(1)}, bf16[19,16,128]{2,1,0:T(8,128)(2,1)S(1)}, u32[]{:S(2)}, u32[]{:S(2)}) %collective-permute-start.3) | collective-permute-done | bytes 77856 | tf_op jit(solution)/shard_map/ppermute | solution.py:50
  21.3 0.4 leaving.1
  21.7 0.7 %collective-permute-start.9 = (s16[9,40,128]{2,1,0:T(8,128)(2,1)S(1)}, s16[9,40,128]{2,1,0:T(8,128)(2,1)S(1)}, u32[]{:S(2)}, u32[]{:S(2)}) collective-permute-start(s16[9,40,128]{2,1,0:T(8,128)(2,1)S(1)} %get-tuple-element.42), channel_id=1, source_target_pairs={{0,4},{4,0},{8,12},{12,8},{16,20},{20,16},{24,28},{28,24},{1,5},{5... | collective-permute-start | bytes 276488 | tf_op jit(solution)/shard_map/ppermute | solution.py:50
  22.3 1.7 %collective-permute-start.10 = (s16[9,40,128]{2,1,0:T(8,128)(2,1)S(1)}, s16[9,40,128]{2,1,0:T(8,128)(2,1)S(1)}, u32[]{:S(2)}, u32[]{:S(2)}) collective-permute-start(s16[9,40,128]{2,1,0:T(8,128)(2,1)S(1)} %get-tuple-element.43), channel_id=1, source_target_pairs={{0,28},{4,8},{8,4},{12,16},{16,12},{20,24},{24,20},{28,0},{1,29},{... | collective-permute-start | bytes 276488 | tf_op jit(solution)/shard_map/ppermute | solution.py:50
  24.0 1.2 %collective-permute-start.7 = (f32[72,128]{1,0:T(8,128)S(1)}, f32[72,128]{1,0:T(8,128)S(1)}, u32[]{:S(2)}, u32[]{:S(2)}) collective-permute-start(f32[72,128]{1,0:T(8,128)S(1)} %add.9.after_this), channel_id=1, source_target_pairs={{0,8},{4,12},{8,0},{12,4},{16,24},{20,28},{24,16},{28,20},{1,9},{5... | collective-permute-start | bytes 110600 | tf_op jit(solution)/shard_map/ppermute | solution.py:907
  25.3 0.6 %picks.1 = (bf16[1024,1024]{1,0:T(8,128)(2,1)S(1)}, f32[128,1024]{1,0:T(8,128)S(1)}) custom-call(s32[8,128]{1,0:T(8,128)S(1)} %bitcast.3, f32[8,128]{1,0:T(8,128)S(1)} %bitcast.4, f32[72,128]{1,0:T(8,128)S(1)} %add.9.after_this), custom_call_target="tpu_custom_call" | custom-call | bytes 2520000 | tf_op jit(solution)/shard_map/picks/pallas_call | solution.py:669
  25.9 2.5 %collective-permute-done.7 = f32[72,128]{1,0:T(8,128)S(1)} collective-permute-done((f32[72,128]{1,0:T(8,128)S(1)}, f32[72,128]{1,0:T(8,128)S(1)}, u32[]{:S(2)}, u32[]{:S(2)}) %collective-permute-start.7) | collective-permute-done | bytes 36896 | tf_op jit(solution)/shard_map/ppermute | solution.py:907
  28.4 0.4 collective-permute-start.8
  28.8 2.0 %ready.1 = (f32[19,16,32,128]{3,2,1,0:T(8,128)S(1)}, f32[5,16,32,128]{3,2,1,0:T(8,128)S(1)}, f32[2,5,16,128]{3,2,1,0:T(8,128)S(1)}, f32[2,5,16,128]{3,2,1,0:T(8,128)S(1)}) custom-call(bf16[19,16,32,128]{3,2,1,0:T(8,128)(2,1)S(1)} %copy-done.1, bf16[19,16,128]{2,1,0:T(8,128)(2,1)S(1)} %collective-permute-done.2.first, ...), custom_call_target="tpu_custom_call" | custom-call | bytes 9000000 | tf_op jit(solution)/shard_map/ready/pallas_call | solution.py:574
  30.8 2.4 %collective-permute-done.8 = f32[72,128]{1,0:T(8,128)S(1)} collective-permute-done((f32[72,128]{1,0:T(8,128)S(1)}, f32[72,128]{1,0:T(8,128)S(1)}, u32[]{:S(2)}, u32[]{:S(2)}) %collective-permute-start.8) | collective-permute-done | bytes 36896 | tf_op jit(solution)/shard_map/ppermute | solution.py:907
  33.3 3.5 %step.1 = (bf16[19,16,32,128]{3,2,1,0:T(8,128)(2,1)}, f32[32,128]{1,0:T(8,128)}, f32[32,1,128]{2,1,0:T(1,128)S(1)}) custom-call(f32[19,16,32,128]{3,2,1,0:T(8,128)S(1)} %get-tuple-element.38.base_ref, f32[5,16,32,128]{3,2,1,0:T(8,128)S(1)} %get-tuple-element.39.shear_ref, f32[2,5,16,128]{3,2,1,0:T(8,128)S(1)} %get-tuple-element.40.edge_ref, ...), custom_call_target="tpu_custom_call" | custom-call | bytes 18000000 | tf_op jit(solution)/shard_map/step/pallas_call | solution.py:845
  36.8 10.6 %all_to_all.5.arrived_ref = f32[32,1,128]{2,1,0:T(1,128)} all-to-all(f32[32,1,128]{2,1,0:T(1,128)S(1)} %get-tuple-element.54), channel_id=1, replica_groups=mesh['span'=8,'cross'=4] {'span','cross'}, dimensions={0} | all-to-all | bytes 32768 | tf_op jit(solution)/shard_map/all_to_all | solution.py:920
  47.3 1.4 %finish.1 = f32[3,8]{1,0:T(4,128)} custom-call(f32[32,1,128]{2,1,0:T(1,128)} %all_to_all.5.arrived_ref), custom_call_target="tpu_custom_call" | custom-call | tf_op jit(solution)/shard_map/finish/pallas_call | solution.py:876
  (14 shorter events, 0.0 us)
Async XLA Ops:
  0.6 1.7 %copy-start = (bf16[19,16,32,128]{3,2,1,0:T(8,128)(2,1)S(1)}, bf16[19,16,32,128]{3,2,1,0:T(8,128)(2,1)}, u32[]{:S(2)}) copy-start(bf16[19,16,32,128]{3,2,1,0:T(8,128)(2,1)} %pops.7) | copy-start | bytes 7471108
  2.3 14.1 %copy-start.1 = (bf16[19,16,32,128]{3,2,1,0:T(8,128)(2,1)S(1)}, bf16[19,16,32,128]{3,2,1,0:T(8,128)(2,1)}, u32[]{:S(2)}) copy-start(bf16[19,16,32,128]{3,2,1,0:T(8,128)(2,1)} %pops.7) | copy-start | bytes 7471108
  2.9 3.2 %collective-permute-start = (s16[9,16,128]{2,1,0:T(8,128)(2,1)S(1)}, s16[9,16,128]{2,1,0:T(8,128)(2,1)S(1)}, u32[]{:S(2)}, u32[]{:S(2)}) collective-permute-start(s16[9,16,128]{2,1,0:T(8,128)(2,1)S(1)} %get-tuple-element.30), channel_id=1, source_target_pairs={{0,1},{1,0},{2,3},{3,2},{4,5},{5,4},{6,7},{7,6},{8,9},{9,8},{10,11... | collective-permute-start | bytes 110600 | tf_op jit(solution)/shard_map/ppermute | solution.py:50
  3.5 4.4 %collective-permute-start.1 = (s16[9,16,128]{2,1,0:T(8,128)(2,1)S(1)}, s16[9,16,128]{2,1,0:T(8,128)(2,1)S(1)}, u32[]{:S(2)}, u32[]{:S(2)}) collective-permute-start(s16[9,16,128]{2,1,0:T(8,128)(2,1)S(1)} %get-tuple-element.31), channel_id=1, source_target_pairs={{0,3},{1,2},{2,1},{3,0},{4,7},{5,6},{6,5},{7,4},{8,11},{9,10},{10,... | collective-permute-start | bytes 110600 | tf_op jit(solution)/shard_map/ppermute | solution.py:50
  8.0 10.4 %collective-permute-start.4 = (s16[6,40,128]{2,1,0:T(8,128)(2,1)S(1)}, s16[6,40,128]{2,1,0:T(8,128)(2,1)S(1)}, u32[]{:S(2)}, u32[]{:S(2)}) collective-permute-start(s16[6,40,128]{2,1,0:T(8,128)(2,1)S(1)} %get-tuple-element.35), channel_id=1, source_target_pairs={{0,4},{4,0},{8,12},{12,8},{16,20},{20,16},{24,28},{28,24},{1,5},{5... | collective-permute-start | bytes 184328 | tf_op jit(solution)/shard_map/ppermute | solution.py:50
  9.6 8.8 %collective-permute-start.5 = (s16[6,40,128]{2,1,0:T(8,128)(2,1)S(1)}, s16[6,40,128]{2,1,0:T(8,128)(2,1)S(1)}, u32[]{:S(2)}, u32[]{:S(2)}) collective-permute-start(s16[6,40,128]{2,1,0:T(8,128)(2,1)S(1)} %get-tuple-element.36), channel_id=1, source_target_pairs={{0,28},{4,8},{8,4},{12,16},{16,12},{20,24},{24,20},{28,0},{1,29},{... | collective-permute-start | bytes 184328 | tf_op jit(solution)/shard_map/ppermute | solution.py:50
  16.6 8.7 %copy-start.2 = (s32[128,8]{0,1:T(8,128)S(1)}, s32[128,8]{0,1:T(8,128)}, u32[]{:S(2)}) copy-start(s32[128,8]{0,1:T(8,128)} %param.5) | copy-start | bytes 12292
  16.6 8.7 %copy-start.3 = (f32[128,8]{0,1:T(8,128)S(1)}, f32[128,8]{0,1:T(8,128)}, u32[]{:S(2)}) copy-start(f32[128,8]{0,1:T(8,128)} %param.6) | copy-start | bytes 12292
  16.6 4.6 %collective-permute-start.3 = (bf16[19,16,128]{2,1,0:T(8,128)(2,1)S(1)}, bf16[19,16,128]{2,1,0:T(8,128)(2,1)S(1)}, u32[]{:S(2)}, u32[]{:S(2)}) collective-permute-start(bf16[19,16,128]{2,1,0:T(8,128)(2,1)S(1)} %get-tuple-element.34), channel_id=1, source_target_pairs={{0,3},{1,2},{2,1},{3,0},{4,7},{5,6},{6,5},{7,4},{8,11},{9,10},{10,... | collective-permute-start | bytes 233480 | tf_op jit(solution)/shard_map/ppermute | solution.py:50
  17.7 3.6 %collective-permute-start.2 = (bf16[19,16,128]{2,1,0:T(8,128)(2,1)S(1)}, bf16[19,16,128]{2,1,0:T(8,128)(2,1)S(1)}, u32[]{:S(2)}, u32[]{:S(2)}) collective-permute-start(bf16[19,16,128]{2,1,0:T(8,128)(2,1)S(1)} %get-tuple-element.33.after_this), channel_id=1, source_target_pairs={{0,1},{1,0},{2,3},{3,2},{4,5},{5,4},{6,7},{7,6},{8,9},{9,8},{10,11... | collective-permute-start | bytes 233480 | tf_op jit(solution)/shard_map/ppermute | solution.py:50
  19.8 13.5 %copy-start.4 = (s32[128]{0:T(128)S(1)}, s32[128]{0:T(128)}, u32[]{:S(2)}) copy-start(s32[128]{0:T(128)} %param.7) | copy-start | bytes 1540
  19.8 4.2 %collective-permute-start.6 = (f32[72,128]{1,0:T(8,128)S(1)}, f32[72,128]{1,0:T(8,128)S(1)}, u32[]{:S(2)}, u32[]{:S(2)}) collective-permute-start(f32[72,128]{1,0:T(8,128)S(1)} %get-tuple-element.37.after_this), channel_id=1, source_target_pairs={{0,4},{4,0},{8,12},{12,8},{16,20},{20,16},{24,28},{28,24},{1,5},{5... | collective-permute-start | bytes 110600 | tf_op jit(solution)/shard_map/ppermute | solution.py:907
  21.7 11.6 %collective-permute-start.9 = (s16[9,40,128]{2,1,0:T(8,128)(2,1)S(1)}, s16[9,40,128]{2,1,0:T(8,128)(2,1)S(1)}, u32[]{:S(2)}, u32[]{:S(2)}) collective-permute-start(s16[9,40,128]{2,1,0:T(8,128)(2,1)S(1)} %get-tuple-element.42), channel_id=1, source_target_pairs={{0,4},{4,0},{8,12},{12,8},{16,20},{20,16},{24,28},{28,24},{1,5},{5... | collective-permute-start | bytes 276488 | tf_op jit(solution)/shard_map/ppermute | solution.py:50
  22.3 10.9 %collective-permute-start.10 = (s16[9,40,128]{2,1,0:T(8,128)(2,1)S(1)}, s16[9,40,128]{2,1,0:T(8,128)(2,1)S(1)}, u32[]{:S(2)}, u32[]{:S(2)}) collective-permute-start(s16[9,40,128]{2,1,0:T(8,128)(2,1)S(1)} %get-tuple-element.43), channel_id=1, source_target_pairs={{0,28},{4,8},{8,4},{12,16},{16,12},{20,24},{24,20},{28,0},{1,29},{... | collective-permute-start | bytes 276488 | tf_op jit(solution)/shard_map/ppermute | solution.py:50
  24.0 4.3 %collective-permute-start.7 = (f32[72,128]{1,0:T(8,128)S(1)}, f32[72,128]{1,0:T(8,128)S(1)}, u32[]{:S(2)}, u32[]{:S(2)}) collective-permute-start(f32[72,128]{1,0:T(8,128)S(1)} %add.9.after_this), channel_id=1, source_target_pairs={{0,8},{4,12},{8,0},{12,4},{16,24},{20,28},{24,16},{28,20},{1,9},{5... | collective-permute-start | bytes 110600 | tf_op jit(solution)/shard_map/ppermute | solution.py:907
  28.4 4.9 %collective-permute-start.8 = (f32[72,128]{1,0:T(8,128)S(1)}, f32[72,128]{1,0:T(8,128)S(1)}, u32[]{:S(2)}, u32[]{:S(2)}) collective-permute-start(f32[72,128]{1,0:T(8,128)S(1)} %add.10), channel_id=1, source_target_pairs={{0,16},{4,20},{8,24},{12,28},{16,0},{20,4},{24,8},{28,12},{1,17},{... | collective-permute-start | bytes 110600 | tf_op jit(solution)/shard_map/ppermute | solution.py:907

commit v5 on v4

--- a/solution.py
+++ b/solution.py
@@ -47,7 +47,7 @@
     count = lax.axis_size(axis)
     near = [(i, i ^ 1) for i in range(count)]
     other = [(i, (i + 1 if i % 2 else i - 1) % count) for i in range(count)]
-    return lax.ppermute(first, axis, near), lax.ppermute(second, axis, other)
+    return lax.ppermute(first, axis, other), lax.ppermute(second, axis, near)
 
 
 def is_odd(axis):
@@ -58,19 +58,19 @@
     odd = is_odd(axis)
 
     @pl.when(odd)
+    def _():
+        first[...] = upwards
+        second[...] = downwards
+
+    @pl.when(jnp.logical_not(odd))
     def _():
         first[...] = downwards
         second[...] = upwards
 
-    @pl.when(jnp.logical_not(odd))
-    def _():
-        first[...] = upwards
-        second[...] = downwards
-
 
 def below_above(axis, first, second):
     odd = is_odd(axis)
-    return jnp.where(odd, first, second), jnp.where(odd, second, first)
+    return jnp.where(odd, second, first), jnp.where(odd, first, second)
 
 
 def full(shape, dtype):

time: 49 us -> 49 us (level)
  starting transfers between devices: 14.2 us -> 16.3 us
  waiting for transfers between devices: 8.12 us -> 6.3 us
    ppermute x3, starting transfers between devices: 1.75 us -> 4.78 us  [local(): other = lax.ppermute(sums, 'span', pairs)]
    ppermute x8, waiting for transfers between devices: 3.19 us -> 1.22 us  [swap(): return (lax.ppermute(first, axis, other), lax.ppermute(second, axis, near))]
    ppermute x8, starting transfers between devices: 12.4 us -> 11.5 us  [swap(): return (lax.ppermute(first, axis, other), lax.ppermute(second, axis, near))]
where the time goes in v5:
time: 49 us; the launch traced here: 48.7 us
  starting transfers between devices  16.3 us (33%)
  Pallas kernels  13.4 us (27%)
  blocking collectives  10.3 us (21%)
  waiting for transfers between devices  6.3 us (13%)
  local copies, waits for them, and re-layouts  1.72 us (4%)
  between operations  0.76 us (2%)
    ppermute x8, starting transfers between devices, swap(): return (lax.ppermute(first, axis, other), lax.ppermute(second, axis, near))  11.5 us
    all_to_all x1, blocking collectives, local(): arrived = lax.all_to_all(packed, ('span', 'cross'), 0, 0)  10.3 us
    ppermute x3, waiting for transfers between devices, local(): other = lax.ppermute(sums, 'span', pairs)  5.08 us
    ppermute x3, starting transfers between devices, local(): other = lax.ppermute(sums, 'span', pairs)  4.78 us
    pallas_call x1, Pallas kernels, step(): pl.pallas_call(step_kernel, out_shape=(full((19, depth, width, lanes), jn...  3.49 us
    pallas_call x1, Pallas kernels, inner_sums(): pl.pallas_call(inner_kernel, out_shape=(full((2, EXT, LANES), jnp.float32...  3.23 us
    pallas_call x1, Pallas kernels, ready(): pl.pallas_call(ready_kernel, out_shape=(full((19, depth, width, lanes), j...  1.98 us
    unnamed x10, local copies, waits for them, and re-layouts  1.72 us
  transfers between devices with their start and end apart: 11, of which 4 were waited for; matrix products, arithmetic and copies ran while one was open for 0% of the time, Pallas kernels for 16%

profile of v5, /device:TPU:0, one launch (start us, length us, event | category | flops | bytes accessed | tf_op | source)
XLA Modules:
  0.0 48.7 jit_solution(6438571063764228914)
XLA Ops:
  0.6 1.7 %copy-done = bf16[19,16,32,128]{3,2,1,0:T(8,128)(2,1)S(1)} copy-done((bf16[19,16,32,128]{3,2,1,0:T(8,128)(2,1)S(1)}, bf16[19,16,32,128]{3,2,1,0:T(8,128)(2,1)}, u32[]{:S(2)}) %copy-start) | copy-done | bytes 2490392
  2.3 0.6 %moments.1 = (f32[3,16,32,128]{3,2,1,0:T(8,128)S(1)}, s16[9,16,128]{2,1,0:T(8,128)(2,1)S(1)}, s16[9,16,128]{2,1,0:T(8,128)(2,1)S(1)}) custom-call(bf16[19,16,32,128]{3,2,1,0:T(8,128)(2,1)S(1)} %copy-done), custom_call_target="tpu_custom_call" | custom-call | bytes 3600000 | tf_op jit(solution)/shard_map/moments/pallas_call | solution.py:164
  2.9 2.5 %collective-permute-start = (s16[9,16,128]{2,1,0:T(8,128)(2,1)S(1)}, s16[9,16,128]{2,1,0:T(8,128)(2,1)S(1)}, u32[]{:S(2)}, u32[]{:S(2)}) collective-permute-start(s16[9,16,128]{2,1,0:T(8,128)(2,1)S(1)} %get-tuple-element.30), channel_id=1, source_target_pairs={{0,3},{1,2},{2,1},{3,0},{4,7},{5,6},{6,5},{7,4},{8,11},{9,10},{10,... | collective-permute-start | bytes 110600 | tf_op jit(solution)/shard_map/ppermute | solution.py:50
  5.4 0.7 %collective-permute-start.1 = (s16[9,16,128]{2,1,0:T(8,128)(2,1)S(1)}, s16[9,16,128]{2,1,0:T(8,128)(2,1)S(1)}, u32[]{:S(2)}, u32[]{:S(2)}) collective-permute-start(s16[9,16,128]{2,1,0:T(8,128)(2,1)S(1)} %get-tuple-element.31), channel_id=1, source_target_pairs={{0,1},{1,0},{2,3},{3,2},{4,5},{5,4},{6,7},{7,6},{8,9},{9,8},{10,11... | collective-permute-start | bytes 110600 | tf_op jit(solution)/shard_map/ppermute | solution.py:50
  6.1 1.2 %collective-permute-done.low_ref = s16[9,16,128]{2,1,0:T(8,128)(2,1)S(1)} collective-permute-done((s16[9,16,128]{2,1,0:T(8,128)(2,1)S(1)}, s16[9,16,128]{2,1,0:T(8,128)(2,1)S(1)}, u32[]{:S(2)}, u32[]{:S(2)}) %collective-permute-start) | collective-permute-done | bytes 36896 | tf_op jit(solution)/shard_map/ppermute | solution.py:50
  7.3 0.0 collective-permute-done.1.high_ref
  7.3 0.1 edges.1
  7.4 5.5 %collective-permute-start.4 = (s16[6,40,128]{2,1,0:T(8,128)(2,1)S(1)}, s16[6,40,128]{2,1,0:T(8,128)(2,1)S(1)}, u32[]{:S(2)}, u32[]{:S(2)}) collective-permute-start(s16[6,40,128]{2,1,0:T(8,128)(2,1)S(1)} %get-tuple-element.35), channel_id=1, source_target_pairs={{0,28},{4,8},{8,4},{12,16},{16,12},{20,24},{24,20},{28,0},{1,29},{... | collective-permute-start | bytes 184328 | tf_op jit(solution)/shard_map/ppermute | solution.py:50
  12.9 3.2 %inner_sums.1 = (f32[2,40,128]{2,1,0:T(8,128)S(1)}, f32[14,40,128]{2,1,0:T(8,128)S(1)}) custom-call(f32[3,16,32,128]{3,2,1,0:T(8,128)S(1)} %get-tuple-element.29.vel_ref, s16[9,16,128]{2,1,0:T(8,128)(2,1)S(1)} %collective-permute-done.low_ref, s16[9,16,128]{2,1,0:T(8,128)(2,1)S(1)} %collective-permute-done.1.high_ref), custom_call_target="tpu_custom_call" | custom-call | bytes 18000000 | tf_op jit(solution)/shard_map/inner_sums/pallas_call | solution.py:350
  16.1 0.2 face_rows.1
  16.3 0.0 copy-start.2
  16.3 0.0 copy-start.3
  16.4 0.1 collective-permute-start.3
  16.4 1.7 %collective-permute-start.2 = (bf16[19,16,128]{2,1,0:T(8,128)(2,1)S(1)}, bf16[19,16,128]{2,1,0:T(8,128)(2,1)S(1)}, u32[]{:S(2)}, u32[]{:S(2)}) collective-permute-start(bf16[19,16,128]{2,1,0:T(8,128)(2,1)S(1)} %get-tuple-element.33.after_this), channel_id=1, source_target_pairs={{0,3},{1,2},{2,1},{3,0},{4,7},{5,6},{6,5},{7,4},{8,11},{9,10},{10,... | collective-permute-start | bytes 233480 | tf_op jit(solution)/shard_map/ppermute | solution.py:50
  18.1 0.0 collective-permute-done.5.second_ref
  18.1 1.4 %outer_sums.1 = (f32[72,128]{1,0:T(8,128)S(1)}, f32[8,40,128]{2,1,0:T(8,128)S(1)}) custom-call(f32[3,16,32,128]{3,2,1,0:T(8,128)S(1)} %get-tuple-element.29.vel_ref, s16[9,16,128]{2,1,0:T(8,128)(2,1)S(1)} %collective-permute-done.low_ref, s16[9,16,128]{2,1,0:T(8,128)(2,1)S(1)} %collective-permute-done.1.high_ref, ...), custom_call_target="tpu_custom_call" | custom-call | bytes 7200000 | tf_op jit(solution)/shard_map/outer_sums/pallas_call | solution.py:407
  19.6 2.1 %collective-permute-start.6 = (f32[72,128]{1,0:T(8,128)S(1)}, f32[72,128]{1,0:T(8,128)S(1)}, u32[]{:S(2)}, u32[]{:S(2)}) collective-permute-start(f32[72,128]{1,0:T(8,128)S(1)} %get-tuple-element.37.after_this), channel_id=1, source_target_pairs={{0,4},{4,0},{8,12},{12,8},{16,20},{20,16},{24,28},{28,24},{1,5},{5... | collective-permute-start | bytes 110600 | tf_op jit(solution)/shard_map/ppermute | solution.py:907
  21.7 0.0 collective-permute-done.3.second
  21.7 0.0 collective-permute-done.2.first
  21.7 0.4 leaving.1
  22.0 0.9 %collective-permute-start.9 = (s16[9,40,128]{2,1,0:T(8,128)(2,1)S(1)}, s16[9,40,128]{2,1,0:T(8,128)(2,1)S(1)}, u32[]{:S(2)}, u32[]{:S(2)}) collective-permute-start(s16[9,40,128]{2,1,0:T(8,128)(2,1)S(1)} %get-tuple-element.42), channel_id=1, source_target_pairs={{0,28},{4,8},{8,4},{12,16},{16,12},{20,24},{24,20},{28,0},{1,29},{... | collective-permute-start | bytes 276488 | tf_op jit(solution)/shard_map/ppermute | solution.py:50
  23.0 0.2 collective-permute-start.10
  23.2 0.4 collective-permute-done.6
  23.6 1.0 %collective-permute-start.7 = (f32[72,128]{1,0:T(8,128)S(1)}, f32[72,128]{1,0:T(8,128)S(1)}, u32[]{:S(2)}, u32[]{:S(2)}) collective-permute-start(f32[72,128]{1,0:T(8,128)S(1)} %add.9.after_this), channel_id=1, source_target_pairs={{0,8},{4,12},{8,0},{12,4},{16,24},{20,28},{24,16},{28,20},{1,9},{5... | collective-permute-start | bytes 110600 | tf_op jit(solution)/shard_map/ppermute | solution.py:907
  24.6 0.6 %picks.1 = (bf16[1024,1024]{1,0:T(8,128)(2,1)S(1)}, f32[128,1024]{1,0:T(8,128)S(1)}) custom-call(s32[8,128]{1,0:T(8,128)S(1)} %bitcast.3, f32[8,128]{1,0:T(8,128)S(1)} %bitcast.4, f32[72,128]{1,0:T(8,128)S(1)} %add.9.after_this), custom_call_target="tpu_custom_call" | custom-call | bytes 2520000 | tf_op jit(solution)/shard_map/picks/pallas_call | solution.py:669
  25.2 3.1 %collective-permute-done.7 = f32[72,128]{1,0:T(8,128)S(1)} collective-permute-done((f32[72,128]{1,0:T(8,128)S(1)}, f32[72,128]{1,0:T(8,128)S(1)}, u32[]{:S(2)}, u32[]{:S(2)}) %collective-permute-start.7) | collective-permute-done | bytes 36896 | tf_op jit(solution)/shard_map/ppermute | solution.py:907
  28.3 1.7 %collective-permute-start.8 = (f32[72,128]{1,0:T(8,128)S(1)}, f32[72,128]{1,0:T(8,128)S(1)}, u32[]{:S(2)}, u32[]{:S(2)}) collective-permute-start(f32[72,128]{1,0:T(8,128)S(1)} %add.10), channel_id=1, source_target_pairs={{0,16},{4,20},{8,24},{12,28},{16,0},{20,4},{24,8},{28,12},{1,17},{... | collective-permute-start | bytes 110600 | tf_op jit(solution)/shard_map/ppermute | solution.py:907
  30.0 2.0 %ready.1 = (f32[19,16,32,128]{3,2,1,0:T(8,128)S(1)}, f32[5,16,32,128]{3,2,1,0:T(8,128)S(1)}, f32[2,5,16,128]{3,2,1,0:T(8,128)S(1)}, f32[2,5,16,128]{3,2,1,0:T(8,128)S(1)}) custom-call(bf16[19,16,32,128]{3,2,1,0:T(8,128)(2,1)S(1)} %copy-done.1, bf16[19,16,128]{2,1,0:T(8,128)(2,1)S(1)} %collective-permute-done.2.first, ...), custom_call_target="tpu_custom_call" | custom-call | bytes 9000000 | tf_op jit(solution)/shard_map/ready/pallas_call | solution.py:574
  32.0 1.6 %collective-permute-done.8 = f32[72,128]{1,0:T(8,128)S(1)} collective-permute-done((f32[72,128]{1,0:T(8,128)S(1)}, f32[72,128]{1,0:T(8,128)S(1)}, u32[]{:S(2)}, u32[]{:S(2)}) %collective-permute-start.8) | collective-permute-done | bytes 36896 | tf_op jit(solution)/shard_map/ppermute | solution.py:907
  33.6 3.5 %step.1 = (bf16[19,16,32,128]{3,2,1,0:T(8,128)(2,1)}, f32[32,128]{1,0:T(8,128)}, f32[32,1,128]{2,1,0:T(1,128)S(1)}) custom-call(f32[19,16,32,128]{3,2,1,0:T(8,128)S(1)} %get-tuple-element.38.base_ref, f32[5,16,32,128]{3,2,1,0:T(8,128)S(1)} %get-tuple-element.39.shear_ref, f32[2,5,16,128]{3,2,1,0:T(8,128)S(1)} %get-tuple-element.40.edge_ref, ...), custom_call_target="tpu_custom_call" | custom-call | bytes 18000000 | tf_op jit(solution)/shard_map/step/pallas_call | solution.py:845
  37.1 10.3 %all_to_all.5.arrived_ref = f32[32,1,128]{2,1,0:T(1,128)} all-to-all(f32[32,1,128]{2,1,0:T(1,128)S(1)} %get-tuple-element.54), channel_id=1, replica_groups=mesh['span'=8,'cross'=4] {'span','cross'}, dimensions={0} | all-to-all | bytes 32768 | tf_op jit(solution)/shard_map/all_to_all | solution.py:920
  47.4 1.4 %finish.1 = f32[3,8]{1,0:T(4,128)} custom-call(f32[32,1,128]{2,1,0:T(1,128)} %all_to_all.5.arrived_ref), custom_call_target="tpu_custom_call" | custom-call | tf_op jit(solution)/shard_map/finish/pallas_call | solution.py:876
  (14 shorter events, 0.0 us)
Async XLA Ops:
  0.6 1.7 %copy-start = (bf16[19,16,32,128]{3,2,1,0:T(8,128)(2,1)S(1)}, bf16[19,16,32,128]{3,2,1,0:T(8,128)(2,1)}, u32[]{:S(2)}) copy-start(bf16[19,16,32,128]{3,2,1,0:T(8,128)(2,1)} %pops.7) | copy-start | bytes 7471108
  2.3 13.8 %copy-start.1 = (bf16[19,16,32,128]{3,2,1,0:T(8,128)(2,1)S(1)}, bf16[19,16,32,128]{3,2,1,0:T(8,128)(2,1)}, u32[]{:S(2)}) copy-start(bf16[19,16,32,128]{3,2,1,0:T(8,128)(2,1)} %pops.7) | copy-start | bytes 7471108
  2.9 4.3 %collective-permute-start = (s16[9,16,128]{2,1,0:T(8,128)(2,1)S(1)}, s16[9,16,128]{2,1,0:T(8,128)(2,1)S(1)}, u32[]{:S(2)}, u32[]{:S(2)}) collective-permute-start(s16[9,16,128]{2,1,0:T(8,128)(2,1)S(1)} %get-tuple-element.30), channel_id=1, source_target_pairs={{0,3},{1,2},{2,1},{3,0},{4,7},{5,6},{6,5},{7,4},{8,11},{9,10},{10,... | collective-permute-start | bytes 110600 | tf_op jit(solution)/shard_map/ppermute | solution.py:50
  5.4 1.9 %collective-permute-start.1 = (s16[9,16,128]{2,1,0:T(8,128)(2,1)S(1)}, s16[9,16,128]{2,1,0:T(8,128)(2,1)S(1)}, u32[]{:S(2)}, u32[]{:S(2)}) collective-permute-start(s16[9,16,128]{2,1,0:T(8,128)(2,1)S(1)} %get-tuple-element.31), channel_id=1, source_target_pairs={{0,1},{1,0},{2,3},{3,2},{4,5},{5,4},{6,7},{7,6},{8,9},{9,8},{10,11... | collective-permute-start | bytes 110600 | tf_op jit(solution)/shard_map/ppermute | solution.py:50
  7.4 10.7 %collective-permute-start.4 = (s16[6,40,128]{2,1,0:T(8,128)(2,1)S(1)}, s16[6,40,128]{2,1,0:T(8,128)(2,1)S(1)}, u32[]{:S(2)}, u32[]{:S(2)}) collective-permute-start(s16[6,40,128]{2,1,0:T(8,128)(2,1)S(1)} %get-tuple-element.35), channel_id=1, source_target_pairs={{0,28},{4,8},{8,4},{12,16},{16,12},{20,24},{24,20},{28,0},{1,29},{... | collective-permute-start | bytes 184328 | tf_op jit(solution)/shard_map/ppermute | solution.py:50
  12.9 5.3 %collective-permute-start.5 = (s16[6,40,128]{2,1,0:T(8,128)(2,1)S(1)}, s16[6,40,128]{2,1,0:T(8,128)(2,1)S(1)}, u32[]{:S(2)}, u32[]{:S(2)}) collective-permute-start(s16[6,40,128]{2,1,0:T(8,128)(2,1)S(1)} %get-tuple-element.36), channel_id=1, source_target_pairs={{0,4},{4,0},{8,12},{12,8},{16,20},{20,16},{24,28},{28,24},{1,5},{5... | collective-permute-start | bytes 184328 | tf_op jit(solution)/shard_map/ppermute | solution.py:50
  16.3 8.3 %copy-start.2 = (s32[128,8]{0,1:T(8,128)S(1)}, s32[128,8]{0,1:T(8,128)}, u32[]{:S(2)}) copy-start(s32[128,8]{0,1:T(8,128)} %param.5) | copy-start | bytes 12292
  16.3 8.3 %copy-start.3 = (f32[128,8]{0,1:T(8,128)S(1)}, f32[128,8]{0,1:T(8,128)}, u32[]{:S(2)}) copy-start(f32[128,8]{0,1:T(8,128)} %param.6) | copy-start | bytes 12292
  16.4 5.3 %collective-permute-start.3 = (bf16[19,16,128]{2,1,0:T(8,128)(2,1)S(1)}, bf16[19,16,128]{2,1,0:T(8,128)(2,1)S(1)}, u32[]{:S(2)}, u32[]{:S(2)}) collective-permute-start(bf16[19,16,128]{2,1,0:T(8,128)(2,1)S(1)} %get-tuple-element.34), channel_id=1, source_target_pairs={{0,1},{1,0},{2,3},{3,2},{4,5},{5,4},{6,7},{7,6},{8,9},{9,8},{10,11... | collective-permute-start | bytes 233480 | tf_op jit(solution)/shard_map/ppermute | solution.py:50
  16.4 5.2 %collective-permute-start.2 = (bf16[19,16,128]{2,1,0:T(8,128)(2,1)S(1)}, bf16[19,16,128]{2,1,0:T(8,128)(2,1)S(1)}, u32[]{:S(2)}, u32[]{:S(2)}) collective-permute-start(bf16[19,16,128]{2,1,0:T(8,128)(2,1)S(1)} %get-tuple-element.33.after_this), channel_id=1, source_target_pairs={{0,3},{1,2},{2,1},{3,0},{4,7},{5,6},{6,5},{7,4},{8,11},{9,10},{10,... | collective-permute-start | bytes 233480 | tf_op jit(solution)/shard_map/ppermute | solution.py:50
  19.6 14.0 %copy-start.4 = (s32[128]{0:T(128)S(1)}, s32[128]{0:T(128)}, u32[]{:S(2)}) copy-start(s32[128]{0:T(128)} %param.7) | copy-start | bytes 1540
  19.6 4.0 %collective-permute-start.6 = (f32[72,128]{1,0:T(8,128)S(1)}, f32[72,128]{1,0:T(8,128)S(1)}, u32[]{:S(2)}, u32[]{:S(2)}) collective-permute-start(f32[72,128]{1,0:T(8,128)S(1)} %get-tuple-element.37.after_this), channel_id=1, source_target_pairs={{0,4},{4,0},{8,12},{12,8},{16,20},{20,16},{24,28},{28,24},{1,5},{5... | collective-permute-start | bytes 110600 | tf_op jit(solution)/shard_map/ppermute | solution.py:907
  22.0 11.5 %collective-permute-start.9 = (s16[9,40,128]{2,1,0:T(8,128)(2,1)S(1)}, s16[9,40,128]{2,1,0:T(8,128)(2,1)S(1)}, u32[]{:S(2)}, u32[]{:S(2)}) collective-permute-start(s16[9,40,128]{2,1,0:T(8,128)(2,1)S(1)} %get-tuple-element.42), channel_id=1, source_target_pairs={{0,28},{4,8},{8,4},{12,16},{16,12},{20,24},{24,20},{28,0},{1,29},{... | collective-permute-start | bytes 276488 | tf_op jit(solution)/shard_map/ppermute | solution.py:50
  23.0 10.6 %collective-permute-start.10 = (s16[9,40,128]{2,1,0:T(8,128)(2,1)S(1)}, s16[9,40,128]{2,1,0:T(8,128)(2,1)S(1)}, u32[]{:S(2)}, u32[]{:S(2)}) collective-permute-start(s16[9,40,128]{2,1,0:T(8,128)(2,1)S(1)} %get-tuple-element.43), channel_id=1, source_target_pairs={{0,4},{4,0},{8,12},{12,8},{16,20},{20,16},{24,28},{28,24},{1,5},{5... | collective-permute-start | bytes 276488 | tf_op jit(solution)/shard_map/ppermute | solution.py:50
  23.6 4.7 %collective-permute-start.7 = (f32[72,128]{1,0:T(8,128)S(1)}, f32[72,128]{1,0:T(8,128)S(1)}, u32[]{:S(2)}, u32[]{:S(2)}) collective-permute-start(f32[72,128]{1,0:T(8,128)S(1)} %add.9.after_this), channel_id=1, source_target_pairs={{0,8},{4,12},{8,0},{12,4},{16,24},{20,28},{24,16},{28,20},{1,9},{5... | collective-permute-start | bytes 110600 | tf_op jit(solution)/shard_map/ppermute | solution.py:907
  28.3 5.3 %collective-permute-start.8 = (f32[72,128]{1,0:T(8,128)S(1)}, f32[72,128]{1,0:T(8,128)S(1)}, u32[]{:S(2)}, u32[]{:S(2)}) collective-permute-start(f32[72,128]{1,0:T(8,128)S(1)} %add.10), channel_id=1, source_target_pairs={{0,16},{4,20},{8,24},{12,28},{16,0},{20,4},{24,8},{28,12},{1,17},{... | collective-permute-start | bytes 110600 | tf_op jit(solution)/shard_map/ppermute | solution.py:907

commit v6 on v4

--- a/solution.py
+++ b/solution.py
@@ -866,22 +866,6 @@
     )(*parts, sums, mag_in, mag_out, *picks, segments, *messages)
 
 
-def finish_kernel(arrived_ref, out_ref):
-    total = jnp.sum(arrived_ref[:, 0, :], axis=0, keepdims=True)
-    for dim in range(3):
-        out_ref[pl.ds(dim, 1), :] = total[:, dim * SEG_DEV : (dim + 1) * SEG_DEV]
-
-
-def finish(arrived):
-    return pl.pallas_call(
-        finish_kernel,
-        out_shape=full((3, SEG_DEV), jnp.float32),
-        in_specs=in_vmem(1),
-        out_specs=in_vmem(1)[0],
-        name="finish",
-    )(arrived)
-
-
 def local(populations, cell_index, marker_weight, segment_id):
     owners = lax.axis_size("span") * lax.axis_size("cross")
     cells, weights, segments = cell_index.T, marker_weight.T, segment_id[None, :]
@@ -918,7 +902,8 @@
         parts, sums, mag_in, mag_out, picks, segments, arriving, owners
     )
     arrived = lax.all_to_all(packed, ("span", "cross"), 0, 0)
-    return (populations_next, eddy_coeff, finish(arrived))
+    forces = jnp.sum(arrived, axis=(0, 1))[: 3 * SEG_DEV].reshape(3, SEG_DEV)
+    return (populations_next, eddy_coeff, forces)
 
 
 def solution(mesh):

time: 49 us -> 48.1 us (0.982)
  Pallas kernels: 13.4 us -> 12 us
  local copies, waits for them, and re-layouts: 1.72 us -> 2.38 us
    pallas_call x1 -> x0, Pallas kernels: 1.38 us -> none  [finish(): pl.pallas_call(finish_kernel, out_shape=full((3, SEG_DEV), jnp.float32),...]
    reshape x0 -> x1, local copies, waits for them, and re-layouts: none -> 0.66 us  [local(): forces = jnp.sum(arrived, axis=(0, 1))[:3 * SEG_DEV].reshape(3, SEG_DEV)]
where the time goes in v6:
time: 48.1 us; the launch traced here: 47.9 us
  starting transfers between devices  14.2 us (30%)
  Pallas kernels  12 us (25%)
  blocking collectives  10.5 us (22%)
  waiting for transfers between devices  8.12 us (17%)
  local copies, waits for them, and re-layouts  2.38 us (5%)
  between operations  0.77 us (2%)
    ppermute x8, starting transfers between devices, swap(): return (lax.ppermute(first, axis, near), lax.ppermute(second, axis, other))  12.4 us
    all_to_all x1, blocking collectives, local(): arrived = lax.all_to_all(packed, ('span', 'cross'), 0, 0)  10.5 us
    ppermute x3, waiting for transfers between devices, local(): other = lax.ppermute(sums, 'span', pairs)  4.93 us
    pallas_call x1, Pallas kernels, step(): pl.pallas_call(step_kernel, out_shape=(full((19, depth, width, lanes), jn...  3.48 us
    pallas_call x1, Pallas kernels, inner_sums(): pl.pallas_call(inner_kernel, out_shape=(full((2, EXT, LANES), jnp.float32...  3.23 us
    ppermute x8, waiting for transfers between devices, swap(): return (lax.ppermute(first, axis, near), lax.ppermute(second, axis, other))  3.19 us
    pallas_call x1, Pallas kernels, ready(): pl.pallas_call(ready_kernel, out_shape=(full((19, depth, width, lanes), j...  1.98 us
    ppermute x3, starting transfers between devices, local(): other = lax.ppermute(sums, 'span', pairs)  1.75 us
  transfers between devices with their start and end apart: 11, of which 4 were waited for; matrix products, arithmetic and copies ran while one was open for 0% of the time, Pallas kernels for 16%

profile of v6, /device:TPU:0, one launch (start us, length us, event | category | flops | bytes accessed | tf_op | source)
XLA Modules:
  0.0 47.9 jit_solution(14622582197265129499)
XLA Ops:
  0.6 1.7 %copy-done = bf16[19,16,32,128]{3,2,1,0:T(8,128)(2,1)S(1)} copy-done((bf16[19,16,32,128]{3,2,1,0:T(8,128)(2,1)S(1)}, bf16[19,16,32,128]{3,2,1,0:T(8,128)(2,1)}, u32[]{:S(2)}) %copy-start) | copy-done | bytes 2490392
  2.3 0.6 %moments.1 = (f32[3,16,32,128]{3,2,1,0:T(8,128)S(1)}, s16[9,16,128]{2,1,0:T(8,128)(2,1)S(1)}, s16[9,16,128]{2,1,0:T(8,128)(2,1)S(1)}) custom-call(bf16[19,16,32,128]{3,2,1,0:T(8,128)(2,1)S(1)} %copy-done), custom_call_target="tpu_custom_call" | custom-call | bytes 3600000 | tf_op jit(solution)/shard_map/moments/pallas_call | solution.py:164
  2.9 0.5 %collective-permute-start = (s16[9,16,128]{2,1,0:T(8,128)(2,1)S(1)}, s16[9,16,128]{2,1,0:T(8,128)(2,1)S(1)}, u32[]{:S(2)}, u32[]{:S(2)}) collective-permute-start(s16[9,16,128]{2,1,0:T(8,128)(2,1)S(1)} %get-tuple-element.30), channel_id=1, source_target_pairs={{0,1},{1,0},{2,3},{3,2},{4,5},{5,4},{6,7},{7,6},{8,9},{9,8},{10,11... | collective-permute-start | bytes 110600 | tf_op jit(solution)/shard_map/ppermute | solution.py:50
  3.5 2.6 %collective-permute-start.1 = (s16[9,16,128]{2,1,0:T(8,128)(2,1)S(1)}, s16[9,16,128]{2,1,0:T(8,128)(2,1)S(1)}, u32[]{:S(2)}, u32[]{:S(2)}) collective-permute-start(s16[9,16,128]{2,1,0:T(8,128)(2,1)S(1)} %get-tuple-element.31), channel_id=1, source_target_pairs={{0,3},{1,2},{2,1},{3,0},{4,7},{5,6},{6,5},{7,4},{8,11},{9,10},{10,... | collective-permute-start | bytes 110600 | tf_op jit(solution)/shard_map/ppermute | solution.py:50
  6.1 0.0 collective-permute-done.low_ref
  6.1 1.8 %collective-permute-done.1.high_ref = s16[9,16,128]{2,1,0:T(8,128)(2,1)S(1)} collective-permute-done((s16[9,16,128]{2,1,0:T(8,128)(2,1)S(1)}, s16[9,16,128]{2,1,0:T(8,128)(2,1)S(1)}, u32[]{:S(2)}, u32[]{:S(2)}) %collective-permute-start.1) | collective-permute-done | bytes 36896 | tf_op jit(solution)/shard_map/ppermute | solution.py:50
  7.9 0.1 edges.1
  8.0 1.6 %collective-permute-start.4 = (s16[6,40,128]{2,1,0:T(8,128)(2,1)S(1)}, s16[6,40,128]{2,1,0:T(8,128)(2,1)S(1)}, u32[]{:S(2)}, u32[]{:S(2)}) collective-permute-start(s16[6,40,128]{2,1,0:T(8,128)(2,1)S(1)} %get-tuple-element.35), channel_id=1, source_target_pairs={{0,4},{4,0},{8,12},{12,8},{16,20},{20,16},{24,28},{28,24},{1,5},{5... | collective-permute-start | bytes 184328 | tf_op jit(solution)/shard_map/ppermute | solution.py:50
  9.6 3.6 %collective-permute-start.5 = (s16[6,40,128]{2,1,0:T(8,128)(2,1)S(1)}, s16[6,40,128]{2,1,0:T(8,128)(2,1)S(1)}, u32[]{:S(2)}, u32[]{:S(2)}) collective-permute-start(s16[6,40,128]{2,1,0:T(8,128)(2,1)S(1)} %get-tuple-element.36), channel_id=1, source_target_pairs={{0,28},{4,8},{8,4},{12,16},{16,12},{20,24},{24,20},{28,0},{1,29},{... | collective-permute-start | bytes 184328 | tf_op jit(solution)/shard_map/ppermute | solution.py:50
  13.2 3.2 %inner_sums.1 = (f32[2,40,128]{2,1,0:T(8,128)S(1)}, f32[14,40,128]{2,1,0:T(8,128)S(1)}) custom-call(f32[3,16,32,128]{3,2,1,0:T(8,128)S(1)} %get-tuple-element.29.vel_ref, s16[9,16,128]{2,1,0:T(8,128)(2,1)S(1)} %collective-permute-done.low_ref, s16[9,16,128]{2,1,0:T(8,128)(2,1)S(1)} %collective-permute-done.1.high_ref), custom_call_target="tpu_custom_call" | custom-call | bytes 18000000 | tf_op jit(solution)/shard_map/inner_sums/pallas_call | solution.py:350
  16.4 0.2 face_rows.1
  16.6 0.0 copy-start.2
  16.6 0.0 copy-start.3
  16.6 1.1 %collective-permute-start.3 = (bf16[19,16,128]{2,1,0:T(8,128)(2,1)S(1)}, bf16[19,16,128]{2,1,0:T(8,128)(2,1)S(1)}, u32[]{:S(2)}, u32[]{:S(2)}) collective-permute-start(bf16[19,16,128]{2,1,0:T(8,128)(2,1)S(1)} %get-tuple-element.34), channel_id=1, source_target_pairs={{0,3},{1,2},{2,1},{3,0},{4,7},{5,6},{6,5},{7,4},{8,11},{9,10},{10,... | collective-permute-start | bytes 233480 | tf_op jit(solution)/shard_map/ppermute | solution.py:50
  17.7 0.6 %collective-permute-start.2 = (bf16[19,16,128]{2,1,0:T(8,128)(2,1)S(1)}, bf16[19,16,128]{2,1,0:T(8,128)(2,1)S(1)}, u32[]{:S(2)}, u32[]{:S(2)}) collective-permute-start(bf16[19,16,128]{2,1,0:T(8,128)(2,1)S(1)} %get-tuple-element.33.after_this), channel_id=1, source_target_pairs={{0,1},{1,0},{2,3},{3,2},{4,5},{5,4},{6,7},{7,6},{8,9},{9,8},{10,11... | collective-permute-start | bytes 233480 | tf_op jit(solution)/shard_map/ppermute | solution.py:50
  18.3 0.0 collective-permute-done.4.first_ref
  18.4 1.4 %outer_sums.1 = (f32[72,128]{1,0:T(8,128)S(1)}, f32[8,40,128]{2,1,0:T(8,128)S(1)}) custom-call(f32[3,16,32,128]{3,2,1,0:T(8,128)S(1)} %get-tuple-element.29.vel_ref, s16[9,16,128]{2,1,0:T(8,128)(2,1)S(1)} %collective-permute-done.low_ref, s16[9,16,128]{2,1,0:T(8,128)(2,1)S(1)} %collective-permute-done.1.high_ref, ...), custom_call_target="tpu_custom_call" | custom-call | bytes 7200000 | tf_op jit(solution)/shard_map/outer_sums/pallas_call | solution.py:407
  19.8 0.1 collective-permute-start.6
  19.9 1.4 %collective-permute-done.3.second = bf16[19,16,128]{2,1,0:T(8,128)(2,1)S(1)} collective-permute-done((bf16[19,16,128]{2,1,0:T(8,128)(2,1)S(1)}, bf16[19,16,128]{2,1,0:T(8,128)(2,1)S(1)}, u32[]{:S(2)}, u32[]{:S(2)}) %collective-permute-start.3) | collective-permute-done | bytes 77856 | tf_op jit(solution)/shard_map/ppermute | solution.py:50
  21.3 0.4 leaving.1
  21.7 0.7 %collective-permute-start.9 = (s16[9,40,128]{2,1,0:T(8,128)(2,1)S(1)}, s16[9,40,128]{2,1,0:T(8,128)(2,1)S(1)}, u32[]{:S(2)}, u32[]{:S(2)}) collective-permute-start(s16[9,40,128]{2,1,0:T(8,128)(2,1)S(1)} %get-tuple-element.42), channel_id=1, source_target_pairs={{0,4},{4,0},{8,12},{12,8},{16,20},{20,16},{24,28},{28,24},{1,5},{5... | collective-permute-start | bytes 276488 | tf_op jit(solution)/shard_map/ppermute | solution.py:50
  22.3 1.7 %collective-permute-start.10 = (s16[9,40,128]{2,1,0:T(8,128)(2,1)S(1)}, s16[9,40,128]{2,1,0:T(8,128)(2,1)S(1)}, u32[]{:S(2)}, u32[]{:S(2)}) collective-permute-start(s16[9,40,128]{2,1,0:T(8,128)(2,1)S(1)} %get-tuple-element.43), channel_id=1, source_target_pairs={{0,28},{4,8},{8,4},{12,16},{16,12},{20,24},{24,20},{28,0},{1,29},{... | collective-permute-start | bytes 276488 | tf_op jit(solution)/shard_map/ppermute | solution.py:50
  24.0 1.2 %collective-permute-start.7 = (f32[72,128]{1,0:T(8,128)S(1)}, f32[72,128]{1,0:T(8,128)S(1)}, u32[]{:S(2)}, u32[]{:S(2)}) collective-permute-start(f32[72,128]{1,0:T(8,128)S(1)} %add.9.after_this), channel_id=1, source_target_pairs={{0,8},{4,12},{8,0},{12,4},{16,24},{20,28},{24,16},{28,20},{1,9},{5... | collective-permute-start | bytes 110600 | tf_op jit(solution)/shard_map/ppermute | solution.py:891
  25.3 0.6 %picks.1 = (bf16[1024,1024]{1,0:T(8,128)(2,1)S(1)}, f32[128,1024]{1,0:T(8,128)S(1)}) custom-call(s32[8,128]{1,0:T(8,128)S(1)} %bitcast.4, f32[8,128]{1,0:T(8,128)S(1)} %bitcast.5, f32[72,128]{1,0:T(8,128)S(1)} %add.9.after_this), custom_call_target="tpu_custom_call" | custom-call | bytes 2520000 | tf_op jit(solution)/shard_map/picks/pallas_call | solution.py:669
  25.9 2.5 %collective-permute-done.7 = f32[72,128]{1,0:T(8,128)S(1)} collective-permute-done((f32[72,128]{1,0:T(8,128)S(1)}, f32[72,128]{1,0:T(8,128)S(1)}, u32[]{:S(2)}, u32[]{:S(2)}) %collective-permute-start.7) | collective-permute-done | bytes 36896 | tf_op jit(solution)/shard_map/ppermute | solution.py:891
  28.4 0.4 collective-permute-start.8
  28.8 2.0 %ready.1 = (f32[19,16,32,128]{3,2,1,0:T(8,128)S(1)}, f32[5,16,32,128]{3,2,1,0:T(8,128)S(1)}, f32[2,5,16,128]{3,2,1,0:T(8,128)S(1)}, f32[2,5,16,128]{3,2,1,0:T(8,128)S(1)}) custom-call(bf16[19,16,32,128]{3,2,1,0:T(8,128)(2,1)S(1)} %copy-done.1, bf16[19,16,128]{2,1,0:T(8,128)(2,1)S(1)} %collective-permute-done.2.first, ...), custom_call_target="tpu_custom_call" | custom-call | bytes 9000000 | tf_op jit(solution)/shard_map/ready/pallas_call | solution.py:574
  30.8 2.4 %collective-permute-done.8 = f32[72,128]{1,0:T(8,128)S(1)} collective-permute-done((f32[72,128]{1,0:T(8,128)S(1)}, f32[72,128]{1,0:T(8,128)S(1)}, u32[]{:S(2)}, u32[]{:S(2)}) %collective-permute-start.8) | collective-permute-done | bytes 36896 | tf_op jit(solution)/shard_map/ppermute | solution.py:891
  33.3 3.5 %step.1 = (bf16[19,16,32,128]{3,2,1,0:T(8,128)(2,1)}, f32[32,128]{1,0:T(8,128)}, f32[32,1,128]{2,1,0:T(1,128)S(1)}) custom-call(f32[19,16,32,128]{3,2,1,0:T(8,128)S(1)} %get-tuple-element.38.base_ref, f32[5,16,32,128]{3,2,1,0:T(8,128)S(1)} %get-tuple-element.39.shear_ref, f32[2,5,16,128]{3,2,1,0:T(8,128)S(1)} %get-tuple-element.40.edge_ref, ...), custom_call_target="tpu_custom_call" | custom-call | bytes 18000000 | tf_op jit(solution)/shard_map/step/pallas_call | solution.py:845
  36.8 10.5 %all_to_all.5 = f32[32,1,128]{2,1,0:T(1,128)S(1)} all-to-all(f32[32,1,128]{2,1,0:T(1,128)S(1)} %get-tuple-element.54), channel_id=1, replica_groups=mesh['span'=8,'cross'=4] {'span','cross'}, dimensions={0} | all-to-all | bytes 32768 | tf_op jit(solution)/shard_map/all_to_all | solution.py:904
  47.2 0.1 reduce_sum.9
  47.3 0.7 %reshape.17 = f32[3,8]{1,0:T(4,128)} reshape(f32[24]{0:T(128)S(1)} %bitcast.7) | data formatting | bytes 192 | tf_op jit(solution)/shard_map/reshape | solution.py:905
  (15 shorter events, 0.0 us)
Async XLA Ops:
  0.6 1.7 %copy-start = (bf16[19,16,32,128]{3,2,1,0:T(8,128)(2,1)S(1)}, bf16[19,16,32,128]{3,2,1,0:T(8,128)(2,1)}, u32[]{:S(2)}) copy-start(bf16[19,16,32,128]{3,2,1,0:T(8,128)(2,1)} %pops.7) | copy-start | bytes 7471108
  2.3 14.1 %copy-start.1 = (bf16[19,16,32,128]{3,2,1,0:T(8,128)(2,1)S(1)}, bf16[19,16,32,128]{3,2,1,0:T(8,128)(2,1)}, u32[]{:S(2)}) copy-start(bf16[19,16,32,128]{3,2,1,0:T(8,128)(2,1)} %pops.7) | copy-start | bytes 7471108
  2.9 3.2 %collective-permute-start = (s16[9,16,128]{2,1,0:T(8,128)(2,1)S(1)}, s16[9,16,128]{2,1,0:T(8,128)(2,1)S(1)}, u32[]{:S(2)}, u32[]{:S(2)}) collective-permute-start(s16[9,16,128]{2,1,0:T(8,128)(2,1)S(1)} %get-tuple-element.30), channel_id=1, source_target_pairs={{0,1},{1,0},{2,3},{3,2},{4,5},{5,4},{6,7},{7,6},{8,9},{9,8},{10,11... | collective-permute-start | bytes 110600 | tf_op jit(solution)/shard_map/ppermute | solution.py:50
  3.5 4.4 %collective-permute-start.1 = (s16[9,16,128]{2,1,0:T(8,128)(2,1)S(1)}, s16[9,16,128]{2,1,0:T(8,128)(2,1)S(1)}, u32[]{:S(2)}, u32[]{:S(2)}) collective-permute-start(s16[9,16,128]{2,1,0:T(8,128)(2,1)S(1)} %get-tuple-element.31), channel_id=1, source_target_pairs={{0,3},{1,2},{2,1},{3,0},{4,7},{5,6},{6,5},{7,4},{8,11},{9,10},{10,... | collective-permute-start | bytes 110600 | tf_op jit(solution)/shard_map/ppermute | solution.py:50
  8.0 10.4 %collective-permute-start.4 = (s16[6,40,128]{2,1,0:T(8,128)(2,1)S(1)}, s16[6,40,128]{2,1,0:T(8,128)(2,1)S(1)}, u32[]{:S(2)}, u32[]{:S(2)}) collective-permute-start(s16[6,40,128]{2,1,0:T(8,128)(2,1)S(1)} %get-tuple-element.35), channel_id=1, source_target_pairs={{0,4},{4,0},{8,12},{12,8},{16,20},{20,16},{24,28},{28,24},{1,5},{5... | collective-permute-start | bytes 184328 | tf_op jit(solution)/shard_map/ppermute | solution.py:50
  9.6 8.8 %collective-permute-start.5 = (s16[6,40,128]{2,1,0:T(8,128)(2,1)S(1)}, s16[6,40,128]{2,1,0:T(8,128)(2,1)S(1)}, u32[]{:S(2)}, u32[]{:S(2)}) collective-permute-start(s16[6,40,128]{2,1,0:T(8,128)(2,1)S(1)} %get-tuple-element.36), channel_id=1, source_target_pairs={{0,28},{4,8},{8,4},{12,16},{16,12},{20,24},{24,20},{28,0},{1,29},{... | collective-permute-start | bytes 184328 | tf_op jit(solution)/shard_map/ppermute | solution.py:50
  16.6 8.7 %copy-start.2 = (s32[128,8]{0,1:T(8,128)S(1)}, s32[128,8]{0,1:T(8,128)}, u32[]{:S(2)}) copy-start(s32[128,8]{0,1:T(8,128)} %param.5) | copy-start | bytes 12292
  16.6 8.7 %copy-start.3 = (f32[128,8]{0,1:T(8,128)S(1)}, f32[128,8]{0,1:T(8,128)}, u32[]{:S(2)}) copy-start(f32[128,8]{0,1:T(8,128)} %param.6) | copy-start | bytes 12292
  16.6 4.6 %collective-permute-start.3 = (bf16[19,16,128]{2,1,0:T(8,128)(2,1)S(1)}, bf16[19,16,128]{2,1,0:T(8,128)(2,1)S(1)}, u32[]{:S(2)}, u32[]{:S(2)}) collective-permute-start(bf16[19,16,128]{2,1,0:T(8,128)(2,1)S(1)} %get-tuple-element.34), channel_id=1, source_target_pairs={{0,3},{1,2},{2,1},{3,0},{4,7},{5,6},{6,5},{7,4},{8,11},{9,10},{10,... | collective-permute-start | bytes 233480 | tf_op jit(solution)/shard_map/ppermute | solution.py:50
  17.7 3.6 %collective-permute-start.2 = (bf16[19,16,128]{2,1,0:T(8,128)(2,1)S(1)}, bf16[19,16,128]{2,1,0:T(8,128)(2,1)S(1)}, u32[]{:S(2)}, u32[]{:S(2)}) collective-permute-start(bf16[19,16,128]{2,1,0:T(8,128)(2,1)S(1)} %get-tuple-element.33.after_this), channel_id=1, source_target_pairs={{0,1},{1,0},{2,3},{3,2},{4,5},{5,4},{6,7},{7,6},{8,9},{9,8},{10,11... | collective-permute-start | bytes 233480 | tf_op jit(solution)/shard_map/ppermute | solution.py:50
  19.8 13.5 %copy-start.4 = (s32[128]{0:T(128)S(1)}, s32[128]{0:T(128)}, u32[]{:S(2)}) copy-start(s32[128]{0:T(128)} %param.7) | copy-start | bytes 1540
  19.8 4.2 %collective-permute-start.6 = (f32[72,128]{1,0:T(8,128)S(1)}, f32[72,128]{1,0:T(8,128)S(1)}, u32[]{:S(2)}, u32[]{:S(2)}) collective-permute-start(f32[72,128]{1,0:T(8,128)S(1)} %get-tuple-element.37.after_this), channel_id=1, source_target_pairs={{0,4},{4,0},{8,12},{12,8},{16,20},{20,16},{24,28},{28,24},{1,5},{5... | collective-permute-start | bytes 110600 | tf_op jit(solution)/shard_map/ppermute | solution.py:891
  21.7 11.6 %collective-permute-start.9 = (s16[9,40,128]{2,1,0:T(8,128)(2,1)S(1)}, s16[9,40,128]{2,1,0:T(8,128)(2,1)S(1)}, u32[]{:S(2)}, u32[]{:S(2)}) collective-permute-start(s16[9,40,128]{2,1,0:T(8,128)(2,1)S(1)} %get-tuple-element.42), channel_id=1, source_target_pairs={{0,4},{4,0},{8,12},{12,8},{16,20},{20,16},{24,28},{28,24},{1,5},{5... | collective-permute-start | bytes 276488 | tf_op jit(solution)/shard_map/ppermute | solution.py:50
  22.3 10.9 %collective-permute-start.10 = (s16[9,40,128]{2,1,0:T(8,128)(2,1)S(1)}, s16[9,40,128]{2,1,0:T(8,128)(2,1)S(1)}, u32[]{:S(2)}, u32[]{:S(2)}) collective-permute-start(s16[9,40,128]{2,1,0:T(8,128)(2,1)S(1)} %get-tuple-element.43), channel_id=1, source_target_pairs={{0,28},{4,8},{8,4},{12,16},{16,12},{20,24},{24,20},{28,0},{1,29},{... | collective-permute-start | bytes 276488 | tf_op jit(solution)/shard_map/ppermute | solution.py:50
  24.0 4.3 %collective-permute-start.7 = (f32[72,128]{1,0:T(8,128)S(1)}, f32[72,128]{1,0:T(8,128)S(1)}, u32[]{:S(2)}, u32[]{:S(2)}) collective-permute-start(f32[72,128]{1,0:T(8,128)S(1)} %add.9.after_this), channel_id=1, source_target_pairs={{0,8},{4,12},{8,0},{12,4},{16,24},{20,28},{24,16},{28,20},{1,9},{5... | collective-permute-start | bytes 110600 | tf_op jit(solution)/shard_map/ppermute | solution.py:891
  28.4 4.9 %collective-permute-start.8 = (f32[72,128]{1,0:T(8,128)S(1)}, f32[72,128]{1,0:T(8,128)S(1)}, u32[]{:S(2)}, u32[]{:S(2)}) collective-permute-start(f32[72,128]{1,0:T(8,128)S(1)} %add.10), channel_id=1, source_target_pairs={{0,16},{4,20},{8,24},{12,28},{16,0},{20,4},{24,8},{28,12},{1,17},{... | collective-permute-start | bytes 110600 | tf_op jit(solution)/shard_map/ppermute | solution.py:891
